TPU v7x, 256 devices: a whole 4x4x8 slice. The times are simulated.
256 devices in a mesh: batch: 16 (over z, y_lo), row: 16 (over x, y_hi, core).
Axes of the slice: x: 4, y: 4 (y_hi: 2, y_lo: 2; y = y_hi * 2 + y_lo), z: 8, core: 2. Of those that a mesh axis runs over, the one named last changes fastest.
Arguments:
- probe_real: float32 [2048, 2048], P('row'), may hold values from -6 to 6
- probe_imag: float32 [2048, 2048], P('row'), may hold values from -6 to 6
- object_real: float32 [2048, 2304], P('row'), may hold values from -5 to 5
- object_imag: float32 [2048, 2304], P('row'), may hold values from -5 to 5
- amplitudes: float32 [16, 2048, 2048], P('batch', 'row'), may hold values from 0.2 to 3
- row_shift: int32 [16], P('batch'), may hold values from 0 to 127
- col_shift: int32 [16], P('batch'), may hold values from 0 to 256
Outputs:
- probe_grad_real: float32 [2048, 2048], P('row', 'batch')
- probe_grad_imag: float32 [2048, 2048], P('row', 'batch')
- object_grad_real: float32 [2048, 2304], P('row', 'batch')
- object_grad_imag: float32 [2048, 2304], P('row', 'batch')
All inputs are finite; a program needn't handle non-finite values.
Results may differ from a plain program's by a relative error of at most 0.0003.
Values sent between devices are 32-bit elements; how exact they have to be, the bound alone decides.
No kernel may reach another device: no remote copies, remote signals or barrier semaphores. Data moves between devices by JAX's collectives and lax.ppermute only.
A program may use at most 128 MiB of HBM per device.

v0:
```python
import math

import jax
import jax.numpy as jnp
from jax import lax
from jax.sharding import PartitionSpec as P

HIGHEST = lax.Precision.HIGHEST


def passed_along(value, axis, by):
    size = lax.axis_size(axis)
    return lax.ppermute(value, axis, [(i, (i + by) % size) for i in range(size)])


def split_length(length):
    leading = 1
    for factor in range(1, math.isqrt(length) + 1):
        if length % factor == 0:
            leading = factor
    return (leading, length // leading)


def unit_table(row_total, col_total, modulus, direction):
    row_ids = jnp.arange(row_total, dtype=jnp.int32)
    col_ids = jnp.arange(col_total, dtype=jnp.int32)
    turn_count = row_ids[:, None] * col_ids[None, :] % modulus
    angles = direction * 2.0 * math.pi / modulus * turn_count.astype(jnp.float32)
    return (jnp.cos(angles), jnp.sin(angles))


def chirp_table(length, direction):
    indices = jnp.arange(length, dtype=jnp.int32)
    frequency = jnp.where(indices < length // 2, indices, indices - length)
    turn_count = frequency * frequency % (4 * length)
    angles = direction * 2.0 * math.pi / (4 * length) * turn_count.astype(jnp.float32)
    return (jnp.cos(angles) / length, jnp.sin(angles) / length)


def block_form(real_part, imag_part):
    return jnp.stack(
        [jnp.stack([real_part, -imag_part], 1), jnp.stack([imag_part, real_part], 1)], 0
    )


def section_tables(length, direction, chirp_sign):
    leading, trailing = split_length(length)
    outer_pair = unit_table(leading, leading, leading, direction)
    inner_pair = unit_table(trailing, trailing, trailing, direction)
    twiddle = unit_table(leading, trailing, length, direction)
    inner_real = (
        inner_pair[0][:, :, None] * twiddle[0].T[None]
        - inner_pair[1][:, :, None] * twiddle[1].T[None]
    )
    inner_imag = (
        inner_pair[0][:, :, None] * twiddle[1].T[None]
        + inner_pair[1][:, :, None] * twiddle[0].T[None]
    )
    if chirp_sign != 0.0:
        factor_pair = chirp_table(length, chirp_sign)
        factor_real = factor_pair[0].reshape(trailing, leading)[:, None, :]
        factor_imag = factor_pair[1].reshape(trailing, leading)[:, None, :]
        inner_real, inner_imag = (
            inner_real * factor_real - inner_imag * factor_imag,
            inner_real * factor_imag + inner_imag * factor_real,
        )
    return (
        leading,
        trailing,
        block_form(outer_pair[0], outer_pair[1]),
        block_form(inner_real, inner_imag),
    )


def transform_lead(field, tables):
    leading, trailing, outer_table, inner_table = tables
    shaped = field.reshape(2, field.shape[1], leading, trailing, field.shape[3])
    sectioned = jnp.einsum("cpda,dqabk->cqpbk", outer_table, shaped, precision=HIGHEST)
    sectioned = jnp.einsum("crdbp,dqpbk->cqrpk", inner_table, sectioned, precision=HIGHEST)
    return sectioned.reshape(field.shape)


def transform_last(field, tables):
    leading, trailing, outer_table, inner_table = tables
    shaped = field.reshape(2, field.shape[1], field.shape[2], leading, trailing)
    sectioned = jnp.einsum("cpda,dqkab->cqkpb", outer_table, shaped, precision=HIGHEST)
    sectioned = jnp.einsum("crdbp,dqkpb->cqkrp", inner_table, sectioned, precision=HIGHEST)
    return sectioned.reshape(field.shape)


def propagate_lead(field, direction):
    length = field.shape[2]
    spectrum = transform_lead(field, section_tables(length, -1.0, direction))
    return transform_lead(spectrum, section_tables(length, 1.0, 0.0))


def propagate_last(field, direction):
    length = field.shape[3]
    spectrum = transform_last(field, section_tables(length, -1.0, direction))
    return transform_last(spectrum, section_tables(length, 1.0, 0.0))


def complex_product(left_value, right_value):
    return jnp.stack(
        [
            left_value[0] * right_value[0] - left_value[1] * right_value[1],
            left_value[0] * right_value[1] + left_value[1] * right_value[0],
        ],
        0,
    )


def conjugate(value):
    return jnp.stack([value[0], -value[1]], 0)


def modulus_step(wave, measured):
    magnitude = jnp.sqrt(wave[0] * wave[0] + wave[1] * wave[1])
    keep_share = 1.0 - measured / jnp.maximum(magnitude, 0.25)
    return wave * keep_share[None]


def forward_rows(piece):
    return propagate_lead(piece, -1.0)


def backward_rows(piece):
    return propagate_lead(piece, 1.0)


def per_device(probe_real, probe_imag, object_real, object_imag, amplitudes, row_shift, col_shift):
    band_rows = object_real.shape[0]
    field_width = probe_real.shape[1]
    below_rows = passed_along((object_real, object_imag), "row", -1)
    stacked = jnp.stack(
        [
            jnp.concatenate([object_real, below_rows[0]], 0),
            jnp.concatenate([object_imag, below_rows[1]], 0),
        ],
        0,
    )
    probe_field = jnp.stack([probe_real, probe_imag], 0)[:, None]

    def window(start_row, start_col):
        zero_index = jnp.zeros((), jnp.int32)
        return lax.dynamic_slice(
            stacked, (zero_index, start_row, start_col), (2, band_rows, field_width)
        )

    patch_field = jax.vmap(window, out_axes=1)(row_shift, col_shift)
    exit_wave = complex_product(probe_field, patch_field)
    along_cols = propagate_last(exit_wave, -1.0)
    columns = forward_rows(
        lax.all_to_all(along_cols, "row", split_axis=3, concat_axis=2, tiled=True)
    )
    detector = lax.all_to_all(columns, "row", split_axis=2, concat_axis=3, tiled=True)
    residual_wave = modulus_step(detector, amplitudes)
    returned = backward_rows(
        lax.all_to_all(residual_wave, "row", split_axis=3, concat_axis=2, tiled=True)
    )
    row_wave = lax.all_to_all(returned, "row", split_axis=2, concat_axis=3, tiled=True)
    gradient = propagate_last(row_wave, 1.0)
    probe_term = jnp.sum(complex_product(conjugate(patch_field), gradient), axis=1)
    object_term = complex_product(conjugate(probe_field), gradient)
    object_acc = jnp.zeros_like(stacked)
    zero_index = jnp.zeros((), jnp.int32)
    corner = (zero_index, row_shift[0], col_shift[0])
    object_acc = lax.dynamic_update_slice(object_acc, object_term[:, 0], corner)
    arrived = passed_along((object_acc[0, band_rows:], object_acc[1, band_rows:]), "row", 1)
    object_full = (object_acc[0, :band_rows] + arrived[0], object_acc[1, :band_rows] + arrived[1])
    object_grad = (
        lax.psum_scatter(object_full[0], "batch", scatter_dimension=1, tiled=True),
        lax.psum_scatter(object_full[1], "batch", scatter_dimension=1, tiled=True),
    )
    probe_grad = (
        lax.psum_scatter(probe_term[0], "batch", scatter_dimension=1, tiled=True),
        lax.psum_scatter(probe_term[1], "batch", scatter_dimension=1, tiled=True),
    )
    return (probe_grad[0], probe_grad[1], object_grad[0], object_grad[1])


def solution(mesh):
    placed = (
        P("row", None),
        P("row", None),
        P("row", None),
        P("row", None),
        P("batch", "row", None),
        P("batch"),
        P("batch"),
    )
    return jax.shard_map(
        per_device,
        mesh=mesh,
        in_specs=placed,
        out_specs=(P("row", "batch"), P("row", "batch"), P("row", "batch"), P("row", "batch")),
        check_vma=False,
    )
```

profile of v0, /device:TPU:4, one launch (start us, length us, event | category | flops | bytes accessed | tf_op | source)
XLA Modules:
  0.0 653.3 jit_solution(13280142688237452759)
XLA Ops:
  25.7 10.8 %collective-permute-done.1 = f32[128,2304]{1,0:T(8,128)} collective-permute-done((f32[128,2304]{1,0:T(8,128)}, f32[128,2304]{1,0:T(8,128)}, u32[]{:S(2)}, u32[]{:S(2)}) %collective-permute-start.1) | collective-permute-done | bytes 1179680 | tf_op jit(solution)/shard_map/ppermute | solution.py:13
  48.5 5.0 fusion.70
  54.7 3.7 fusion.36
  58.5 5.0 fusion.39
  64.7 7.6 %copy.185 = f32[2,1,128,2048]{2,0,1,3:T(2,128)S(1)} copy(f32[2,1,128,2048]{2,3,0,1:T(8,128)S(1)} %bitcast.299) | data formatting | bytes 4194304 | tf_op jit(solution)/shard_map/reshape | solution.py:88
  72.3 36.1 %all_to_all.63 = f32[2,1,128,2048]{2,0,1,3:T(2,128)S(1)} all-to-all(f32[2,1,128,2048]{2,0,1,3:T(2,128)S(1)} %copy.185), channel_id=1, replica_groups=mesh['batch'=16,'row'=16] {'row'}, dimensions={3} | all-to-all | bytes 4194304 | tf_op jit(solution)/shard_map/all_to_all | solution.py:154
  113.1 4.9 fusion.42
  118.0 5.0 fusion.73
  128.0 5.0 fusion.48
  134.3 8.6 %copy.194 = f32[2,1,2048,128]{3,0,1,2:T(2,128)} copy(f32[2,1,2048,128]{3,2,0,1:T(8,128)S(1)} %bitcast.303) | data formatting | bytes 4194304 | tf_op jit(solution)/shard_map/reshape | solution.py:80
  142.9 6.7 %all-to-all-start.1 = ((f32[2,1,2048,128]{3,0,1,2:T(2,128)}), f32[2,1,2048,128]{3,0,1,2:T(2,128)}, u32[]{:S(2)}, u32[]{:S(2)}) async-start(f32[2,1,2048,128]{3,0,1,2:T(2,128)} %copy.194), calls=%async_computation.1 | async-start | bytes 4194304 | tf_op jit(solution)/shard_map/all_to_all | solution.py:156
  152.2 24.7 %all-to-all-done.1 = f32[2,1,2048,128]{3,0,1,2:T(2,128)} async-done(((f32[2,1,2048,128]{3,0,1,2:T(2,128)}), f32[2,1,2048,128]{3,0,1,2:T(2,128)}, u32[]{:S(2)}, u32[]{:S(2)}) %all-to-all-start.1) | async-done | bytes 2097184 | tf_op jit(solution)/shard_map/all_to_all | solution.py:156
  190.7 8.6 %copy.199 = f32[2,1,128,2048]{2,0,1,3:T(2,128)} copy(f32[2,1,128,2048]{2,3,0,1:T(8,128)S(1)} %bitcast_multiply_fusion) | data formatting | bytes 4194304 | tf_op jit(solution)/shard_map/mul | solution.py:120
  199.3 6.9 %all-to-all-start.2 = ((f32[2,1,128,2048]{2,0,1,3:T(2,128)}), f32[2,1,128,2048]{2,0,1,3:T(2,128)}, u32[]{:S(2)}, u32[]{:S(2)}) async-start(f32[2,1,128,2048]{2,0,1,3:T(2,128)} %copy.199), calls=%async_computation.2 | async-start | bytes 4194304 | tf_op jit(solution)/shard_map/all_to_all | solution.py:159
  206.3 5.1 maximum_bitcast_fusion.8
  211.3 22.1 %all-to-all-done.2 = f32[2,1,128,2048]{2,0,1,3:T(2,128)} async-done(((f32[2,1,128,2048]{2,0,1,3:T(2,128)}), f32[2,1,128,2048]{2,0,1,3:T(2,128)}, u32[]{:S(2)}, u32[]{:S(2)}) %all-to-all-start.2) | async-done | bytes 2097184 | tf_op jit(solution)/shard_map/all_to_all | solution.py:159
  239.6 4.9 fusion.51
  244.6 5.0 fusion.76
  250.8 3.7 fusion.54
  254.5 5.0 fusion.57
  260.8 7.6 %copy.209 = f32[2,1,2048,128]{3,0,1,2:T(2,128)S(1)} copy(f32[2,1,2048,128]{3,2,0,1:T(8,128)S(1)} %bitcast.307) | data formatting | bytes 4194304 | tf_op jit(solution)/shard_map/reshape | solution.py:80
  268.4 33.6 %all_to_all.64 = f32[2,1,2048,128]{3,0,1,2:T(2,128)S(1)} all-to-all(f32[2,1,2048,128]{3,0,1,2:T(2,128)S(1)} %copy.209), channel_id=1, replica_groups=mesh['batch'=16,'row'=16] {'row'}, dimensions={2} | all-to-all | bytes 4194304 | tf_op jit(solution)/shard_map/all_to_all | solution.py:161
  306.7 4.9 fusion.60
  311.6 5.0 fusion.81
  321.4 5.0 fusion.66
  337.0 16.0 %dynamic_update_slice.3 = f32[2,256,2304]{1,2,0:T(8,128)} dynamic-update-slice(f32[2,256,2304]{1,2,0:T(8,128)} %broadcast_in_dim.8, f32[2,128,2048]{1,2,0:T(8,128)S(1)} %maximum_bitcast_fusion.10, s32[]{:T(128)} %constant.187.clone.1, s32[]{:T(128)S(6)} %select_n.268, s32[]{:T(128)S(6)} %select_n.269) | dynamic-update-slice | bytes 4194308 | tf_op jit(solution)/shard_map/dynamic_update_slice | solution.py:168
  355.9 18.6 %collective-permute-done.3 = f32[128,2304]{0,1:T(8,128)S(1)} collective-permute-done((f32[128,2304]{0,1:T(8,128)S(1)}, f32[128,2304]{0,1:T(8,128)S(1)}, u32[]{:S(2)}, u32[]{:S(2)}) %collective-permute-start.3) | collective-permute-done | bytes 1179680 | tf_op jit(solution)/shard_map/ppermute | solution.py:13
  374.5 12.6 %collective-permute-done.2 = f32[128,2304]{0,1:T(8,128)S(1)} collective-permute-done((f32[128,2304]{0,1:T(8,128)S(1)}, f32[128,2304]{0,1:T(8,128)S(1)}, u32[]{:S(2)}, u32[]{:S(2)}) %collective-permute-start.2) | collective-permute-done | bytes 1179680 | tf_op jit(solution)/shard_map/ppermute | solution.py:13
  389.5 13.0 %reduce-scatter.5.cloned.1.call-done = f32[128,128]{0,1:T(8,128)} async-done(((f32[128,2048]{0,1:T(8,128)}), f32[128,128]{0,1:T(8,128)}) %reduce-scatter.5.cloned.1.call-update) | async-done | bytes 65552 | tf_op jit(solution)/shard_map/reduce_scatter | solution.py:176
  404.1 95.0 %reduce-scatter.7.cloned.1.call-done = f32[128,128]{0,1:T(8,128)} async-done(((f32[128,2048]{0,1:T(8,128)}), f32[128,128]{0,1:T(8,128)}) %reduce-scatter.7.cloned.1.call-update) | async-done | bytes 65552 | tf_op jit(solution)/shard_map/reduce_scatter | solution.py:177
  500.7 72.5 %reduce-scatter.9.cloned.1.call-done = f32[128,144]{0,1:T(8,128)} async-done(((f32[128,2304]{0,1:T(8,128)}), f32[128,144]{0,1:T(8,128)}) %reduce-scatter.9.cloned.1.call-update) | async-done | bytes 73744 | tf_op jit(solution)/shard_map/reduce_scatter | solution.py:172
  573.1 73.4 %reduce-scatter.11.cloned.1.call-done = f32[128,144]{0,1:T(8,128)} async-done(((f32[128,2304]{0,1:T(8,128)}), f32[128,144]{0,1:T(8,128)}) %reduce-scatter.11.cloned.1.call-update) | async-done | bytes 73744 | tf_op jit(solution)/shard_map/reduce_scatter | solution.py:173
  (110 shorter events, 95.6 us)
Async XLA Ops:
  7.2 17.1 %collective-permute-start = (f32[128,2304]{1,0:T(8,128)}, f32[128,2304]{1,0:T(8,128)}, u32[]{:S(2)}, u32[]{:S(2)}) collective-permute-start(f32[128,2304]{1,0:T(8,128)} %param.9), channel_id=1, source_target_pairs={{0,15},{1,0},{2,1},{3,2},{4,3},{5,4},{6,5},{7,6},{8,7},{9,8},{10,9... | collective-permute-start | bytes 3538952 | tf_op jit(solution)/shard_map/ppermute | solution.py:13
  9.8 26.7 %collective-permute-start.1 = (f32[128,2304]{1,0:T(8,128)}, f32[128,2304]{1,0:T(8,128)}, u32[]{:S(2)}, u32[]{:S(2)}) collective-permute-start(f32[128,2304]{1,0:T(8,128)} %param.10), channel_id=1, source_target_pairs={{0,15},{1,0},{2,1},{3,2},{4,3},{5,4},{6,5},{7,6},{8,7},{9,8},{10,9... | collective-permute-start | bytes 3538952 | tf_op jit(solution)/shard_map/ppermute | solution.py:13
  21.7 2.5 copy-start.17
  24.2 12.3 %copy-start.18 = (f32[128,2304]{1,0:T(8,128)S(1)}, f32[128,2304]{1,0:T(8,128)}, u32[]{:S(2)}) copy-start(f32[128,2304]{1,0:T(8,128)} %param.10) | copy-start | bytes 3538948
  46.3 2.0 copy-start.6
  46.3 2.2 copy-start.8
  54.7 3.7 copy-start
  113.1 5.0 copy-start.7
  113.1 5.0 copy-start.9
  124.3 3.7 copy-start.1
  142.9 33.9 %all-to-all-start.1 = ((f32[2,1,2048,128]{3,0,1,2:T(2,128)}), f32[2,1,2048,128]{3,0,1,2:T(2,128)}, u32[]{:S(2)}, u32[]{:S(2)}) async-start(f32[2,1,2048,128]{3,0,1,2:T(2,128)} %copy.194), calls=%async_computation.1 | async-start | bytes 4194304 | tf_op jit(solution)/shard_map/all_to_all | solution.py:156
  188.3 2.2 copy-start.16
  199.3 34.0 %all-to-all-start.2 = ((f32[2,1,128,2048]{2,0,1,3:T(2,128)}), f32[2,1,128,2048]{2,0,1,3:T(2,128)}, u32[]{:S(2)}, u32[]{:S(2)}) async-start(f32[2,1,128,2048]{2,0,1,3:T(2,128)} %copy.199), calls=%async_computation.2 | async-start | bytes 4194304 | tf_op jit(solution)/shard_map/all_to_all | solution.py:159
  206.2 196.3 %reduce-scatter.5.cloned.1.call-start = ((), (), s32[]{:S(2)}) async-start(), calls=%async_computation.8 | async-start | bytes 1114112 | tf_op jit(solution)/shard_map/reduce_scatter | solution.py:176
  239.6 5.0 copy-start.10
  239.6 5.0 copy-start.12
  250.8 3.7 copy-start.2
  306.6 5.0 copy-start.11
  306.6 5.0 copy-start.13
  317.9 3.6 copy-start.3
  326.7 1.6 copy-start.4
  327.3 2.6 copy-start.14
  328.3 1.7 copy-start.15
  330.0 169.1 %reduce-scatter.7.cloned.1.call-start = ((), (), s32[]{:S(2)}) async-start(), calls=%async_computation.9 | async-start | bytes 1114112 | tf_op jit(solution)/shard_map/reduce_scatter | solution.py:177
  333.2 240.0 %reduce-scatter.9.cloned.1.call-start = ((), (), s32[]{:S(2)}) async-start(), calls=%async_computation.10 | async-start | bytes 1253376 | tf_op jit(solution)/shard_map/reduce_scatter | solution.py:172
  353.0 34.2 %copy-start.5 = (f32[2,256,2304]{1,2,0:T(8,128)S(1)}, f32[2,256,2304]{1,2,0:T(8,128)}, u32[]{:S(2)}) copy-start(f32[2,256,2304]{1,2,0:T(8,128)} %dynamic_update_slice.3) | copy-start | bytes 14155780
  354.9 19.6 %collective-permute-start.3 = (f32[128,2304]{0,1:T(8,128)S(1)}, f32[128,2304]{0,1:T(8,128)S(1)}, u32[]{:S(2)}, u32[]{:S(2)}) collective-permute-start(f32[128,2304]{0,1:T(8,128)S(1)} %get-tuple-element.33), channel_id=1, source_target_pairs={{0,1},{1,2},{2,3},{3,4},{4,5},{5,6},{6,7},{7,8},{8,9},{9,10},{10,1... | collective-permute-start | bytes 3538952 | tf_op jit(solution)/shard_map/ppermute | solution.py:13
  355.0 32.1 %collective-permute-start.2 = (f32[128,2304]{0,1:T(8,128)S(1)}, f32[128,2304]{0,1:T(8,128)S(1)}, u32[]{:S(2)}, u32[]{:S(2)}) collective-permute-start(f32[128,2304]{0,1:T(8,128)S(1)} %get-tuple-element.34), channel_id=1, source_target_pairs={{0,1},{1,2},{2,3},{3,4},{4,5},{5,6},{6,7},{7,8},{8,9},{9,10},{10,1... | collective-permute-start | bytes 3538952 | tf_op jit(solution)/shard_map/ppermute | solution.py:13
  388.9 257.6 %reduce-scatter.11.cloned.1.call-start = ((), (), s32[]{:S(2)}) async-start(), calls=%async_computation.11 | async-start | bytes 1253376 | tf_op jit(solution)/shard_map/reduce_scatter | solution.py:173
Sparse Core Ops, SparseCore 0:
  330.1 72.3 reduce-scatter.4
  405.2 93.8 reduce-scatter.6
  502.2 70.8 reduce-scatter.8
  576.1 70.4 reduce-scatter.10
where the time goes:
time: 659 us; the launch traced here: 653 us
  waiting for transfers between devices  343 us (52%)
  local copies, waits for them, and re-layouts  102 us (15%)
  matrix products  71.6 us (11%)
  blocking collectives  69.8 us (11%)
  other arithmetic  33 us (5%)
  starting transfers between devices  18.1 us (3%)
  between operations  15.8 us (2%)
    reduce_scatter x1, waiting for transfers between devices, per_device(): lax.psum_scatter(probe_term[1], 'batch', scatter_dimension=1, tiled=True)  95 us
    reduce_scatter x1, waiting for transfers between devices, per_device(): lax.psum_scatter(object_full[1], 'batch', scatter_dimension=1, tiled=True)  73.4 us
    reduce_scatter x1, waiting for transfers between devices, per_device(): lax.psum_scatter(object_full[0], 'batch', scatter_dimension=1, tiled=True)  72.5 us
    ppermute x4, waiting for transfers between devices, passed_along(): lax.ppermute(value, axis, [(i, (i + by) % size) for i in range(size)])  42 us
    all_to_all x1, blocking collectives, per_device(): lax.all_to_all(along_cols, 'row', split_axis=3, concat_axis=2, tiled=True)  36.1 us
    all_to_all x1, blocking collectives, per_device(): lax.all_to_all(returned, 'row', split_axis=2, concat_axis=3, tiled=True)  33.6 us
    all_to_all x1, waiting for transfers between devices, per_device(): lax.all_to_all(columns, 'row', split_axis=2, concat_axis=3, tiled=True)  24.7 us
    all_to_all x1, waiting for transfers between devices, per_device(): lax.all_to_all(residual_wave, 'row', split_axis=3, concat_axis=2, tiled=T...  22.1 us
  transfers between devices with their start and end apart: 10, of which 9 were waited for; matrix products, arithmetic and copies ran while one was open for 8% of the time, Pallas kernels for 0%

commit v1 on v0

v1 whole, which is shorter than its diff:
```python
import functools
import math

import jax
import jax.numpy as jnp
import ml_dtypes
import numpy as np
from jax import lax
from jax.experimental import pallas as pl
from jax.experimental.pallas import tpu as pltpu
from jax.sharding import Mesh, PartitionSpec as P

F32 = jnp.float32
BF16 = jnp.bfloat16
LANES = 128
LEAD = 16
ROWS = 128
GROUP = 4
PART = ROWS // GROUP
VMEM_LIMIT = 56 * 1024 * 1024


def split_pair(table):
    high = table.astype(ml_dtypes.bfloat16)
    low = (table - high.astype(np.float64)).astype(ml_dtypes.bfloat16)
    return high, low


@functools.lru_cache(maxsize=None)
def propagation_tables(length):
    index = np.arange(length, dtype=np.int64)
    frequency = np.where(index < length // 2, index, index - length)
    chirp = np.exp(-2j * np.pi * ((frequency * frequency) % (4 * length)) / (4 * length))
    offsets = np.arange(-(LANES - 1), LANES, dtype=np.int64)
    place = np.arange(LANES)
    right = np.empty((LEAD, 2 * LANES, 2 * LANES))
    for c in range(LEAD):
        tone = c + LEAD * np.arange(LANES, dtype=np.int64)
        phase = np.exp(2j * np.pi * ((offsets[:, None] * tone[None, :]) % length) / length)
        line = phase @ chirp[tone] / length
        middle = line[place[:, None] - place[None, :] + LANES - 1]
        left = np.block([[middle.real, -middle.imag], [middle.imag, middle.real]])
        right[c] = left.T
    return split_pair(right) + split_pair(np.ascontiguousarray(np.swapaxes(right, 1, 2)))


def times(value, cosine, sine):
    real, imag = value
    if sine == 0.0 and cosine == 1.0:
        return value
    if cosine == 0.0 and sine == -1.0:
        return (imag, -real)
    if cosine == 0.0 and sine == 1.0:
        return (-imag, real)
    return (real * cosine - imag * sine, real * sine + imag * cosine)


def add(left, right):
    return (left[0] + right[0], left[1] + right[1])


def sub(left, right):
    return (left[0] - right[0], left[1] - right[1])


def dft4(values, sign):
    a, b, c, d = values
    even, odd = add(a, c), sub(a, c)
    both, gap = add(b, d), sub(b, d)
    turned = (-sign * gap[1], sign * gap[0]) if sign < 0 else (-gap[1], gap[0])
    if sign < 0:
        turned = (gap[1], -gap[0])
    return [add(even, both), add(odd, turned), sub(even, both), sub(odd, turned)]


def dft16(values, sign):
    inner = [dft4([values[4 * n1 + n2] for n1 in range(4)], sign) for n2 in range(4)]
    result = [None] * 16
    for k1 in range(4):
        column = []
        for n2 in range(4):
            turns = n2 * k1 % 16
            angle = 2.0 * math.pi * turns / 16
            cosine, sine = math.cos(angle), sign * math.sin(angle)
            if turns in (0, 4, 8, 12):
                cosine, sine = float(round(cosine)), float(round(sine))
            column.append(times(inner[n2][k1], cosine, sine))
        for k2, value in enumerate(dft4(column, sign)):
            result[k1 + 4 * k2] = value
    return result


def halves(value):
    high = value.astype(BF16)
    return high, (value - high.astype(F32)).astype(BF16)


def dot(left, right):
    return jnp.dot(left, right, preferred_element_type=F32)


def mix_right(store, table_high, table_low):
    rows = store.shape[1]

    def step(c, carry):
        high, low = halves(store[c])
        wide = dot(jnp.concatenate([high, low], 0), table_high[c])
        store[c] = wide[:rows] + (wide[rows:] + dot(high, table_low[c]))
        return carry

    lax.fori_loop(0, LEAD, step, 0, unroll=True)


def mix_left(store, table_high, table_low):
    cols = store.shape[2]

    def step(c, carry):
        high, low = halves(store[c])
        wide = dot(table_high[c], jnp.concatenate([high, low], 1))
        store[c] = wide[:, :cols] + (wide[:, cols:] + dot(table_low[c], high))
        return carry

    lax.fori_loop(0, LEAD, step, 0, unroll=True)


def lane_parts(col_shift):
    tile = lax.div(col_shift, LANES)
    return tile, col_shift - tile * LANES


def eight_rows(window, part, start, lanes):
    base = lax.div(start, 8) * 8
    shift = start - base
    after = jnp.minimum(base + 8, window.shape[1] - 8)
    back = lax.rem(8 - shift, 8)
    upper = pltpu.roll(window[part, pl.ds(pl.multiple_of(base, 8), 8), lanes], back, 0)
    lower = pltpu.roll(window[part, pl.ds(pl.multiple_of(after, 8), 8), lanes], back, 0)
    row = lax.broadcasted_iota(jnp.int32, upper.shape, 0)
    return jnp.where(row < 8 - shift, upper, lower)


def shifted_tiles(window, part, row_start, tile, shift):
    last = window.shape[2] // LANES - 1
    back = lax.rem(LANES - shift, LANES)
    lane = lax.broadcasted_iota(jnp.int32, (8, LANES), 1)
    rolled = []
    for j in range(LEAD + 1):
        at = pl.multiple_of(jnp.minimum(tile + j, last) * LANES, LANES)
        rolled.append(pltpu.roll(eight_rows(window, part, row_start, pl.ds(at, LANES)), back, 1))
    keep = lane < LANES - shift
    return [jnp.where(keep, rolled[j], rolled[j + 1]) for j in range(LEAD)]


def fetch(pairs, sems):
    copies = [pltpu.make_async_copy(src, dst, sems.at[n]) for n, (src, dst) in enumerate(pairs)]
    for copy in copies:
        copy.start()
    for copy in copies:
        copy.wait()


def exit_kernel(
    shifts, probe_r, probe_i, object_r, object_i, below_r, below_i, table_high, table_low, out,
    window, store, sems,
):
    fetch(
        [
            (object_r, window.at[0, pl.ds(0, ROWS)]),
            (object_i, window.at[1, pl.ds(0, ROWS)]),
            (below_r, window.at[0, pl.ds(ROWS, ROWS)]),
            (below_i, window.at[1, pl.ds(ROWS, ROWS)]),
        ],
        sems,
    )
    row_shift = shifts[0]
    tile, shift = lane_parts(shifts[1])

    def gather(k, carry):
        at = pl.multiple_of(k * 8, 8)
        rows = pl.ds(at, 8)
        patch_r = shifted_tiles(window, 0, row_shift + at, tile, shift)
        patch_i = shifted_tiles(window, 1, row_shift + at, tile, shift)
        values = []
        for a in range(LEAD):
            lanes = pl.ds(a * LANES, LANES)
            real, imag = probe_r[rows, lanes], probe_i[rows, lanes]
            values.append(
                (real * patch_r[a] - imag * patch_i[a], real * patch_i[a] + imag * patch_r[a])
            )
        for c, (real, imag) in enumerate(dft16(values, -1)):
            store[c, rows, pl.ds(0, LANES)] = real
            store[c, rows, pl.ds(LANES, LANES)] = imag
        return carry

    lax.fori_loop(0, ROWS // 8, gather, 0)
    mix_right(store, table_high, table_low)

    def spread(k, carry):
        rows = pl.ds(pl.multiple_of(k * 8, 8), 8)
        values = [(store[c, rows, pl.ds(0, LANES)], store[c, rows, pl.ds(LANES, LANES)]) for c in range(LEAD)]
        for a, (real, imag) in enumerate(dft16(values, 1)):
            out[a, 0, rows] = real
            out[a, 1, rows] = imag
        return carry

    lax.fori_loop(0, ROWS // 8, spread, 0)


def detector_kernel(shifts, columns, measured, table_high, table_low, out, store, wrapped):
    row_shift = shifts[0]

    def load(c, k):
        at = pl.multiple_of(k * 8, 8)
        return (store[c, pl.ds(at, 8)], store[c, pl.ds(pl.multiple_of(ROWS + k * 8, 8), 8)])

    def save(values, k):
        for c, (real, imag) in enumerate(values):
            store[c, pl.ds(pl.multiple_of(k * 8, 8), 8)] = real
            store[c, pl.ds(pl.multiple_of(ROWS + k * 8, 8), 8)] = imag

    def first(k, carry):
        rows = pl.ds(pl.multiple_of(k * 8, 8), 8)
        save(dft16([(columns[a, 0, rows], columns[a, 1, rows]) for a in range(LEAD)], -1), k)
        return carry

    lax.fori_loop(0, ROWS // 8, first, 0)
    mix_left(store, table_high, table_low)

    def modulus(k, carry):
        rows = pl.ds(pl.multiple_of(k * 8, 8), 8)
        residual = []
        for a, (real, imag) in enumerate(dft16([load(c, k) for c in range(LEAD)], 1)):
            share = measured[a, rows] * lax.rsqrt(jnp.maximum(real * real + imag * imag, 0.0625))
            keep = 1.0 - share
            residual.append((real * keep, -imag * keep))
        save(dft16(residual, -1), k)
        return carry

    lax.fori_loop(0, ROWS // 8, modulus, 0)
    mix_left(store, table_high, table_low)

    def last(k, carry):
        for a, (real, imag) in enumerate(dft16([load(c, k) for c in range(LEAD)], 1)):
            at = pl.multiple_of((a + 1) * ROWS + k * 8, 8)
            wrapped[0, pl.ds(at, 8)] = real
            wrapped[1, pl.ds(at, 8)] = -imag
            if a == LEAD - 1:
                first_at = pl.multiple_of(k * 8, 8)
                wrapped[0, pl.ds(first_at, 8)] = real
                wrapped[1, pl.ds(first_at, 8)] = -imag
        return carry

    lax.fori_loop(0, ROWS // 8, last, 0)

    def place(n, carry):
        part = lax.div(n, LEAD)
        start = ROWS * (n - part * LEAD + 1) + PART * part
        aligned = pl.multiple_of(start, 8)
        for half in range(2):
            out[n, half] = wrapped[half, pl.ds(aligned, PART)]
            for k in range(PART // 8):
                out[n, 2 + half, pl.ds(8 * k, 8)] = eight_rows(
                    wrapped, half, start - row_shift + 8 * k, slice(None)
                )
        return carry

    lax.fori_loop(0, GROUP * LEAD, place, 0)


def gradient_kernel(
    shifts, rows_in, probe_r, probe_i, above_r, above_i, object_r, object_i, below_r, below_i,
    table_high, table_low, out, probe_window, object_window, store, probe_acc, object_acc, sems,
):
    fetch(
        [
            (above_r, probe_window.at[0, pl.ds(0, ROWS)]),
            (above_i, probe_window.at[1, pl.ds(0, ROWS)]),
            (probe_r, probe_window.at[0, pl.ds(ROWS, ROWS)]),
            (probe_i, probe_window.at[1, pl.ds(ROWS, ROWS)]),
            (object_r, object_window.at[0, pl.ds(0, ROWS)]),
            (object_i, object_window.at[1, pl.ds(0, ROWS)]),
            (below_r, object_window.at[0, pl.ds(ROWS, ROWS)]),
            (below_i, object_window.at[1, pl.ds(ROWS, ROWS)]),
        ],
        sems,
    )
    own = shifts[2 * GROUP]
    own_start = own * PART
    chunks = PART // 8

    def first(m, carry):
        aligned = lax.div(m, GROUP * chunks)
        position = lax.rem(lax.div(m, chunks), GROUP)
        rows = pl.ds(pl.multiple_of(lax.rem(m, chunks) * 8, 8), 8)
        at = pl.ds(pl.multiple_of(m * 8, 8), 8)
        values = [
            (rows_in[position * LEAD + a, 2 * aligned, rows], -rows_in[position * LEAD + a, 2 * aligned + 1, rows])
            for a in range(LEAD)
        ]
        for c, (real, imag) in enumerate(dft16(values, -1)):
            store[c, at, pl.ds(0, LANES)] = real
            store[c, at, pl.ds(LANES, LANES)] = imag
        return carry

    lax.fori_loop(0, 2 * GROUP * chunks, first, 0)
    mix_right(store, table_high, table_low)
    probe_acc[...] = jnp.zeros_like(probe_acc)
    object_acc[...] = jnp.zeros_like(object_acc)

    def back(m):
        at = pl.ds(pl.multiple_of(m * 8, 8), 8)
        values = [(store[c, at, pl.ds(0, LANES)], store[c, at, pl.ds(LANES, LANES)]) for c in range(LEAD)]
        return [(real, -imag) for real, imag in dft16(values, 1)]

    def probe_term(m, carry):
        position = lax.div(m, chunks)
        offset = pl.multiple_of(lax.rem(m, chunks) * 8, 8)
        rows = pl.ds(offset, 8)
        entry = 2 * lax.bitwise_xor(own, position)
        tile, shift = lane_parts(shifts[entry + 1])
        start = own_start + shifts[entry] + offset
        patch_r = shifted_tiles(object_window, 0, start, tile, shift)
        patch_i = shifted_tiles(object_window, 1, start, tile, shift)
        for a, (real, imag) in enumerate(back(m)):
            lanes = pl.ds(a * LANES, LANES)
            probe_acc[0, rows, lanes] += patch_r[a] * real + patch_i[a] * imag
            probe_acc[1, rows, lanes] += patch_r[a] * imag - patch_i[a] * real
        return carry

    lax.fori_loop(0, GROUP * chunks, probe_term, 0)
    lane = lax.broadcasted_iota(jnp.int32, (8, LANES), 1)

    def object_term(m, carry):
        position = lax.div(m, chunks)
        offset = pl.multiple_of(lax.rem(m, chunks) * 8, 8)
        rows = pl.ds(offset, 8)
        entry = 2 * lax.bitwise_xor(own, position)
        tile, shift = lane_parts(shifts[entry + 1])
        start = ROWS + own_start - shifts[entry] + offset
        rolled = []
        for a, (real, imag) in enumerate(back(GROUP * chunks + m)):
            lanes = pl.ds(a * LANES, LANES)
            probe_real = eight_rows(probe_window, 0, start, lanes)
            probe_imag = eight_rows(probe_window, 1, start, lanes)
            rolled.append(
                (
                    pltpu.roll(probe_real * real + probe_imag * imag, shift, 1),
                    pltpu.roll(probe_real * imag - probe_imag * real, shift, 1),
                )
            )
        keep = lane >= shift
        for j in range(LEAD + 1):
            lanes = pl.ds(pl.multiple_of((tile + j) * LANES, LANES), LANES)
            for half in range(2):
                here = rolled[j][half] if j < LEAD else 0.0
                left = rolled[j - 1][half] if j > 0 else 0.0
                object_acc[half, rows, lanes] += jnp.where(keep, here, left)
        return carry

    lax.fori_loop(0, GROUP * chunks, object_term, 0)
    own = object_acc.shape[2] // LANES * LANES
    width = LANES + LANES // 8
    for b in range(LEAD):
        for half in range(2):
            out[b, pl.ds(half * PART, PART)] = probe_acc[half, :, pl.ds(b * LANES, LANES)]
            out[b, pl.ds((2 + half) * PART, PART)] = object_acc[half, :, pl.ds(b * width, LANES)]
        pieces = []
        for k in range(chunks):
            for half in range(2):
                pieces.append(object_acc[half, pl.ds(8 * k, 8), pl.ds(b * width + LANES, width - LANES)])
        out[b, pl.ds(4 * PART, 8)] = jnp.concatenate(pieces, 1)


def total_kernel(terms, probe_r, probe_i, object_r, object_i):
    width = LANES // 8
    totals = []
    for part in range(GROUP):
        total = terms[part]
        for high in range(1, LEAD // GROUP):
            total = total + terms[high * GROUP + part]
        totals.append(total)
    for half, (probe_out, object_out) in enumerate(((probe_r, object_r), (probe_i, object_i))):
        for part in range(GROUP):
            probe_out[pl.ds(part * PART, PART)] = totals[part][half * PART : (half + 1) * PART]
        left = [totals[part][(2 + half) * PART : (3 + half) * PART] for part in range(GROUP)]
        object_out[pl.ds(0, LANES)] = jnp.concatenate(left, 0).T
        right = []
        for part in range(GROUP):
            for k in range(PART // 8):
                at = (2 * k + half) * width
                right.append(totals[part][4 * PART : 4 * PART + 8, at : at + width])
        object_out[pl.ds(LANES, width)] = jnp.concatenate(right, 0).T


SMEM = pl.BlockSpec(memory_space=pltpu.SMEM)
VMEM = pl.BlockSpec(memory_space=pltpu.VMEM)
ANY = pl.BlockSpec(memory_space=pl.ANY)
PARAMS = pltpu.CompilerParams(vmem_limit_bytes=VMEM_LIMIT)


def shape(*sizes):
    return jax.ShapeDtypeStruct(sizes, F32)


def passed_along(value, by):
    size = lax.axis_size("row")
    return lax.ppermute(value, "row", [(i, (i + by) % size) for i in range(size)])


def per_device(tables, probe_r, probe_i, object_r, object_i, amplitudes, row_shift, col_shift):
    right_high, right_low, left_high, left_low = tables
    width = object_r.shape[1]
    field = probe_r.shape[1]
    group = ("zl", "yl")
    below_r, below_i = passed_along(object_r, -1), passed_along(object_i, -1)
    own = lax.axis_index(group).astype(jnp.int32)
    own_shift = jnp.concatenate([row_shift, col_shift])
    others = [
        lax.ppermute(own_shift, group, [(i, i ^ by) for i in range(GROUP)]) for by in range(1, GROUP)
    ]
    all_shifts = jnp.concatenate([own_shift] + others + [own[None]])
    measured = amplitudes[0].reshape(ROWS, LEAD, LANES).transpose(1, 0, 2)
    measured = lax.all_to_all(measured, "row", 0, 0, tiled=True)

    below_r, below_i, late_r, late_i = lax.optimization_barrier((below_r, below_i, probe_r, probe_i))
    above_r, above_i = passed_along(late_r, 1), passed_along(late_i, 1)
    exit_spread = pl.pallas_call(
        exit_kernel,
        out_shape=shape(LEAD, 2, ROWS, LANES),
        in_specs=[SMEM, VMEM, VMEM, ANY, ANY, ANY, ANY, VMEM, VMEM],
        out_specs=VMEM,
        scratch_shapes=[
            pltpu.VMEM((2, 2 * ROWS, width), F32),
            pltpu.VMEM((LEAD, ROWS, 2 * LANES), F32),
            pltpu.SemaphoreType.DMA((4,)),
        ],
        compiler_params=PARAMS,
        name="exit_kernel",
    )(all_shifts, probe_r, probe_i, object_r, object_i, below_r, below_i, right_high, right_low)
    columns = lax.all_to_all(exit_spread, "row", 0, 0, tiled=True)
    columns, above_r, above_i = lax.optimization_barrier((columns, above_r, above_i))
    returned = pl.pallas_call(
        detector_kernel,
        out_shape=shape(GROUP * LEAD, 4, PART, LANES),
        in_specs=[SMEM, VMEM, VMEM, VMEM, VMEM],
        out_specs=VMEM,
        scratch_shapes=[
            pltpu.VMEM((LEAD, 2 * ROWS, LANES), F32),
            pltpu.VMEM((2, (LEAD + 1) * ROWS, LANES), F32),
        ],
        compiler_params=PARAMS,
        name="detector_kernel",
    )(all_shifts, columns, measured, left_high, left_low)
    rows_in = lax.all_to_all(returned, group + ("row",), 0, 0, tiled=True)
    terms = pl.pallas_call(
        gradient_kernel,
        out_shape=shape(LEAD, 4 * PART + 8, LANES),
        in_specs=[SMEM, VMEM] + [ANY] * 8 + [VMEM, VMEM],
        out_specs=VMEM,
        scratch_shapes=[
            pltpu.VMEM((2, 2 * ROWS, field), F32),
            pltpu.VMEM((2, 2 * ROWS, width), F32),
            pltpu.VMEM((LEAD, 2 * ROWS, 2 * LANES), F32),
            pltpu.VMEM((2, PART, field), F32),
            pltpu.VMEM((2, PART, width + LANES), F32),
            pltpu.SemaphoreType.DMA((8,)),
        ],
        compiler_params=PARAMS,
        name="gradient_kernel",
    )(
        all_shifts, rows_in, probe_r, probe_i, above_r, above_i, object_r, object_i, below_r, below_i,
        right_high, right_low,
    )
    terms = lax.all_to_all(terms, ("zh",) + group, 0, 0, tiled=True)
    own_width = width // LEAD
    probe_r, probe_i, object_r, object_i = pl.pallas_call(
        total_kernel,
        out_shape=(shape(ROWS, LANES), shape(ROWS, LANES), shape(own_width, ROWS), shape(own_width, ROWS)),
        in_specs=[VMEM],
        out_specs=(VMEM, VMEM, VMEM, VMEM),
        compiler_params=PARAMS,
        name="total_kernel",
    )(terms)
    return probe_r, probe_i, object_r.T, object_i.T


def solution(mesh):
    fine = Mesh(mesh.devices.reshape(4, 2, 2, LEAD), ("zh", "zl", "yl", "row"))
    batch = ("zh", "zl", "yl")
    tables = propagation_tables(LEAD * LANES)

    def step(*arguments):
        held = tuple(jnp.asarray(table) for table in tables)
        return functools.partial(per_device, held)(*arguments)

    placed = (
        P("row", None),
        P("row", None),
        P("row", None),
        P("row", None),
        P(batch, "row", None),
        P(batch),
        P(batch),
    )
    return jax.shard_map(
        step,
        mesh=fine,
        in_specs=placed,
        out_specs=(P("row", batch),) * 4,
        check_vma=False,
    )
```

time: 659 us -> 247 us (0.37)
  the two profiles are of different devices: /device:TPU:4 before, /device:TPU:1 now
where the time goes in v1:
time: 247 us
  blocking collectives  100 us (40%)
  waiting for transfers between devices  69.5 us (28%)
  Pallas kernels  42.4 us (17%)
  starting transfers between devices  27.2 us (11%)
  local copies, waits for them, and re-layouts  5.49 us (2%)
    all_to_all x1, blocking collectives, per_device(): rows_in = lax.all_to_all(returned, group + ('row',), 0, 0, tiled=True)  58.9 us
    all_to_all x1, blocking collectives, per_device(): terms = lax.all_to_all(terms, ('zh',) + group, 0, 0, tiled=True)  41.3 us
    ppermute x4, waiting for transfers between devices, passed_along(): lax.ppermute(value, 'row', [(i, (i + by) % size) for i in range(size)])  39.7 us
    all_to_all x1, waiting for transfers between devices, per_device(): columns = lax.all_to_all(exit_spread, 'row', 0, 0, tiled=True)  22.3 us
    pallas_call x1, Pallas kernels, per_device(): pl.pallas_call(gradient_kernel, out_shape=shape(LEAD, 4 * PART + 8, LANES...  16.9 us
    pallas_call x1, Pallas kernels, per_device(): pl.pallas_call(detector_kernel, out_shape=shape(GROUP * LEAD, 4, PART, LA...  12.6 us
    pallas_call x1, Pallas kernels, per_device(): pl.pallas_call(exit_kernel, out_shape=shape(LEAD, 2, ROWS, LANES), in_spe...  10.8 us
    ppermute x4, starting transfers between devices, passed_along(): lax.ppermute(value, 'row', [(i, (i + by) % size) for i in range(size)])  9.7 us
  transfers between devices with their start and end apart: 9, of which 9 were waited for; matrix products, arithmetic and copies ran while one was open for 1% of the time, Pallas kernels for 0%

profile of v1, /device:TPU:1, one launch (start us, length us, event | category | flops | bytes accessed | tf_op | source)
XLA Modules:
  0.0 246.8 jit_solution(15503381307513241249)
XLA Ops:
  0.6 3.3 %collective-permute-start.3 = (f32[128,2304]{1,0:T(8,128)}, f32[128,2304]{1,0:T(8,128)S(1)}, u32[]{:S(2)}, u32[]{:S(2)}) collective-permute-start(f32[128,2304]{1,0:T(8,128)} %object_r.3), channel_id=1, source_target_pairs={{0,15},{1,0},{2,1},{3,2},{4,3},{5,4},{6,5},{7,6},{8,7},{9,8},{10,9... | collective-permute-start | bytes 3538952 | tf_op jit(solution)/shard_map/ppermute | solution.py:407
  3.9 3.1 %collective-permute-start.4 = (f32[128,2304]{1,0:T(8,128)}, f32[128,2304]{1,0:T(8,128)S(1)}, u32[]{:S(2)}, u32[]{:S(2)}) collective-permute-start(f32[128,2304]{1,0:T(8,128)} %object_i.3), channel_id=1, source_target_pairs={{0,15},{1,0},{2,1},{3,2},{4,3},{5,4},{6,5},{7,6},{8,7},{9,8},{10,9... | collective-permute-start | bytes 3538952 | tf_op jit(solution)/shard_map/ppermute | solution.py:407
  8.3 0.1 pad_add_fusion
  8.4 1.8 collective-permute-start.2
  10.2 0.0 collective-permute-start.1
  10.2 1.1 collective-permute-start
  11.3 0.5 collective-permute-done.2
  11.7 0.8 collective-permute-done.1
  12.6 0.1 collective-permute-done
  12.6 0.6 concatenate.8.shifts
  13.2 5.9 %collective-permute-done.3.below_r = f32[128,2304]{1,0:T(8,128)S(1)} collective-permute-done((f32[128,2304]{1,0:T(8,128)}, f32[128,2304]{1,0:T(8,128)S(1)}, u32[]{:S(2)}, u32[]{:S(2)}) %collective-permute-start.3) | collective-permute-done | bytes 1179680 | tf_op jit(solution)/shard_map/ppermute | solution.py:407
  19.1 12.6 %collective-permute-done.4.below_i = f32[128,2304]{1,0:T(8,128)S(1)} collective-permute-done((f32[128,2304]{1,0:T(8,128)}, f32[128,2304]{1,0:T(8,128)S(1)}, u32[]{:S(2)}, u32[]{:S(2)}) %collective-permute-start.4) | collective-permute-done | bytes 1179680 | tf_op jit(solution)/shard_map/ppermute | solution.py:407
  31.8 0.0 copy-done.1
  31.8 1.1 copy-done.2
  32.8 10.8 %exit_kernel.1 = f32[16,2,128,128]{3,2,1,0:T(8,128)} custom-call(s32[9]{0:T(128)} %concatenate.8.shifts, f32[128,2048]{1,0:T(8,128)} %probe_r.3, f32[128,2048]{1,0:T(8,128)} %probe_i.3, f32[128,2304]{1,0:T(8,128)} %object_r.3, f32[128,2304]{1,0:T(8,128)} %object_i.3, f32[128,2304]{1,0:T(8,128)} %copy-done.1, f32[128,2304]{1,0:T(8,128)} %copy-done.2, ...), custom_call_target="tpu_custom_call" | custom-call | tf_op jit(solution)/shard_map/exit_kernel/pallas_call | solution.py:427
  43.6 8.7 %all-to-all-start = ((f32[16,2,128,128]{3,2,1,0:T(8,128)}), f32[16,2,128,128]{3,2,1,0:T(8,128)S(1)}, u32[]{:S(2)}, u32[]{:S(2)}) async-start(f32[16,2,128,128]{3,2,1,0:T(8,128)} %exit_kernel.1), calls=%async_computation | async-start | bytes 4194304 | tf_op jit(solution)/shard_map/all_to_all | solution.py:440
  52.3 3.1 %collective-permute-start.5 = (f32[128,2048]{1,0:T(8,128)}, f32[128,2048]{1,0:T(8,128)}, u32[]{:S(2)}, u32[]{:S(2)}) collective-permute-start(f32[128,2048]{1,0:T(8,128)} %probe_r.3), channel_id=1, source_target_pairs={{0,1},{1,2},{2,3},{3,4},{4,5},{5,6},{6,7},{7,8},{8,9},{9,10},{10,1... | collective-permute-start | bytes 3145736 | tf_op jit(solution)/shard_map/ppermute | solution.py:407
  55.4 0.1 collective-permute-start.6
  55.6 1.5 copy.15
  57.2 1.3 copy.16
  58.5 22.3 %all-to-all-done.columns = f32[16,2,128,128]{3,2,1,0:T(8,128)S(1)} async-done(((f32[16,2,128,128]{3,2,1,0:T(8,128)}), f32[16,2,128,128]{3,2,1,0:T(8,128)S(1)}, u32[]{:S(2)}, u32[]{:S(2)}) %all-to-all-start) | async-done | bytes 2097184 | tf_op jit(solution)/shard_map/all_to_all | solution.py:440
  80.8 6.0 %all-to-all-start.1 = ((f32[16,128,128]{2,1,0:T(8,128)}), f32[16,128,128]{2,1,0:T(8,128)S(1)}, u32[]{:S(2)}, u32[]{:S(2)}) async-start(f32[16,128,128]{2,1,0:T(8,128)} %bitcast.5), calls=%async_computation.1 | async-start | bytes 2097152 | tf_op jit(solution)/shard_map/all_to_all | solution.py:423
  86.8 0.1 collective-permute-done.5.above_r
  86.8 21.1 %collective-permute-done.6.above_i = f32[128,2048]{1,0:T(8,128)} collective-permute-done((f32[128,2048]{1,0:T(8,128)}, f32[128,2048]{1,0:T(8,128)}, u32[]{:S(2)}, u32[]{:S(2)}) %collective-permute-start.6) | collective-permute-done | bytes 1048608 | tf_op jit(solution)/shard_map/ppermute | solution.py:407
  107.9 6.2 %all-to-all-done.1.measured = f32[16,128,128]{2,1,0:T(8,128)S(1)} async-done(((f32[16,128,128]{2,1,0:T(8,128)}), f32[16,128,128]{2,1,0:T(8,128)S(1)}, u32[]{:S(2)}, u32[]{:S(2)}) %all-to-all-start.1) | async-done | bytes 1048608 | tf_op jit(solution)/shard_map/all_to_all | solution.py:423
  114.1 0.0 copy-done
  114.1 1.0 copy-done.3
  115.1 12.6 %detector_kernel.1 = f32[64,4,32,128]{3,2,1,0:T(8,128)} custom-call(s32[9]{0:T(128)} %concatenate.8.shifts, f32[16,2,128,128]{3,2,1,0:T(8,128)} %copy-done, f32[16,128,128]{2,1,0:T(8,128)} %copy-done.3, bf16[16,256,256]{2,1,0:T(8,128)(2,1)} %constant.22.clone.table_high, bf16[16,256,256]{2,1,0:T(8,128)(2,1)} %constant.23.clone.table_low), custom_call_target="tpu_custom_call" | custom-call | tf_op jit(solution)/shard_map/detector_kernel/pallas_call | solution.py:442
  127.7 58.9 %all_to_all.20.rows_in = f32[64,4,32,128]{3,2,1,0:T(8,128)} all-to-all(f32[64,4,32,128]{3,2,1,0:T(8,128)} %detector_kernel.1), channel_id=1, replica_groups=mesh['zh'=4,'zl'=2,'yl'=2,'row'=16] {'zl','yl','row'}, dimensions={0} | all-to-all | bytes 8388608 | tf_op jit(solution)/shard_map/all_to_all | solution.py:454
  186.5 16.9 %gradient_kernel.1 = f32[16,136,128]{2,1,0:T(8,128)} custom-call(s32[9]{0:T(128)} %concatenate.8.shifts, f32[64,4,32,128]{3,2,1,0:T(8,128)} %all_to_all.20.rows_in, f32[128,2048]{1,0:T(8,128)} %probe_r.3, f32[128,2048]{1,0:T(8,128)} %probe_i.3, f32[128,2048]{1,0:T(8,128)} %collective-permute-done.5.above_r, f32[128,2048]{1,0:T(8,128)} %collective-permute-done.6.above_i, ...), custom_call_target="tpu_custom_call" | custom-call | tf_op jit(solution)/shard_map/gradient_kernel/pallas_call | solution.py:455
  203.4 41.3 %all_to_all.21.terms = f32[16,136,128]{2,1,0:T(8,128)} all-to-all(f32[16,136,128]{2,1,0:T(8,128)} %gradient_kernel.1), channel_id=1, replica_groups=mesh['zh'=4,'zl'=2,'yl'=2,'row'=16] {'zh','zl','yl'}, dimensions={0} | all-to-all | bytes 2228224 | tf_op jit(solution)/shard_map/all_to_all | solution.py:474
  244.7 2.1 total_kernel.1
  (4 shorter events, 0.0 us)
Async XLA Ops:
  0.6 18.5 %collective-permute-start.3 = (f32[128,2304]{1,0:T(8,128)}, f32[128,2304]{1,0:T(8,128)S(1)}, u32[]{:S(2)}, u32[]{:S(2)}) collective-permute-start(f32[128,2304]{1,0:T(8,128)} %object_r.3), channel_id=1, source_target_pairs={{0,15},{1,0},{2,1},{3,2},{4,3},{5,4},{6,5},{7,6},{8,7},{9,8},{10,9... | collective-permute-start | bytes 3538952 | tf_op jit(solution)/shard_map/ppermute | solution.py:407
  3.9 27.8 %collective-permute-start.4 = (f32[128,2304]{1,0:T(8,128)}, f32[128,2304]{1,0:T(8,128)S(1)}, u32[]{:S(2)}, u32[]{:S(2)}) collective-permute-start(f32[128,2304]{1,0:T(8,128)} %object_i.3), channel_id=1, source_target_pairs={{0,15},{1,0},{2,1},{3,2},{4,3},{5,4},{6,5},{7,6},{8,7},{9,8},{10,9... | collective-permute-start | bytes 3538952 | tf_op jit(solution)/shard_map/ppermute | solution.py:407
  8.4 3.3 %collective-permute-start.2 = (s32[2]{0:T(128)S(1)}, s32[2]{0:T(128)S(1)}, u32[]{:S(2)}, u32[]{:S(2)}) collective-permute-start(s32[2]{0:T(128)S(1)} %pad_add_fusion), channel_id=1, source_target_pairs={{0,48},{16,32},{32,16},{48,0},{1,49},{17,33},{33,17},{49,1},{2,50}... | collective-permute-start | bytes 32 | tf_op jit(solution)/shard_map/ppermute | solution.py:419
  10.2 2.4 collective-permute-start.1
  10.2 2.4 collective-permute-start
  19.1 12.6 %copy-start.1 = (f32[128,2304]{1,0:T(8,128)}, f32[128,2304]{1,0:T(8,128)S(1)}, u32[]{:S(2)}) copy-start(f32[128,2304]{1,0:T(8,128)S(1)} %collective-permute-done.3.below_r) | copy-start | bytes 3538948
  31.8 1.1 copy-start.2
  43.6 37.1 %all-to-all-start = ((f32[16,2,128,128]{3,2,1,0:T(8,128)}), f32[16,2,128,128]{3,2,1,0:T(8,128)S(1)}, u32[]{:S(2)}, u32[]{:S(2)}) async-start(f32[16,2,128,128]{3,2,1,0:T(8,128)} %exit_kernel.1), calls=%async_computation | async-start | bytes 4194304 | tf_op jit(solution)/shard_map/all_to_all | solution.py:440
  52.3 34.5 %collective-permute-start.5 = (f32[128,2048]{1,0:T(8,128)}, f32[128,2048]{1,0:T(8,128)}, u32[]{:S(2)}, u32[]{:S(2)}) collective-permute-start(f32[128,2048]{1,0:T(8,128)} %probe_r.3), channel_id=1, source_target_pairs={{0,1},{1,2},{2,3},{3,4},{4,5},{5,6},{6,7},{7,8},{8,9},{9,10},{10,1... | collective-permute-start | bytes 3145736 | tf_op jit(solution)/shard_map/ppermute | solution.py:407
  55.4 52.5 %collective-permute-start.6 = (f32[128,2048]{1,0:T(8,128)}, f32[128,2048]{1,0:T(8,128)}, u32[]{:S(2)}, u32[]{:S(2)}) collective-permute-start(f32[128,2048]{1,0:T(8,128)} %probe_i.3), channel_id=1, source_target_pairs={{0,1},{1,2},{2,3},{3,4},{4,5},{5,6},{6,7},{7,8},{8,9},{9,10},{10,1... | collective-permute-start | bytes 3145736 | tf_op jit(solution)/shard_map/ppermute | solution.py:407
  80.8 33.4 %copy-start = (f32[16,2,128,128]{3,2,1,0:T(8,128)}, f32[16,2,128,128]{3,2,1,0:T(8,128)S(1)}, u32[]{:S(2)}) copy-start(f32[16,2,128,128]{3,2,1,0:T(8,128)S(1)} %all-to-all-done.columns) | copy-start | bytes 6291460
  80.8 33.4 %all-to-all-start.1 = ((f32[16,128,128]{2,1,0:T(8,128)}), f32[16,128,128]{2,1,0:T(8,128)S(1)}, u32[]{:S(2)}, u32[]{:S(2)}) async-start(f32[16,128,128]{2,1,0:T(8,128)} %bitcast.5), calls=%async_computation.1 | async-start | bytes 2097152 | tf_op jit(solution)/shard_map/all_to_all | solution.py:423
  114.1 1.0 copy-start.3

commit v2 on v1

--- a/solution.py
+++ b/solution.py
@@ -17,7 +17,7 @@
 ROWS = 128
 GROUP = 4
 PART = ROWS // GROUP
-VMEM_LIMIT = 56 * 1024 * 1024
+MEBI = 1024 * 1024
 
 
 def split_pair(table):
@@ -151,27 +151,58 @@
     return [jnp.where(keep, rolled[j], rolled[j + 1]) for j in range(LEAD)]
 
 
-def fetch(pairs, sems):
-    copies = [pltpu.make_async_copy(src, dst, sems.at[n]) for n, (src, dst) in enumerate(pairs)]
+def block_copies(window, block, at, sems):
+    rows = block[0].shape[0]
+    return [
+        pltpu.make_async_copy(block[half], window.at[half, pl.ds(at, rows)], sems.at[half])
+        for half in range(2)
+    ]
+
+
+def halo_copies(window, halo, at, shifts, sems):
+    near = block_copies(window, halo[:2], at, sems.at[0])
+    far = []
+    for by in range(GROUP):
+        part = halo[2 + by]
+        place = pl.multiple_of(at + PART * lax.bitwise_xor(shifts[2 * GROUP + 2], by), PART)
+        far += block_copies(window, (part.at[0], part.at[1]), place, sems.at[by])
+    return near, far
+
+
+def run_all(copies, method):
     for copy in copies:
-        copy.start()
-    for copy in copies:
-        copy.wait()
+        getattr(copy, method)()
+
+
+def run_halo(copies, from_chip, method):
+    @pl.when(from_chip)
+    def _():
+        run_all(copies[0], method)
+
+    @pl.when(jnp.logical_not(from_chip))
+    def _():
+        run_all(copies[1], method)
 
 
 def exit_kernel(
-    shifts, probe_r, probe_i, object_r, object_i, below_r, below_i, table_high, table_low, out,
-    window, store, sems,
+    shifts, probe_r, probe_i, object_r, object_i, below_r, below_i, measured, high_in, low_in, out,
+    window, probe, table_high, table_low, store, spread, sems, table_sems, measured_sems, out_sems,
 ):
-    fetch(
-        [
-            (object_r, window.at[0, pl.ds(0, ROWS)]),
-            (object_i, window.at[1, pl.ds(0, ROWS)]),
-            (below_r, window.at[0, pl.ds(ROWS, ROWS)]),
-            (below_i, window.at[1, pl.ds(ROWS, ROWS)]),
-        ],
-        sems,
-    )
+    fields = block_copies(window, (object_r, object_i), 0, sems.at[0])
+    fields += block_copies(window, (below_r, below_i), ROWS, sems.at[1])
+    fields += block_copies(probe, (probe_r, probe_i), 0, sems.at[2])
+    tables = [
+        pltpu.make_async_copy(source, target, table_sems.at[n])
+        for n, (source, target) in enumerate(((high_in, table_high), (low_in, table_low)))
+    ]
+    passing = [
+        pltpu.make_async_copy(measured.at[0, :, pl.ds(a * LANES, LANES)], spread.at[a, 2], measured_sems.at[a])
+        for a in range(LEAD)
+    ]
+    run_all(fields, "start")
+    run_all(tables, "start")
+    run_all(passing, "start")
+    run_all(fields, "wait")
     row_shift = shifts[0]
     tile, shift = lane_parts(shifts[1])
 
@@ -183,7 +214,7 @@
         values = []
         for a in range(LEAD):
             lanes = pl.ds(a * LANES, LANES)
-            real, imag = probe_r[rows, lanes], probe_i[rows, lanes]
+            real, imag = probe[0, rows, lanes], probe[1, rows, lanes]
             values.append(
                 (real * patch_r[a] - imag * patch_i[a], real * patch_i[a] + imag * patch_r[a])
             )
@@ -193,21 +224,43 @@
         return carry
 
     lax.fori_loop(0, ROWS // 8, gather, 0)
+    run_all(tables, "wait")
     mix_right(store, table_high, table_low)
 
-    def spread(k, carry):
+    def scatter(k, carry):
         rows = pl.ds(pl.multiple_of(k * 8, 8), 8)
         values = [(store[c, rows, pl.ds(0, LANES)], store[c, rows, pl.ds(LANES, LANES)]) for c in range(LEAD)]
         for a, (real, imag) in enumerate(dft16(values, 1)):
-            out[a, 0, rows] = real
-            out[a, 1, rows] = imag
-        return carry
-
-    lax.fori_loop(0, ROWS // 8, spread, 0)
-
-
-def detector_kernel(shifts, columns, measured, table_high, table_low, out, store, wrapped):
-    row_shift = shifts[0]
+            spread[a, 0, rows] = real
+            spread[a, 1, rows] = imag
+        return carry
+
+    run_all(passing, "wait")
+    sends = []
+    for part in range(GROUP):
+        lax.fori_loop(part * PART // 8, (part + 1) * PART // 8, scatter, 0)
+        rows = pl.ds(part * PART, PART)
+        send = pltpu.make_async_copy(spread.at[:, :, rows], out.at[:, :, rows], out_sems.at[part])
+        send.start()
+        sends.append(send)
+    run_all(sends, "wait")
+
+
+def detector_kernel(
+    shifts, columns_in, high_in, low_in, out, columns, table_high, table_low, store, wrapped, straight,
+    shifted, sems, table_sems, out_sems,
+):
+    pieces = [pl.ds(part * PART, PART) for part in range(GROUP)]
+    arriving = [
+        pltpu.make_async_copy(columns_in.at[:, :, rows], columns.at[:, :, rows], sems.at[part])
+        for part, rows in enumerate(pieces)
+    ]
+    tables = [
+        pltpu.make_async_copy(source, target, table_sems.at[n])
+        for n, (source, target) in enumerate(((high_in, table_high), (low_in, table_low)))
+    ]
+    run_all(arriving, "start")
+    run_all(tables, "start")
 
     def load(c, k):
         at = pl.multiple_of(k * 8, 8)
@@ -223,14 +276,17 @@
         save(dft16([(columns[a, 0, rows], columns[a, 1, rows]) for a in range(LEAD)], -1), k)
         return carry
 
-    lax.fori_loop(0, ROWS // 8, first, 0)
+    for part in range(GROUP):
+        arriving[part].wait()
+        lax.fori_loop(part * PART // 8, (part + 1) * PART // 8, first, 0)
+    run_all(tables, "wait")
     mix_left(store, table_high, table_low)
 
     def modulus(k, carry):
         rows = pl.ds(pl.multiple_of(k * 8, 8), 8)
         residual = []
         for a, (real, imag) in enumerate(dft16([load(c, k) for c in range(LEAD)], 1)):
-            share = measured[a, rows] * lax.rsqrt(jnp.maximum(real * real + imag * imag, 0.0625))
+            share = columns[a, 2, rows] * lax.rsqrt(jnp.maximum(real * real + imag * imag, 0.0625))
             keep = 1.0 - share
             residual.append((real * keep, -imag * keep))
         save(dft16(residual, -1), k)
@@ -240,50 +296,65 @@
     mix_left(store, table_high, table_low)
 
     def last(k, carry):
+        rows = pl.ds(pl.multiple_of(k * 8, 8), 8)
         for a, (real, imag) in enumerate(dft16([load(c, k) for c in range(LEAD)], 1)):
             at = pl.multiple_of((a + 1) * ROWS + k * 8, 8)
-            wrapped[0, pl.ds(at, 8)] = real
-            wrapped[1, pl.ds(at, 8)] = -imag
-            if a == LEAD - 1:
-                first_at = pl.multiple_of(k * 8, 8)
-                wrapped[0, pl.ds(first_at, 8)] = real
-                wrapped[1, pl.ds(first_at, 8)] = -imag
-        return carry
-
-    lax.fori_loop(0, ROWS // 8, last, 0)
-
-    def place(n, carry):
-        part = lax.div(n, LEAD)
-        start = ROWS * (n - part * LEAD + 1) + PART * part
-        aligned = pl.multiple_of(start, 8)
-        for half in range(2):
-            out[n, half] = wrapped[half, pl.ds(aligned, PART)]
-            for k in range(PART // 8):
-                out[n, 2 + half, pl.ds(8 * k, 8)] = eight_rows(
-                    wrapped, half, start - row_shift + 8 * k, slice(None)
-                )
-        return carry
-
-    lax.fori_loop(0, GROUP * LEAD, place, 0)
-
-
-def gradient_kernel(
-    shifts, rows_in, probe_r, probe_i, above_r, above_i, object_r, object_i, below_r, below_i,
-    table_high, table_low, out, probe_window, object_window, store, probe_acc, object_acc, sems,
-):
-    fetch(
-        [
-            (above_r, probe_window.at[0, pl.ds(0, ROWS)]),
-            (above_i, probe_window.at[1, pl.ds(0, ROWS)]),
-            (probe_r, probe_window.at[0, pl.ds(ROWS, ROWS)]),
-            (probe_i, probe_window.at[1, pl.ds(ROWS, ROWS)]),
-            (object_r, object_window.at[0, pl.ds(0, ROWS)]),
-            (object_i, object_window.at[1, pl.ds(0, ROWS)]),
-            (below_r, object_window.at[0, pl.ds(ROWS, ROWS)]),
-            (below_i, object_window.at[1, pl.ds(ROWS, ROWS)]),
-        ],
-        sems,
-    )
+            for half, value in enumerate((real, -imag)):
+                straight[half, a, rows] = value
+                wrapped[half, pl.ds(at, 8)] = value
+                if a == LEAD - 1:
+                    wrapped[half, rows] = value
+        return carry
+
+    sends = []
+
+    def send(source, half, part):
+        target = out.at[pl.ds(part * LEAD, LEAD), half]
+        copy = pltpu.make_async_copy(source.at[half % 2, :, pieces[part]], target, out_sems.at[half, part])
+        copy.start()
+        sends.append(copy)
+
+    for part in range(GROUP):
+        lax.fori_loop(part * PART // 8, (part + 1) * PART // 8, last, 0)
+        send(straight, 0, part)
+        send(straight, 1, part)
+    base = lax.div(shifts[0] + 7, 8) * 8
+    keep = lax.broadcasted_iota(jnp.int32, (8, LANES), 0) < 8 - (base - shifts[0])
+    back = lax.rem(8 - (base - shifts[0]), 8)
+    limit = wrapped.shape[1] - 8
+
+    for part in range(GROUP):
+
+        def place(a, carry):
+            start = (a + 1) * ROWS + part * PART - base
+            for half in range(2):
+                rolled = []
+                for k in range(PART // 8 + 1):
+                    at = pl.multiple_of(jnp.minimum(start + 8 * k, limit), 8)
+                    rolled.append(pltpu.roll(wrapped[half, pl.ds(at, 8)], back, 0))
+                for k in range(PART // 8):
+                    rows = pl.ds(part * PART + 8 * k, 8)
+                    shifted[half, a, rows] = jnp.where(keep, rolled[k], rolled[k + 1])
+            return carry
+
+        lax.fori_loop(0, LEAD, place, 0)
+        send(shifted, 2, part)
+        send(shifted, 3, part)
+    run_all(sends, "wait")
+
+
+def gradient_kernel(shifts, rows_in, *refs):
+    halo = 2 + GROUP
+    object_own, object_below = refs[2 + halo : 4 + halo], refs[4 + halo : 6 + halo]
+    table_high, table_low, out = refs[6 + halo : 9 + halo]
+    probe_window, object_window, store, probe_acc, object_acc, sems, halo_sems = refs[9 + halo :]
+    core = shifts[2 * GROUP + 1]
+    held = block_copies(probe_window, refs[:2], ROWS, sems.at[0])
+    held += block_copies(object_window, object_own, 0, sems.at[1])
+    held += block_copies(object_window, object_below, ROWS, sems.at[2])
+    moved = halo_copies(probe_window, refs[2 : 2 + halo], 0, shifts, halo_sems)
+    run_all(held, "start")
+    run_halo(moved, core == 1, "start")
     own = shifts[2 * GROUP]
     own_start = own * PART
     chunks = PART // 8
@@ -304,6 +375,8 @@
 
     lax.fori_loop(0, 2 * GROUP * chunks, first, 0)
     mix_right(store, table_high, table_low)
+    run_all(held, "wait")
+    run_halo(moved, core == 1, "wait")
     probe_acc[...] = jnp.zeros_like(probe_acc)
     object_acc[...] = jnp.zeros_like(object_acc)
 
@@ -395,16 +468,40 @@
 SMEM = pl.BlockSpec(memory_space=pltpu.SMEM)
 VMEM = pl.BlockSpec(memory_space=pltpu.VMEM)
 ANY = pl.BlockSpec(memory_space=pl.ANY)
-PARAMS = pltpu.CompilerParams(vmem_limit_bytes=VMEM_LIMIT)
+
+
+def params(mebibytes):
+    return pltpu.CompilerParams(vmem_limit_bytes=mebibytes * MEBI)
 
 
 def shape(*sizes):
     return jax.ShapeDtypeStruct(sizes, F32)
 
 
-def passed_along(value, by):
-    size = lax.axis_size("row")
-    return lax.ppermute(value, "row", [(i, (i + by) % size) for i in range(size)])
+def row_pairs(by, inside):
+    pairs = [(r, (r + by) % LEAD) for r in range(LEAD)]
+    return [(a, b) for a, b in pairs if (a // 2 == b // 2) == inside]
+
+
+def fetched_part():
+    return lax.axis_index(("zh", "zl")) % GROUP
+
+
+def own_part(real, imag):
+    at = fetched_part() * PART
+    return jnp.stack([lax.dynamic_slice_in_dim(value, at, PART, 0) for value in (real, imag)])
+
+
+def passed_on(part, takers):
+    parts = [part]
+    for by in range(1, GROUP):
+        pairs = [(z * LEAD + r, (z ^ by) * LEAD + r) for z in range(8) for r in takers]
+        parts.append(lax.ppermute(part, ("zh", "zl", "row"), pairs))
+    return tuple(parts)
+
+
+def together(*values):
+    return lax.optimization_barrier(values)
 
 
 def per_device(tables, probe_r, probe_i, object_r, object_i, amplitudes, row_shift, col_shift):
@@ -412,50 +509,77 @@
     width = object_r.shape[1]
     field = probe_r.shape[1]
     group = ("zl", "yl")
-    below_r, below_i = passed_along(object_r, -1), passed_along(object_i, -1)
+    below_r, below_i = (
+        lax.ppermute(value, "row", row_pairs(-1, False) + row_pairs(-1, True)) for value in (object_r, object_i)
+    )
     own = lax.axis_index(group).astype(jnp.int32)
+    core = lax.axis_index("row").astype(jnp.int32) % 2
+    part = fetched_part().astype(jnp.int32)
     own_shift = jnp.concatenate([row_shift, col_shift])
     others = [
         lax.ppermute(own_shift, group, [(i, i ^ by) for i in range(GROUP)]) for by in range(1, GROUP)
     ]
-    all_shifts = jnp.concatenate([own_shift] + others + [own[None]])
-    measured = amplitudes[0].reshape(ROWS, LEAD, LANES).transpose(1, 0, 2)
-    measured = lax.all_to_all(measured, "row", 0, 0, tiled=True)
-
-    below_r, below_i, late_r, late_i = lax.optimization_barrier((below_r, below_i, probe_r, probe_i))
-    above_r, above_i = passed_along(late_r, 1), passed_along(late_i, 1)
+    all_shifts = jnp.concatenate([own_shift] + others + [own[None], core[None], part[None]])
+    above_part = own_part(probe_r, probe_i)
+    near_above = tuple(lax.ppermute(value, "row", row_pairs(1, True)) for value in (probe_r, probe_i))
+    below_r, below_i, above_part, all_shifts, near_above = together(
+        below_r, below_i, above_part, all_shifts, near_above
+    )
+    above_part = lax.ppermute(above_part, "row", row_pairs(1, False))
     exit_spread = pl.pallas_call(
         exit_kernel,
-        out_shape=shape(LEAD, 2, ROWS, LANES),
-        in_specs=[SMEM, VMEM, VMEM, ANY, ANY, ANY, ANY, VMEM, VMEM],
-        out_specs=VMEM,
+        out_shape=shape(LEAD, 3, ROWS, LANES),
+        in_specs=[SMEM, ANY, ANY, ANY, ANY, ANY, ANY, ANY, ANY, ANY],
+        out_specs=ANY,
         scratch_shapes=[
             pltpu.VMEM((2, 2 * ROWS, width), F32),
+            pltpu.VMEM((2, ROWS, field), F32),
+            pltpu.VMEM(right_high.shape, BF16),
+            pltpu.VMEM(right_low.shape, BF16),
             pltpu.VMEM((LEAD, ROWS, 2 * LANES), F32),
-            pltpu.SemaphoreType.DMA((4,)),
+            pltpu.VMEM((LEAD, 3, ROWS, LANES), F32),
+            pltpu.SemaphoreType.DMA((3, 2)),
+            pltpu.SemaphoreType.DMA((2,)),
+            pltpu.SemaphoreType.DMA((LEAD,)),
+            pltpu.SemaphoreType.DMA((GROUP,)),
         ],
-        compiler_params=PARAMS,
+        compiler_params=params(60),
+        cost_estimate=pl.CostEstimate(flops=int(2e9), bytes_accessed=int(20e6), transcendentals=0),
         name="exit_kernel",
-    )(all_shifts, probe_r, probe_i, object_r, object_i, below_r, below_i, right_high, right_low)
+    )(
+        all_shifts, probe_r, probe_i, object_r, object_i, below_r, below_i, amplitudes, right_high,
+        right_low,
+    )
+    exit_spread, above_part = together(exit_spread, above_part)
     columns = lax.all_to_all(exit_spread, "row", 0, 0, tiled=True)
-    columns, above_r, above_i = lax.optimization_barrier((columns, above_r, above_i))
+    above = passed_on(above_part, range(0, LEAD, 2))
     returned = pl.pallas_call(
         detector_kernel,
         out_shape=shape(GROUP * LEAD, 4, PART, LANES),
-        in_specs=[SMEM, VMEM, VMEM, VMEM, VMEM],
-        out_specs=VMEM,
+        in_specs=[SMEM, ANY, ANY, ANY],
+        out_specs=ANY,
         scratch_shapes=[
+            pltpu.VMEM((LEAD, 3, ROWS, LANES), F32),
+            pltpu.VMEM(left_high.shape, BF16),
+            pltpu.VMEM(left_low.shape, BF16),
             pltpu.VMEM((LEAD, 2 * ROWS, LANES), F32),
             pltpu.VMEM((2, (LEAD + 1) * ROWS, LANES), F32),
+            pltpu.VMEM((2, LEAD, ROWS, LANES), F32),
+            pltpu.VMEM((2, LEAD, ROWS, LANES), F32),
+            pltpu.SemaphoreType.DMA((GROUP,)),
+            pltpu.SemaphoreType.DMA((2,)),
+            pltpu.SemaphoreType.DMA((4, GROUP)),
         ],
-        compiler_params=PARAMS,
+        compiler_params=params(60),
+        cost_estimate=pl.CostEstimate(flops=4000000000, bytes_accessed=36000000, transcendentals=0),
         name="detector_kernel",
-    )(all_shifts, columns, measured, left_high, left_low)
+    )(all_shifts, columns, left_high, left_low)
+    returned, above = together(returned, above)
     rows_in = lax.all_to_all(returned, group + ("row",), 0, 0, tiled=True)
     terms = pl.pallas_call(
         gradient_kernel,
         out_shape=shape(LEAD, 4 * PART + 8, LANES),
-        in_specs=[SMEM, VMEM] + [ANY] * 8 + [VMEM, VMEM],
+        in_specs=[SMEM, VMEM] + [ANY] * (8 + GROUP) + [VMEM, VMEM],
         out_specs=VMEM,
         scratch_shapes=[
             pltpu.VMEM((2, 2 * ROWS, field), F32),
@@ -463,12 +587,14 @@
             pltpu.VMEM((LEAD, 2 * ROWS, 2 * LANES), F32),
             pltpu.VMEM((2, PART, field), F32),
             pltpu.VMEM((2, PART, width + LANES), F32),
-            pltpu.SemaphoreType.DMA((8,)),
+            pltpu.SemaphoreType.DMA((3, 2)),
+            pltpu.SemaphoreType.DMA((GROUP, 2)),
         ],
-        compiler_params=PARAMS,
+        compiler_params=params(28),
+        cost_estimate=pl.CostEstimate(flops=4000000000, bytes_accessed=50000000, transcendentals=0),
         name="gradient_kernel",
     )(
-        all_shifts, rows_in, probe_r, probe_i, above_r, above_i, object_r, object_i, below_r, below_i,
+        all_shifts, rows_in, probe_r, probe_i, *near_above, *above, object_r, object_i, below_r, below_i,
         right_high, right_low,
     )
     terms = lax.all_to_all(terms, ("zh",) + group, 0, 0, tiled=True)
@@ -478,7 +604,8 @@
         out_shape=(shape(ROWS, LANES), shape(ROWS, LANES), shape(own_width, ROWS), shape(own_width, ROWS)),
         in_specs=[VMEM],
         out_specs=(VMEM, VMEM, VMEM, VMEM),
-        compiler_params=PARAMS,
+        compiler_params=params(8),
+        cost_estimate=pl.CostEstimate(flops=10000000, bytes_accessed=6000000, transcendentals=0),
         name="total_kernel",
     )(terms)
     return probe_r, probe_i, object_r.T, object_i.T

time: 247 us -> 219 us (0.89)
  waiting for transfers between devices: 69.5 us -> 50.5 us
  Pallas kernels: 42.4 us -> 33 us
  local copies, waits for them, and re-layouts: 5.49 us -> 1.72 us
  blocking collectives: 100 us -> 103 us
    ppermute x4 -> x8, waiting for transfers between devices: 39.7 us -> 11.8 us  [the longest x2 11.8 us: per_device(): lax.ppermute(value, 'row', row_pairs(-1, False) + row_pairs(-1, True))]
    all_to_all x1, waiting for transfers between devices: 22.3 us -> 35.5 us  [per_device(): columns = lax.all_to_all(exit_spread, 'row', 0, 0, tiled=True)]
    ppermute x4 -> x8, starting transfers between devices: 9.7 us -> 18.2 us  [the longest x2 6.41 us: per_device(): lax.ppermute(value, 'row', row_pairs(-1, False) + row_pairs(-1, True))]
    all_to_all x1 -> x0, waiting for transfers between devices: 6.22 us -> none  [per_device(): measured = lax.all_to_all(measured, 'row', 0, 0, tiled=True)]
    all_to_all x1 -> x0, starting transfers between devices: 6.01 us -> none  [per_device(): measured = lax.all_to_all(measured, 'row', 0, 0, tiled=True)]
    pallas_call x1, Pallas kernels: 16.9 us -> 10.9 us  [per_device(): pl.pallas_call(gradient_kernel, out_shape=shape(LEAD, 4 * PART + 8, LANES...]
    all_to_all x1, blocking collectives: 58.9 us -> 63.2 us  [per_device(): rows_in = lax.all_to_all(returned, group + ('row',), 0, 0, tiled=True)]
    unnamed x9 -> x22, local copies, waits for them, and re-layouts: 3.58 us -> 0.06 us
  transfers between devices with their start and end apart: 9 -> 12, of which waited for: 9 -> 5; matrix products, arithmetic and copies ran while one was open for 1% -> 1% of each run, Pallas kernels for 0% -> 10%
where the time goes in v2:
time: 219 us
  blocking collectives  103 us (47%)
  waiting for transfers between devices  50.5 us (23%)
  Pallas kernels  33 us (15%)
  starting transfers between devices  27.9 us (13%)
    all_to_all x1, blocking collectives, per_device(): rows_in = lax.all_to_all(returned, group + ('row',), 0, 0, tiled=True)  63.2 us
    all_to_all x1, blocking collectives, per_device(): terms = lax.all_to_all(terms, ('zh',) + group, 0, 0, tiled=True)  40 us
    all_to_all x1, waiting for transfers between devices, per_device(): columns = lax.all_to_all(exit_spread, 'row', 0, 0, tiled=True)  35.5 us
    ppermute x2, waiting for transfers between devices, per_device(): lax.ppermute(value, 'row', row_pairs(-1, False) + row_pairs(-1, True))  11.8 us
    pallas_call x1, Pallas kernels, per_device(): pl.pallas_call(gradient_kernel, out_shape=shape(LEAD, 4 * PART + 8, LANES...  10.9 us
    pallas_call x1, Pallas kernels, per_device(): pl.pallas_call(detector_kernel, out_shape=shape(GROUP * LEAD, 4, PART, LA...  10.9 us
    pallas_call x1, Pallas kernels, per_device(): pl.pallas_call(exit_kernel, out_shape=shape(LEAD, 3, ROWS, LANES), in_spe...  10.4 us
    ppermute x2, starting transfers between devices, per_device(): lax.ppermute(value, 'row', row_pairs(-1, False) + row_pairs(-1, True))  6.41 us
  transfers between devices with their start and end apart: 12, of which 5 were waited for; matrix products, arithmetic and copies ran while one was open for 1% of the time, Pallas kernels for 10%

profile of v2, /device:TPU:1, one launch (start us, length us, event | category | flops | bytes accessed | tf_op | source)
XLA Modules:
  0.0 218.7 jit_solution(12782507081332166366)
XLA Ops:
  0.6 3.3 %collective-permute-start = (f32[128,2304]{1,0:T(8,128)}, f32[128,2304]{1,0:T(8,128)S(1)}, u32[]{:S(2)}, u32[]{:S(2)}) collective-permute-start(f32[128,2304]{1,0:T(8,128)} %refs_8_.1), channel_id=1, source_target_pairs={{0,15},{2,1},{4,3},{6,5},{8,7},{10,9},{12,11},{14,13},{1,0},{3,2},... | collective-permute-start | bytes 3538952 | tf_op jit(solution)/shard_map/ppermute | solution.py:513
  3.9 3.1 %collective-permute-start.1 = (f32[128,2304]{1,0:T(8,128)}, f32[128,2304]{1,0:T(8,128)S(1)}, u32[]{:S(2)}, u32[]{:S(2)}) collective-permute-start(f32[128,2304]{1,0:T(8,128)} %refs_9_.1), channel_id=1, source_target_pairs={{0,15},{2,1},{4,3},{6,5},{8,7},{10,9},{12,11},{14,13},{1,0},{3,2},... | collective-permute-start | bytes 3538952 | tf_op jit(solution)/shard_map/ppermute | solution.py:513
  7.0 1.3 collective-permute-start.5
  8.3 1.3 collective-permute-start.6
  10.9 0.1 pad_add_fusion
  11.0 1.8 collective-permute-start.4
  12.8 1.1 dynamic-slice_bitcast_fusion
  13.9 0.4 collective-permute-done.4
  14.3 1.6 collective-permute-start.3
  16.0 0.9 collective-permute-done.3
  16.9 0.6 collective-permute-start.2
  17.4 1.9 collective-permute-done.2
  19.3 0.6 concatenate.8.shifts
  20.0 11.8 %collective-permute-done.1.below_i.refs_11_ = f32[128,2304]{1,0:T(8,128)S(1)} collective-permute-done((f32[128,2304]{1,0:T(8,128)}, f32[128,2304]{1,0:T(8,128)S(1)}, u32[]{:S(2)}, u32[]{:S(2)}) %collective-permute-start.1) | collective-permute-done | bytes 1179680 | tf_op jit(solution)/shard_map/ppermute | solution.py:513
  31.8 4.8 %collective-permute-start.7 = (f32[2,32,2048]{2,1,0:T(8,128)S(1)}, f32[2,32,2048]{2,1,0:T(8,128)S(1)}, u32[]{:S(2)}, u32[]{:S(2)}) collective-permute-start(f32[2,32,2048]{2,1,0:T(8,128)S(1)} %pad_maximum_fusion), channel_id=1, source_target_pairs={{1,2},{3,4},{5,6},{7,8},{9,10},{11,12},{13,14},{15,0},{17,18},{19,... | collective-permute-start | bytes 1572872 | tf_op jit(solution)/shard_map/ppermute | solution.py:528
  36.6 10.4 %exit_kernel.1 = f32[16,3,128,128]{3,2,1,0:T(8,128)} custom-call(s32[11]{0:T(128)} %concatenate.8.shifts, f32[128,2048]{1,0:T(8,128)} %refs_0_.1, f32[128,2048]{1,0:T(8,128)} %refs_1_.1, f32[128,2304]{1,0:T(8,128)} %refs_8_.1, f32[128,2304]{1,0:T(8,128)} %refs_9_.1, f32[128,2304]{1,0:T(8,128)} %copy-done.6, f32[128,2304]{1,0:T(8,128)} %copy-done.8, ...), custom_call_target="tpu_custom_call" | custom-call | flops 2000000000 | bytes 20000000 | tf_op jit(solution)/shard_map/exit_kernel/pallas_call | solution.py:529
  47.0 5.7 %all-to-all-start = ((f32[16,3,128,128]{3,2,1,0:T(8,128)}), f32[16,3,128,128]{3,2,1,0:T(8,128)}, u32[]{:S(2)}, u32[]{:S(2)}) async-start(f32[16,3,128,128]{3,2,1,0:T(8,128)} %exit_kernel.1), calls=%async_computation | async-start | bytes 6291456 | tf_op jit(solution)/shard_map/all_to_all | solution.py:554
  52.7 1.5 collective-permute-start.10
  54.2 1.5 collective-permute-start.9
  55.7 1.5 collective-permute-start.8
  57.1 35.5 %all-to-all-done.columns_in = f32[16,3,128,128]{3,2,1,0:T(8,128)} async-done(((f32[16,3,128,128]{3,2,1,0:T(8,128)}), f32[16,3,128,128]{3,2,1,0:T(8,128)}, u32[]{:S(2)}, u32[]{:S(2)}) %all-to-all-start) | async-done | bytes 3145760 | tf_op jit(solution)/shard_map/all_to_all | solution.py:554
  92.6 10.9 %detector_kernel.1 = f32[64,4,32,128]{3,2,1,0:T(8,128)} custom-call(s32[11]{0:T(128)} %concatenate.8.shifts, f32[16,3,128,128]{3,2,1,0:T(8,128)} %all-to-all-done.columns_in, bf16[16,256,256]{2,1,0:T(8,128)(2,1)} %constant.59.clone.high_in, bf16[16,256,256]{2,1,0:T(8,128)(2,1)} %constant.60.clone.low_in), custom_call_target="tpu_custom_call" | custom-call | flops 4000000000 | bytes 36000000 | tf_op jit(solution)/shard_map/detector_kernel/pallas_call | solution.py:556
  103.5 0.0 copy-start
  103.5 0.0 copy-start.1
  103.5 0.0 copy-start.2
  103.5 0.0 copy-start.3
  103.5 0.0 copy-start.4
  103.5 0.0 copy-start.10
  103.6 63.2 %all_to_all.15.rows_in = f32[64,4,32,128]{3,2,1,0:T(8,128)S(1)} all-to-all(f32[64,4,32,128]{3,2,1,0:T(8,128)} %detector_kernel.1), channel_id=1, replica_groups=mesh['zh'=4,'zl'=2,'yl'=2,'row'=16] {'zl','yl','row'}, dimensions={0} | all-to-all | bytes 8388608 | tf_op jit(solution)/shard_map/all_to_all | solution.py:578
  166.9 10.9 %gradient_kernel.1 = f32[16,136,128]{2,1,0:T(8,128)S(1)} custom-call(s32[11]{0:T(128)S(1)} %copy-done.10, f32[64,4,32,128]{3,2,1,0:T(8,128)S(1)} %all_to_all.15.rows_in, f32[128,2048]{1,0:T(8,128)S(1)} %copy-done.2, f32[128,2048]{1,0:T(8,128)S(1)} %copy-done.3, f32[128,2048]{1,0:T(8,128)} %collective-permute-done.5.refs_2_, ...), custom_call_target="tpu_custom_call" | custom-call | flops 4000000000 | bytes 50000000 | tf_op jit(solution)/shard_map/gradient_kernel/pallas_call | solution.py:579
  177.8 40.0 %all_to_all.16.terms = f32[16,136,128]{2,1,0:T(8,128)S(1)} all-to-all(f32[16,136,128]{2,1,0:T(8,128)S(1)} %gradient_kernel.1), channel_id=1, replica_groups=mesh['zh'=4,'zl'=2,'yl'=2,'row'=16] {'zh','zl','yl'}, dimensions={0} | all-to-all | bytes 2228224 | tf_op jit(solution)/shard_map/all_to_all | solution.py:600
  217.8 0.9 total_kernel.1
  (24 shorter events, 0.1 us)
Async XLA Ops:
  0.6 19.3 %collective-permute-start = (f32[128,2304]{1,0:T(8,128)}, f32[128,2304]{1,0:T(8,128)S(1)}, u32[]{:S(2)}, u32[]{:S(2)}) collective-permute-start(f32[128,2304]{1,0:T(8,128)} %refs_8_.1), channel_id=1, source_target_pairs={{0,15},{2,1},{4,3},{6,5},{8,7},{10,9},{12,11},{14,13},{1,0},{3,2},... | collective-permute-start | bytes 3538952 | tf_op jit(solution)/shard_map/ppermute | solution.py:513
  3.9 27.8 %collective-permute-start.1 = (f32[128,2304]{1,0:T(8,128)}, f32[128,2304]{1,0:T(8,128)S(1)}, u32[]{:S(2)}, u32[]{:S(2)}) collective-permute-start(f32[128,2304]{1,0:T(8,128)} %refs_9_.1), channel_id=1, source_target_pairs={{0,15},{2,1},{4,3},{6,5},{8,7},{10,9},{12,11},{14,13},{1,0},{3,2},... | collective-permute-start | bytes 3538952 | tf_op jit(solution)/shard_map/ppermute | solution.py:513
  7.0 12.9 %collective-permute-start.5 = (f32[128,2048]{1,0:T(8,128)}, f32[128,2048]{1,0:T(8,128)}, u32[]{:S(2)}, u32[]{:S(2)}) collective-permute-start(f32[128,2048]{1,0:T(8,128)} %refs_0_.1), channel_id=1, source_target_pairs={{0,1},{2,3},{4,5},{6,7},{8,9},{10,11},{12,13},{14,15},{16,17},{18,... | collective-permute-start | bytes 3145736 | tf_op jit(solution)/shard_map/ppermute | solution.py:524
  8.3 11.6 %collective-permute-start.6 = (f32[128,2048]{1,0:T(8,128)}, f32[128,2048]{1,0:T(8,128)}, u32[]{:S(2)}, u32[]{:S(2)}) collective-permute-start(f32[128,2048]{1,0:T(8,128)} %refs_1_.1), channel_id=1, source_target_pairs={{0,1},{2,3},{4,5},{6,7},{8,9},{10,11},{12,13},{14,15},{16,17},{18,... | collective-permute-start | bytes 3145736 | tf_op jit(solution)/shard_map/ppermute | solution.py:524
  11.0 3.3 %collective-permute-start.4 = (s32[2]{0:T(128)S(1)}, s32[2]{0:T(128)S(1)}, u32[]{:S(2)}, u32[]{:S(2)}) collective-permute-start(s32[2]{0:T(128)S(1)} %pad_add_fusion), channel_id=1, source_target_pairs={{0,48},{16,32},{32,16},{48,0},{1,49},{17,33},{33,17},{49,1},{2,50}... | collective-permute-start | bytes 32 | tf_op jit(solution)/shard_map/ppermute | solution.py:520
  14.3 2.6 %collective-permute-start.3 = (s32[2]{0:T(128)S(1)}, s32[2]{0:T(128)S(1)}, u32[]{:S(2)}, u32[]{:S(2)}) collective-permute-start(s32[2]{0:T(128)S(1)} %pad_add_fusion), channel_id=1, source_target_pairs={{0,32},{16,48},{32,0},{48,16},{1,33},{17,49},{33,1},{49,17},{2,34}... | collective-permute-start | bytes 32 | tf_op jit(solution)/shard_map/ppermute | solution.py:520
  16.9 2.4 %collective-permute-start.2 = (s32[2]{0:T(128)S(1)}, s32[2]{0:T(128)S(1)}, u32[]{:S(2)}, u32[]{:S(2)}) collective-permute-start(s32[2]{0:T(128)S(1)} %pad_add_fusion), channel_id=1, source_target_pairs={{0,16},{16,0},{32,48},{48,32},{1,17},{17,1},{33,49},{49,33},{2,18}... | collective-permute-start | bytes 32 | tf_op jit(solution)/shard_map/ppermute | solution.py:520
  19.9 16.6 %copy-start.6 = (f32[128,2304]{1,0:T(8,128)}, f32[128,2304]{1,0:T(8,128)S(1)}, u32[]{:S(2)}) copy-start(f32[128,2304]{1,0:T(8,128)S(1)} %collective-permute-done.below_r.refs_10_) | copy-start | bytes 3538948
  31.8 4.8 %copy-start.8 = (f32[128,2304]{1,0:T(8,128)}, f32[128,2304]{1,0:T(8,128)S(1)}, u32[]{:S(2)}) copy-start(f32[128,2304]{1,0:T(8,128)S(1)} %collective-permute-done.1.below_i.refs_11_) | copy-start | bytes 3538948
  31.8 15.2 %collective-permute-start.7 = (f32[2,32,2048]{2,1,0:T(8,128)S(1)}, f32[2,32,2048]{2,1,0:T(8,128)S(1)}, u32[]{:S(2)}, u32[]{:S(2)}) collective-permute-start(f32[2,32,2048]{2,1,0:T(8,128)S(1)} %pad_maximum_fusion), channel_id=1, source_target_pairs={{1,2},{3,4},{5,6},{7,8},{9,10},{11,12},{13,14},{15,0},{17,18},{19,... | collective-permute-start | bytes 1572872 | tf_op jit(solution)/shard_map/ppermute | solution.py:528
  47.0 45.6 %all-to-all-start = ((f32[16,3,128,128]{3,2,1,0:T(8,128)}), f32[16,3,128,128]{3,2,1,0:T(8,128)}, u32[]{:S(2)}, u32[]{:S(2)}) async-start(f32[16,3,128,128]{3,2,1,0:T(8,128)} %exit_kernel.1), calls=%async_computation | async-start | bytes 6291456 | tf_op jit(solution)/shard_map/all_to_all | solution.py:554
  52.7 50.8 %collective-permute-start.10 = (f32[2,32,2048]{2,1,0:T(8,128)S(1)}, f32[2,32,2048]{2,1,0:T(8,128)}, u32[]{:S(2)}, u32[]{:S(2)}) collective-permute-start(f32[2,32,2048]{2,1,0:T(8,128)S(1)} %collective-permute-done.7.refs_4_), channel_id=1, source_target_pairs={{0,96},{2,98},{4,100},{6,102},{8,104},{10,106},{12,108},{14,110},{... | collective-permute-start | bytes 1572872 | tf_op jit(solution)/shard_map/ppermute | solution.py:499
  54.2 49.4 %collective-permute-start.9 = (f32[2,32,2048]{2,1,0:T(8,128)S(1)}, f32[2,32,2048]{2,1,0:T(8,128)}, u32[]{:S(2)}, u32[]{:S(2)}) collective-permute-start(f32[2,32,2048]{2,1,0:T(8,128)S(1)} %collective-permute-done.7.refs_4_), channel_id=1, source_target_pairs={{0,64},{2,66},{4,68},{6,70},{8,72},{10,74},{12,76},{14,78},{32,96}... | collective-permute-start | bytes 1572872 | tf_op jit(solution)/shard_map/ppermute | solution.py:499
  55.7 47.9 %collective-permute-start.8 = (f32[2,32,2048]{2,1,0:T(8,128)S(1)}, f32[2,32,2048]{2,1,0:T(8,128)}, u32[]{:S(2)}, u32[]{:S(2)}) collective-permute-start(f32[2,32,2048]{2,1,0:T(8,128)S(1)} %collective-permute-done.7.refs_4_), channel_id=1, source_target_pairs={{0,32},{2,34},{4,36},{6,38},{8,40},{10,42},{12,44},{14,46},{32,0},... | collective-permute-start | bytes 1572872 | tf_op jit(solution)/shard_map/ppermute | solution.py:499
  92.6 74.2 %copy-start.5 = (f32[128,2304]{1,0:T(8,128)S(1)}, f32[128,2304]{1,0:T(8,128)}, u32[]{:S(2)}) copy-start(f32[128,2304]{1,0:T(8,128)} %refs_9_.1) | copy-start | bytes 3538948
  92.6 74.2 %copy-start.7 = (f32[128,2304]{1,0:T(8,128)S(1)}, f32[128,2304]{1,0:T(8,128)}, u32[]{:S(2)}) copy-start(f32[128,2304]{1,0:T(8,128)} %copy-done.6) | copy-start | bytes 3538948
  92.6 74.2 %copy-start.9 = (f32[128,2304]{1,0:T(8,128)S(1)}, f32[128,2304]{1,0:T(8,128)}, u32[]{:S(2)}) copy-start(f32[128,2304]{1,0:T(8,128)} %copy-done.8) | copy-start | bytes 3538948
  103.5 63.4 %copy-start = (bf16[16,256,256]{2,1,0:T(8,128)(2,1)S(1)}, bf16[16,256,256]{2,1,0:T(8,128)(2,1)}, u32[]{:S(2)}) copy-start(bf16[16,256,256]{2,1,0:T(8,128)(2,1)} %constant.58.clone.low_in.refs_13_) | copy-start | bytes 6291460
  103.5 63.4 %copy-start.1 = (bf16[16,256,256]{2,1,0:T(8,128)(2,1)S(1)}, bf16[16,256,256]{2,1,0:T(8,128)(2,1)}, u32[]{:S(2)}) copy-start(bf16[16,256,256]{2,1,0:T(8,128)(2,1)} %constant.57.clone.high_in.refs_12_) | copy-start | bytes 6291460
  103.5 63.3 %copy-start.2 = (f32[128,2048]{1,0:T(8,128)S(1)}, f32[128,2048]{1,0:T(8,128)}, u32[]{:S(2)}) copy-start(f32[128,2048]{1,0:T(8,128)} %refs_0_.1) | copy-start | bytes 3145732
  103.5 63.3 %copy-start.3 = (f32[128,2048]{1,0:T(8,128)S(1)}, f32[128,2048]{1,0:T(8,128)}, u32[]{:S(2)}) copy-start(f32[128,2048]{1,0:T(8,128)} %refs_1_.1) | copy-start | bytes 3145732
  103.5 63.3 %copy-start.4 = (f32[128,2304]{1,0:T(8,128)S(1)}, f32[128,2304]{1,0:T(8,128)}, u32[]{:S(2)}) copy-start(f32[128,2304]{1,0:T(8,128)} %refs_8_.1) | copy-start | bytes 3538948
  103.5 63.3 %copy-start.10 = (s32[11]{0:T(128)S(1)}, s32[11]{0:T(128)}, u32[]{:S(2)}) copy-start(s32[11]{0:T(128)} %concatenate.8.shifts) | copy-start | bytes 136

commit v3 on v2

--- a/solution.py
+++ b/solution.py
@@ -16,6 +16,7 @@
 LEAD = 16
 ROWS = 128
 GROUP = 4
+UNROLL = 4
 PART = ROWS // GROUP
 MEBI = 1024 * 1024
 
@@ -184,13 +185,27 @@
         run_all(copies[1], method)
 
 
+def part_kernel(place, real, imag, out, sems):
+    rows = pl.ds(pl.multiple_of(place[0] * PART, PART), PART)
+    copies = block_copies(out, (real.at[rows], imag.at[rows]), 0, sems)
+    run_all(copies, "start")
+    run_all(copies, "wait")
+
+
 def exit_kernel(
     shifts, probe_r, probe_i, object_r, object_i, below_r, below_i, measured, high_in, low_in, out,
     window, probe, table_high, table_low, store, spread, sems, table_sems, measured_sems, out_sems,
 ):
-    fields = block_copies(window, (object_r, object_i), 0, sems.at[0])
-    fields += block_copies(window, (below_r, below_i), ROWS, sems.at[1])
-    fields += block_copies(probe, (probe_r, probe_i), 0, sems.at[2])
+    held = block_copies(window, (object_r, object_i), 0, sems.at[0])
+    pieces = []
+    for part in range(GROUP):
+        rows = pl.ds(part * PART, PART)
+        piece = block_copies(
+            window, (below_r.at[rows], below_i.at[rows]), ROWS + part * PART, sems.at[1 + part]
+        )
+        pieces.append(
+            piece + block_copies(probe, (probe_r.at[rows], probe_i.at[rows]), part * PART, sems.at[5 + part])
+        )
     tables = [
         pltpu.make_async_copy(source, target, table_sems.at[n])
         for n, (source, target) in enumerate(((high_in, table_high), (low_in, table_low)))
@@ -199,10 +214,12 @@
         pltpu.make_async_copy(measured.at[0, :, pl.ds(a * LANES, LANES)], spread.at[a, 2], measured_sems.at[a])
         for a in range(LEAD)
     ]
-    run_all(fields, "start")
+    run_all(held, "start")
+    for piece in pieces:
+        run_all(piece, "start")
     run_all(tables, "start")
     run_all(passing, "start")
-    run_all(fields, "wait")
+    run_all(held, "wait")
     row_shift = shifts[0]
     tile, shift = lane_parts(shifts[1])
 
@@ -223,7 +240,9 @@
             store[c, rows, pl.ds(LANES, LANES)] = imag
         return carry
 
-    lax.fori_loop(0, ROWS // 8, gather, 0)
+    for part in range(GROUP):
+        run_all(pieces[part], "wait")
+        lax.fori_loop(part * PART // 8, (part + 1) * PART // 8, gather, 0, unroll=UNROLL)
     run_all(tables, "wait")
     mix_right(store, table_high, table_low)
 
@@ -238,7 +257,7 @@
     run_all(passing, "wait")
     sends = []
     for part in range(GROUP):
-        lax.fori_loop(part * PART // 8, (part + 1) * PART // 8, scatter, 0)
+        lax.fori_loop(part * PART // 8, (part + 1) * PART // 8, scatter, 0, unroll=UNROLL)
         rows = pl.ds(part * PART, PART)
         send = pltpu.make_async_copy(spread.at[:, :, rows], out.at[:, :, rows], out_sems.at[part])
         send.start()
@@ -278,7 +297,7 @@
 
     for part in range(GROUP):
         arriving[part].wait()
-        lax.fori_loop(part * PART // 8, (part + 1) * PART // 8, first, 0)
+        lax.fori_loop(part * PART // 8, (part + 1) * PART // 8, first, 0, unroll=UNROLL)
     run_all(tables, "wait")
     mix_left(store, table_high, table_low)
 
@@ -292,7 +311,7 @@
         save(dft16(residual, -1), k)
         return carry
 
-    lax.fori_loop(0, ROWS // 8, modulus, 0)
+    lax.fori_loop(0, ROWS // 8, modulus, 0, unroll=UNROLL)
     mix_left(store, table_high, table_low)
 
     def last(k, carry):
@@ -315,7 +334,7 @@
         sends.append(copy)
 
     for part in range(GROUP):
-        lax.fori_loop(part * PART // 8, (part + 1) * PART // 8, last, 0)
+        lax.fori_loop(part * PART // 8, (part + 1) * PART // 8, last, 0, unroll=UNROLL)
         send(straight, 0, part)
         send(straight, 1, part)
     base = lax.div(shifts[0] + 7, 8) * 8
@@ -337,7 +356,7 @@
                     shifted[half, a, rows] = jnp.where(keep, rolled[k], rolled[k + 1])
             return carry
 
-        lax.fori_loop(0, LEAD, place, 0)
+        lax.fori_loop(0, LEAD, place, 0, unroll=UNROLL)
         send(shifted, 2, part)
         send(shifted, 3, part)
     run_all(sends, "wait")
@@ -373,7 +392,7 @@
             store[c, at, pl.ds(LANES, LANES)] = imag
         return carry
 
-    lax.fori_loop(0, 2 * GROUP * chunks, first, 0)
+    lax.fori_loop(0, 2 * GROUP * chunks, first, 0, unroll=UNROLL)
     mix_right(store, table_high, table_low)
     run_all(held, "wait")
     run_halo(moved, core == 1, "wait")
@@ -400,7 +419,7 @@
             probe_acc[1, rows, lanes] += patch_r[a] * imag - patch_i[a] * real
         return carry
 
-    lax.fori_loop(0, GROUP * chunks, probe_term, 0)
+    lax.fori_loop(0, GROUP * chunks, probe_term, 0, unroll=UNROLL)
     lane = lax.broadcasted_iota(jnp.int32, (8, LANES), 1)
 
     def object_term(m, carry):
@@ -430,7 +449,7 @@
                 object_acc[half, rows, lanes] += jnp.where(keep, here, left)
         return carry
 
-    lax.fori_loop(0, GROUP * chunks, object_term, 0)
+    lax.fori_loop(0, GROUP * chunks, object_term, 0, unroll=UNROLL)
     own = object_acc.shape[2] // LANES * LANES
     width = LANES + LANES // 8
     for b in range(LEAD):
@@ -487,16 +506,27 @@
     return lax.axis_index(("zh", "zl")) % GROUP
 
 
-def own_part(real, imag):
-    at = fetched_part() * PART
-    return jnp.stack([lax.dynamic_slice_in_dim(value, at, PART, 0) for value in (real, imag)])
+def own_part(place, real, imag):
+    return pl.pallas_call(
+        part_kernel,
+        out_shape=shape(2, PART, real.shape[1]),
+        in_specs=[SMEM, ANY, ANY],
+        out_specs=VMEM,
+        scratch_shapes=[pltpu.SemaphoreType.DMA((2,))],
+        compiler_params=params(4),
+        name="part_kernel",
+    )(place, real, imag)
 
 
 def passed_on(part, takers):
     parts = [part]
     for by in range(1, GROUP):
-        pairs = [(z * LEAD + r, (z ^ by) * LEAD + r) for z in range(8) for r in takers]
-        parts.append(lax.ppermute(part, ("zh", "zl", "row"), pairs))
+        pairs = []
+        for z in range(8):
+            for yl in range(2):
+                if z % GROUP >= 2 * ((z ^ by) % 2) + yl:
+                    pairs += [((2 * z + yl) * LEAD + r, (2 * (z ^ by) + yl) * LEAD + r) for r in takers]
+        parts.append(lax.ppermute(part, ("zh", "zl", "yl", "row"), pairs))
     return tuple(parts)
 
 
@@ -520,7 +550,7 @@
         lax.ppermute(own_shift, group, [(i, i ^ by) for i in range(GROUP)]) for by in range(1, GROUP)
     ]
     all_shifts = jnp.concatenate([own_shift] + others + [own[None], core[None], part[None]])
-    above_part = own_part(probe_r, probe_i)
+    above_part = own_part(part[None], probe_r, probe_i)
     near_above = tuple(lax.ppermute(value, "row", row_pairs(1, True)) for value in (probe_r, probe_i))
     below_r, below_i, above_part, all_shifts, near_above = together(
         below_r, below_i, above_part, all_shifts, near_above
@@ -538,7 +568,7 @@
             pltpu.VMEM(right_low.shape, BF16),
             pltpu.VMEM((LEAD, ROWS, 2 * LANES), F32),
             pltpu.VMEM((LEAD, 3, ROWS, LANES), F32),
-            pltpu.SemaphoreType.DMA((3, 2)),
+            pltpu.SemaphoreType.DMA((1 + 2 * GROUP, 2)),
             pltpu.SemaphoreType.DMA((2,)),
             pltpu.SemaphoreType.DMA((LEAD,)),
             pltpu.SemaphoreType.DMA((GROUP,)),

time: 219 us -> 215 us (0.982)
  Pallas kernels: 33 us -> 28.4 us
    unnamed x22 -> x26, local copies, waits for them, and re-layouts: 0.06 us -> 2.51 us
    pallas_call x1, Pallas kernels: 10.9 us -> 8.63 us  [per_device(): pl.pallas_call(gradient_kernel, out_shape=shape(LEAD, 4 * PART + 8, LANES...]
  transfers between devices with their start and end apart: 12 -> 12, of which waited for: 5 -> 4; matrix products, arithmetic and copies ran while one was open for 1% -> 0% of each run, Pallas kernels for 10% -> 9%
where the time goes in v3:
time: 215 us
  blocking collectives  103 us (48%)
  waiting for transfers between devices  49.6 us (23%)
  starting transfers between devices  28.8 us (13%)
  Pallas kernels  28.4 us (13%)
  local copies, waits for them, and re-layouts  3.11 us (1%)
  between operations  2.17 us (1%)
    all_to_all x1, blocking collectives, per_device(): rows_in = lax.all_to_all(returned, group + ('row',), 0, 0, tiled=True)  62.7 us
    all_to_all x1, blocking collectives, per_device(): terms = lax.all_to_all(terms, ('zh',) + group, 0, 0, tiled=True)  40.1 us
    all_to_all x1, waiting for transfers between devices, per_device(): columns = lax.all_to_all(exit_spread, 'row', 0, 0, tiled=True)  35.5 us
    ppermute x2, waiting for transfers between devices, per_device(): lax.ppermute(value, 'row', row_pairs(-1, False) + row_pairs(-1, True))  10.9 us
    pallas_call x1, Pallas kernels, per_device(): pl.pallas_call(detector_kernel, out_shape=shape(GROUP * LEAD, 4, PART, LA...  10.5 us
    pallas_call x1, Pallas kernels, per_device(): pl.pallas_call(gradient_kernel, out_shape=shape(LEAD, 4 * PART + 8, LANES...  8.63 us
    pallas_call x1, Pallas kernels, per_device(): pl.pallas_call(exit_kernel, out_shape=shape(LEAD, 3, ROWS, LANES), in_spe...  8.37 us
    all_to_all x1, starting transfers between devices, per_device(): columns = lax.all_to_all(exit_spread, 'row', 0, 0, tiled=True)  7.07 us
  transfers between devices with their start and end apart: 12, of which 4 were waited for; matrix products, arithmetic and copies ran while one was open for 0% of the time, Pallas kernels for 9%

profile of v3, /device:TPU:1, one launch (start us, length us, event | category | flops | bytes accessed | tf_op | source)
XLA Modules:
  0.0 214.9 jit_solution(14887171232441350769)
XLA Ops:
  0.6 3.3 %collective-permute-start = (f32[128,2304]{1,0:T(8,128)}, f32[128,2304]{1,0:T(8,128)S(1)}, u32[]{:S(2)}, u32[]{:S(2)}) collective-permute-start(f32[128,2304]{1,0:T(8,128)} %refs_8_.1), channel_id=1, source_target_pairs={{0,15},{2,1},{4,3},{6,5},{8,7},{10,9},{12,11},{14,13},{1,0},{3,2},... | collective-permute-start | bytes 3538952 | tf_op jit(solution)/shard_map/ppermute | solution.py:543
  3.9 3.1 %collective-permute-start.1 = (f32[128,2304]{1,0:T(8,128)}, f32[128,2304]{1,0:T(8,128)S(1)}, u32[]{:S(2)}, u32[]{:S(2)}) collective-permute-start(f32[128,2304]{1,0:T(8,128)} %refs_9_.1), channel_id=1, source_target_pairs={{0,15},{2,1},{4,3},{6,5},{8,7},{10,9},{12,11},{14,13},{1,0},{3,2},... | collective-permute-start | bytes 3538952 | tf_op jit(solution)/shard_map/ppermute | solution.py:543
  7.0 1.3 collective-permute-start.5
  8.3 1.3 collective-permute-start.6
  10.9 0.1 pad_add_fusion
  11.0 1.8 collective-permute-start.4
  12.8 1.2 copy-done
  14.0 1.2 copy-done.2
  15.2 0.1 part_kernel.1
  15.3 0.6 collective-permute-start.3
  16.0 1.8 collective-permute-done.3
  17.8 1.1 collective-permute-start.2
  18.9 1.4 collective-permute-done.2
  20.2 0.6 concatenate.8.shifts
  20.9 10.9 %collective-permute-done.1.below_i.refs_11_ = f32[128,2304]{1,0:T(8,128)S(1)} collective-permute-done((f32[128,2304]{1,0:T(8,128)}, f32[128,2304]{1,0:T(8,128)S(1)}, u32[]{:S(2)}, u32[]{:S(2)}) %collective-permute-start.1) | collective-permute-done | bytes 1179680 | tf_op jit(solution)/shard_map/ppermute | solution.py:543
  31.8 4.8 %collective-permute-start.7 = (f32[2,32,2048]{2,1,0:T(8,128)S(1)}, f32[2,32,2048]{2,1,0:T(8,128)S(1)}, u32[]{:S(2)}, u32[]{:S(2)}) collective-permute-start(f32[2,32,2048]{2,1,0:T(8,128)S(1)} %part_kernel.1), channel_id=1, source_target_pairs={{1,2},{3,4},{5,6},{7,8},{9,10},{11,12},{13,14},{15,0},{17,18},{19,... | collective-permute-start | bytes 1572872 | tf_op jit(solution)/shard_map/ppermute | solution.py:558
  36.6 8.4 %exit_kernel.1 = f32[16,3,128,128]{3,2,1,0:T(8,128)} custom-call(s32[11]{0:T(128)} %concatenate.8.shifts, f32[128,2048]{1,0:T(8,128)} %refs_0_.1, f32[128,2048]{1,0:T(8,128)} %refs_1_.1, f32[128,2304]{1,0:T(8,128)} %refs_8_.1, f32[128,2304]{1,0:T(8,128)} %refs_9_.1, f32[128,2304]{1,0:T(8,128)} %copy-done.8, f32[128,2304]{1,0:T(8,128)} %copy-done.10, ...), custom_call_target="tpu_custom_call" | custom-call | flops 2000000000 | bytes 20000000 | tf_op jit(solution)/shard_map/exit_kernel/pallas_call | solution.py:559
  45.0 7.1 %all-to-all-start = ((f32[16,3,128,128]{3,2,1,0:T(8,128)}), f32[16,3,128,128]{3,2,1,0:T(8,128)}, u32[]{:S(2)}, u32[]{:S(2)}) async-start(f32[16,3,128,128]{3,2,1,0:T(8,128)} %exit_kernel.1), calls=%async_computation | async-start | bytes 6291456 | tf_op jit(solution)/shard_map/all_to_all | solution.py:584
  52.1 1.5 collective-permute-start.10
  53.5 1.5 collective-permute-start.9
  55.0 1.5 collective-permute-start.8
  56.5 35.5 %all-to-all-done.columns_in = f32[16,3,128,128]{3,2,1,0:T(8,128)} async-done(((f32[16,3,128,128]{3,2,1,0:T(8,128)}), f32[16,3,128,128]{3,2,1,0:T(8,128)}, u32[]{:S(2)}, u32[]{:S(2)}) %all-to-all-start) | async-done | bytes 3145760 | tf_op jit(solution)/shard_map/all_to_all | solution.py:584
  92.0 10.5 %detector_kernel.1 = f32[64,4,32,128]{3,2,1,0:T(8,128)} custom-call(s32[11]{0:T(128)} %concatenate.8.shifts, f32[16,3,128,128]{3,2,1,0:T(8,128)} %all-to-all-done.columns_in, bf16[16,256,256]{2,1,0:T(8,128)(2,1)} %constant.52.clone.high_in, bf16[16,256,256]{2,1,0:T(8,128)(2,1)} %constant.53.clone.low_in), custom_call_target="tpu_custom_call" | custom-call | flops 4000000000 | bytes 36000000 | tf_op jit(solution)/shard_map/detector_kernel/pallas_call | solution.py:586
  102.5 0.0 copy-start.1
  102.5 0.0 copy-start.4
  102.5 0.0 copy-start.5
  102.5 0.0 copy-start.6
  102.5 0.0 copy-start.12
  102.6 62.7 %all_to_all.15.rows_in = f32[64,4,32,128]{3,2,1,0:T(8,128)S(1)} all-to-all(f32[64,4,32,128]{3,2,1,0:T(8,128)} %detector_kernel.1), channel_id=1, replica_groups=mesh['zh'=4,'zl'=2,'yl'=2,'row'=16] {'zl','yl','row'}, dimensions={0} | all-to-all | bytes 8388608 | tf_op jit(solution)/shard_map/all_to_all | solution.py:608
  165.4 8.6 %gradient_kernel.1 = f32[16,136,128]{2,1,0:T(8,128)S(1)} custom-call(s32[11]{0:T(128)S(1)} %copy-done.12, f32[64,4,32,128]{3,2,1,0:T(8,128)S(1)} %all_to_all.15.rows_in, f32[128,2048]{1,0:T(8,128)S(1)} %copy-done.1, f32[128,2048]{1,0:T(8,128)S(1)} %copy-done.3, f32[128,2048]{1,0:T(8,128)} %collective-permute-done.5.refs_2_, ...), custom_call_target="tpu_custom_call" | custom-call | flops 4000000000 | bytes 50000000 | tf_op jit(solution)/shard_map/gradient_kernel/pallas_call | solution.py:609
  174.0 40.1 %all_to_all.16.terms = f32[16,136,128]{2,1,0:T(8,128)S(1)} all-to-all(f32[16,136,128]{2,1,0:T(8,128)S(1)} %gradient_kernel.1), channel_id=1, replica_groups=mesh['zh'=4,'zl'=2,'yl'=2,'row'=16] {'zh','zl','yl'}, dimensions={0} | all-to-all | bytes 2228224 | tf_op jit(solution)/shard_map/all_to_all | solution.py:630
  214.1 0.9 total_kernel.1
  (27 shorter events, 0.1 us)
Async XLA Ops:
  0.6 20.2 %collective-permute-start = (f32[128,2304]{1,0:T(8,128)}, f32[128,2304]{1,0:T(8,128)S(1)}, u32[]{:S(2)}, u32[]{:S(2)}) collective-permute-start(f32[128,2304]{1,0:T(8,128)} %refs_8_.1), channel_id=1, source_target_pairs={{0,15},{2,1},{4,3},{6,5},{8,7},{10,9},{12,11},{14,13},{1,0},{3,2},... | collective-permute-start | bytes 3538952 | tf_op jit(solution)/shard_map/ppermute | solution.py:543
  3.9 27.8 %collective-permute-start.1 = (f32[128,2304]{1,0:T(8,128)}, f32[128,2304]{1,0:T(8,128)S(1)}, u32[]{:S(2)}, u32[]{:S(2)}) collective-permute-start(f32[128,2304]{1,0:T(8,128)} %refs_9_.1), channel_id=1, source_target_pairs={{0,15},{2,1},{4,3},{6,5},{8,7},{10,9},{12,11},{14,13},{1,0},{3,2},... | collective-permute-start | bytes 3538952 | tf_op jit(solution)/shard_map/ppermute | solution.py:543
  7.0 13.8 %collective-permute-start.5 = (f32[128,2048]{1,0:T(8,128)}, f32[128,2048]{1,0:T(8,128)}, u32[]{:S(2)}, u32[]{:S(2)}) collective-permute-start(f32[128,2048]{1,0:T(8,128)} %refs_0_.1), channel_id=1, source_target_pairs={{0,1},{2,3},{4,5},{6,7},{8,9},{10,11},{12,13},{14,15},{16,17},{18,... | collective-permute-start | bytes 3145736 | tf_op jit(solution)/shard_map/ppermute | solution.py:554
  8.3 12.5 %collective-permute-start.6 = (f32[128,2048]{1,0:T(8,128)}, f32[128,2048]{1,0:T(8,128)}, u32[]{:S(2)}, u32[]{:S(2)}) collective-permute-start(f32[128,2048]{1,0:T(8,128)} %refs_1_.1), channel_id=1, source_target_pairs={{0,1},{2,3},{4,5},{6,7},{8,9},{10,11},{12,13},{14,15},{16,17},{18,... | collective-permute-start | bytes 3145736 | tf_op jit(solution)/shard_map/ppermute | solution.py:554
  11.0 4.3 %collective-permute-start.4 = (s32[2]{0:T(128)S(1)}, s32[2]{0:T(128)S(1)}, u32[]{:S(2)}, u32[]{:S(2)}) collective-permute-start(s32[2]{0:T(128)S(1)} %pad_add_fusion), channel_id=1, source_target_pairs={{0,48},{16,32},{32,16},{48,0},{1,49},{17,33},{33,17},{49,1},{2,50}... | collective-permute-start | bytes 32 | tf_op jit(solution)/shard_map/ppermute | solution.py:550
  12.8 1.2 copy-start
  14.0 1.2 copy-start.2
  15.3 2.5 %collective-permute-start.3 = (s32[2]{0:T(128)S(1)}, s32[2]{0:T(128)S(1)}, u32[]{:S(2)}, u32[]{:S(2)}) collective-permute-start(s32[2]{0:T(128)S(1)} %pad_add_fusion), channel_id=1, source_target_pairs={{0,32},{16,48},{32,0},{48,16},{1,33},{17,49},{33,1},{49,17},{2,34}... | collective-permute-start | bytes 32 | tf_op jit(solution)/shard_map/ppermute | solution.py:550
  17.8 2.4 %collective-permute-start.2 = (s32[2]{0:T(128)S(1)}, s32[2]{0:T(128)S(1)}, u32[]{:S(2)}, u32[]{:S(2)}) collective-permute-start(s32[2]{0:T(128)S(1)} %pad_add_fusion), channel_id=1, source_target_pairs={{0,16},{16,0},{32,48},{48,32},{1,17},{17,1},{33,49},{49,33},{2,18}... | collective-permute-start | bytes 32 | tf_op jit(solution)/shard_map/ppermute | solution.py:550
  20.9 15.7 %copy-start.8 = (f32[128,2304]{1,0:T(8,128)}, f32[128,2304]{1,0:T(8,128)S(1)}, u32[]{:S(2)}) copy-start(f32[128,2304]{1,0:T(8,128)S(1)} %collective-permute-done.below_r.refs_10_) | copy-start | bytes 3538948
  31.8 4.8 %copy-start.10 = (f32[128,2304]{1,0:T(8,128)}, f32[128,2304]{1,0:T(8,128)S(1)}, u32[]{:S(2)}) copy-start(f32[128,2304]{1,0:T(8,128)S(1)} %collective-permute-done.1.below_i.refs_11_) | copy-start | bytes 3538948
  31.8 13.2 %collective-permute-start.7 = (f32[2,32,2048]{2,1,0:T(8,128)S(1)}, f32[2,32,2048]{2,1,0:T(8,128)S(1)}, u32[]{:S(2)}, u32[]{:S(2)}) collective-permute-start(f32[2,32,2048]{2,1,0:T(8,128)S(1)} %part_kernel.1), channel_id=1, source_target_pairs={{1,2},{3,4},{5,6},{7,8},{9,10},{11,12},{13,14},{15,0},{17,18},{19,... | collective-permute-start | bytes 1572872 | tf_op jit(solution)/shard_map/ppermute | solution.py:558
  45.0 47.0 %all-to-all-start = ((f32[16,3,128,128]{3,2,1,0:T(8,128)}), f32[16,3,128,128]{3,2,1,0:T(8,128)}, u32[]{:S(2)}, u32[]{:S(2)}) async-start(f32[16,3,128,128]{3,2,1,0:T(8,128)} %exit_kernel.1), calls=%async_computation | async-start | bytes 6291456 | tf_op jit(solution)/shard_map/all_to_all | solution.py:584
  52.1 50.5 %collective-permute-start.10 = (f32[2,32,2048]{2,1,0:T(8,128)S(1)}, f32[2,32,2048]{2,1,0:T(8,128)}, u32[]{:S(2)}, u32[]{:S(2)}) collective-permute-start(f32[2,32,2048]{2,1,0:T(8,128)S(1)} %collective-permute-done.7.refs_4_), channel_id=1, source_target_pairs={{32,64},{34,66},{36,68},{38,70},{40,72},{42,74},{44,76},{46,78},{4... | collective-permute-start | bytes 1572872 | tf_op jit(solution)/shard_map/ppermute | solution.py:529
  53.5 49.0 %collective-permute-start.9 = (f32[2,32,2048]{2,1,0:T(8,128)S(1)}, f32[2,32,2048]{2,1,0:T(8,128)}, u32[]{:S(2)}, u32[]{:S(2)}) collective-permute-start(f32[2,32,2048]{2,1,0:T(8,128)S(1)} %collective-permute-done.7.refs_4_), channel_id=1, source_target_pairs={{0,64},{2,66},{4,68},{6,70},{8,72},{10,74},{12,76},{14,78},{64,0},... | collective-permute-start | bytes 1572872 | tf_op jit(solution)/shard_map/ppermute | solution.py:529
  55.0 47.5 %collective-permute-start.8 = (f32[2,32,2048]{2,1,0:T(8,128)S(1)}, f32[2,32,2048]{2,1,0:T(8,128)}, u32[]{:S(2)}, u32[]{:S(2)}) collective-permute-start(f32[2,32,2048]{2,1,0:T(8,128)S(1)} %collective-permute-done.7.refs_4_), channel_id=1, source_target_pairs={{32,0},{34,2},{36,4},{38,6},{40,8},{42,10},{44,12},{46,14},{48,16}... | collective-permute-start | bytes 1572872 | tf_op jit(solution)/shard_map/ppermute | solution.py:529
  92.0 73.3 %copy-start.7 = (f32[128,2304]{1,0:T(8,128)S(1)}, f32[128,2304]{1,0:T(8,128)}, u32[]{:S(2)}) copy-start(f32[128,2304]{1,0:T(8,128)} %refs_9_.1) | copy-start | bytes 3538948
  92.0 73.3 %copy-start.9 = (f32[128,2304]{1,0:T(8,128)S(1)}, f32[128,2304]{1,0:T(8,128)}, u32[]{:S(2)}) copy-start(f32[128,2304]{1,0:T(8,128)} %copy-done.8) | copy-start | bytes 3538948
  92.0 73.3 %copy-start.11 = (f32[128,2304]{1,0:T(8,128)S(1)}, f32[128,2304]{1,0:T(8,128)}, u32[]{:S(2)}) copy-start(f32[128,2304]{1,0:T(8,128)} %copy-done.10) | copy-start | bytes 3538948
  102.5 62.8 %copy-start.1 = (f32[128,2048]{1,0:T(8,128)S(1)}, f32[128,2048]{1,0:T(8,128)}, u32[]{:S(2)}) copy-start(f32[128,2048]{1,0:T(8,128)} %refs_0_.1) | copy-start | bytes 3145732
  102.5 62.8 %copy-start.3 = (f32[128,2048]{1,0:T(8,128)S(1)}, f32[128,2048]{1,0:T(8,128)}, u32[]{:S(2)}) copy-start(f32[128,2048]{1,0:T(8,128)} %refs_1_.1) | copy-start | bytes 3145732
  102.5 62.8 %copy-start.4 = (bf16[16,256,256]{2,1,0:T(8,128)(2,1)S(1)}, bf16[16,256,256]{2,1,0:T(8,128)(2,1)}, u32[]{:S(2)}) copy-start(bf16[16,256,256]{2,1,0:T(8,128)(2,1)} %constant.51.clone.low_in.refs_13_) | copy-start | bytes 6291460
  102.5 62.8 %copy-start.5 = (bf16[16,256,256]{2,1,0:T(8,128)(2,1)S(1)}, bf16[16,256,256]{2,1,0:T(8,128)(2,1)}, u32[]{:S(2)}) copy-start(bf16[16,256,256]{2,1,0:T(8,128)(2,1)} %constant.50.clone.high_in.refs_12_) | copy-start | bytes 6291460
  102.5 62.8 %copy-start.6 = (f32[128,2304]{1,0:T(8,128)S(1)}, f32[128,2304]{1,0:T(8,128)}, u32[]{:S(2)}) copy-start(f32[128,2304]{1,0:T(8,128)} %refs_8_.1) | copy-start | bytes 3538948
  102.5 62.8 %copy-start.12 = (s32[11]{0:T(128)S(1)}, s32[11]{0:T(128)}, u32[]{:S(2)}) copy-start(s32[11]{0:T(128)} %concatenate.8.shifts) | copy-start | bytes 136

commit v4 on v3

--- a/solution.py
+++ b/solution.py
@@ -34,15 +34,15 @@
     chirp = np.exp(-2j * np.pi * ((frequency * frequency) % (4 * length)) / (4 * length))
     offsets = np.arange(-(LANES - 1), LANES, dtype=np.int64)
     place = np.arange(LANES)
-    right = np.empty((LEAD, 2 * LANES, 2 * LANES))
+    right, left = np.empty((LEAD, LANES, 2 * LANES)), np.empty((LEAD, LANES, 2 * LANES))
     for c in range(LEAD):
         tone = c + LEAD * np.arange(LANES, dtype=np.int64)
         phase = np.exp(2j * np.pi * ((offsets[:, None] * tone[None, :]) % length) / length)
         line = phase @ chirp[tone] / length
         middle = line[place[:, None] - place[None, :] + LANES - 1]
-        left = np.block([[middle.real, -middle.imag], [middle.imag, middle.real]])
-        right[c] = left.T
-    return split_pair(right) + split_pair(np.ascontiguousarray(np.swapaxes(right, 1, 2)))
+        right[c] = np.concatenate([middle.real.T, middle.imag.T], 1)
+        left[c] = np.concatenate([middle.real, middle.imag], 1)
+    return split_pair(right) + split_pair(left)
 
 
 def times(value, cosine, sine):
@@ -100,13 +100,23 @@
     return jnp.dot(left, right, preferred_element_type=F32)
 
 
+def right_block(pair):
+    real, imag = pair[:, :LANES], pair[:, LANES:]
+    return jnp.concatenate([pair, jnp.concatenate([-imag, real], 1)], 0)
+
+
+def left_block(pair):
+    real, imag = pair[:, :LANES], pair[:, LANES:]
+    return jnp.concatenate([jnp.concatenate([real, -imag], 1), jnp.concatenate([imag, real], 1)], 0)
+
+
 def mix_right(store, table_high, table_low):
     rows = store.shape[1]
 
     def step(c, carry):
         high, low = halves(store[c])
-        wide = dot(jnp.concatenate([high, low], 0), table_high[c])
-        store[c] = wide[:rows] + (wide[rows:] + dot(high, table_low[c]))
+        wide = dot(jnp.concatenate([high, low], 0), right_block(table_high[c]))
+        store[c] = wide[:rows] + (wide[rows:] + dot(high, right_block(table_low[c])))
         return carry
 
     lax.fori_loop(0, LEAD, step, 0, unroll=True)
@@ -117,8 +127,8 @@
 
     def step(c, carry):
         high, low = halves(store[c])
-        wide = dot(table_high[c], jnp.concatenate([high, low], 1))
-        store[c] = wide[:, :cols] + (wide[:, cols:] + dot(table_low[c], high))
+        wide = dot(left_block(table_high[c]), jnp.concatenate([high, low], 1))
+        store[c] = wide[:, :cols] + (wide[:, cols:] + dot(left_block(table_low[c]), high))
         return carry
 
     lax.fori_loop(0, LEAD, step, 0, unroll=True)
@@ -196,16 +206,28 @@
     shifts, probe_r, probe_i, object_r, object_i, below_r, below_i, measured, high_in, low_in, out,
     window, probe, table_high, table_low, store, spread, sems, table_sems, measured_sems, out_sems,
 ):
-    held = block_copies(window, (object_r, object_i), 0, sems.at[0])
-    pieces = []
+    row_shift = shifts[0]
+    held, moved, pieces = [], [], []
     for part in range(GROUP):
         rows = pl.ds(part * PART, PART)
-        piece = block_copies(
-            window, (below_r.at[rows], below_i.at[rows]), ROWS + part * PART, sems.at[1 + part]
+        held.append(block_copies(window, (object_r.at[rows], object_i.at[rows]), part * PART, sems.at[part]))
+        moved.append(
+            block_copies(window, (below_r.at[rows], below_i.at[rows]), ROWS + part * PART, sems.at[GROUP + part])
         )
         pieces.append(
-            piece + block_copies(probe, (probe_r.at[rows], probe_i.at[rows]), part * PART, sems.at[5 + part])
+            block_copies(probe, (probe_r.at[rows], probe_i.at[rows]), part * PART, sems.at[2 * GROUP + part])
         )
+
+    def run_held(part, method):
+        @pl.when(row_shift < (part + 1) * PART)
+        def _():
+            run_all(held[part], method)
+
+    def run_moved(part, method):
+        @pl.when(row_shift > part * PART)
+        def _():
+            run_all(moved[part], method)
+
     tables = [
         pltpu.make_async_copy(source, target, table_sems.at[n])
         for n, (source, target) in enumerate(((high_in, table_high), (low_in, table_low)))
@@ -214,13 +236,15 @@
         pltpu.make_async_copy(measured.at[0, :, pl.ds(a * LANES, LANES)], spread.at[a, 2], measured_sems.at[a])
         for a in range(LEAD)
     ]
-    run_all(held, "start")
-    for piece in pieces:
-        run_all(piece, "start")
+    for part in range(GROUP):
+        run_held(part, "start")
+    for part in range(GROUP):
+        run_moved(part, "start")
+        run_all(pieces[part], "start")
     run_all(tables, "start")
     run_all(passing, "start")
-    run_all(held, "wait")
-    row_shift = shifts[0]
+    for part in range(GROUP):
+        run_held(part, "wait")
     tile, shift = lane_parts(shifts[1])
 
     def gather(k, carry):
@@ -241,6 +265,7 @@
         return carry
 
     for part in range(GROUP):
+        run_moved(part, "wait")
         run_all(pieces[part], "wait")
         lax.fori_loop(part * PART // 8, (part + 1) * PART // 8, gather, 0, unroll=UNROLL)
     run_all(tables, "wait")
@@ -271,15 +296,19 @@
 ):
     pieces = [pl.ds(part * PART, PART) for part in range(GROUP)]
     arriving = [
-        pltpu.make_async_copy(columns_in.at[:, :, rows], columns.at[:, :, rows], sems.at[part])
+        pltpu.make_async_copy(
+            columns_in.at[:, pl.ds(0, 2), rows], columns.at[:, pl.ds(0, 2), rows], sems.at[part]
+        )
         for part, rows in enumerate(pieces)
     ]
     tables = [
         pltpu.make_async_copy(source, target, table_sems.at[n])
         for n, (source, target) in enumerate(((high_in, table_high), (low_in, table_low)))
     ]
+    measured = pltpu.make_async_copy(columns_in.at[:, 2], columns.at[:, 2], table_sems.at[2])
     run_all(arriving, "start")
     run_all(tables, "start")
+    measured.start()
 
     def load(c, k):
         at = pl.multiple_of(k * 8, 8)
@@ -311,6 +340,7 @@
         save(dft16(residual, -1), k)
         return carry
 
+    measured.wait()
     lax.fori_loop(0, ROWS // 8, modulus, 0, unroll=UNROLL)
     mix_left(store, table_high, table_low)
 
@@ -568,7 +598,7 @@
             pltpu.VMEM(right_low.shape, BF16),
             pltpu.VMEM((LEAD, ROWS, 2 * LANES), F32),
             pltpu.VMEM((LEAD, 3, ROWS, LANES), F32),
-            pltpu.SemaphoreType.DMA((1 + 2 * GROUP, 2)),
+            pltpu.SemaphoreType.DMA((3 * GROUP, 2)),
             pltpu.SemaphoreType.DMA((2,)),
             pltpu.SemaphoreType.DMA((LEAD,)),
             pltpu.SemaphoreType.DMA((GROUP,)),
@@ -597,7 +627,7 @@
             pltpu.VMEM((2, LEAD, ROWS, LANES), F32),
             pltpu.VMEM((2, LEAD, ROWS, LANES), F32),
             pltpu.SemaphoreType.DMA((GROUP,)),
-            pltpu.SemaphoreType.DMA((2,)),
+            pltpu.SemaphoreType.DMA((3,)),
             pltpu.SemaphoreType.DMA((4, GROUP)),
         ],
         compiler_params=params(60),

time: 215 us -> 215 us (level)
  Pallas kernels: 28.4 us -> 26 us
  waiting for transfers between devices: 49.6 us -> 51.8 us
    ppermute x3, starting transfers between devices: 4.43 us -> 2.07 us  [passed_on(): parts.append(lax.ppermute(part, ('zh', 'zl', 'yl', 'row'), pairs))]
    all_to_all x1, waiting for transfers between devices: 35.5 us -> 37.8 us  [per_device(): columns = lax.all_to_all(exit_spread, 'row', 0, 0, tiled=True)]
  transfers between devices with their start and end apart: 12 -> 12, of which waited for: 4 -> 4; matrix products, arithmetic and copies ran while one was open for 0% -> 0% of each run, Pallas kernels for 9% -> 8%
where the time goes in v4:
time: 215 us; the launch traced here: 214 us
  blocking collectives  103 us (48%)
  waiting for transfers between devices  51.8 us (24%)
  starting transfers between devices  27.2 us (13%)
  Pallas kernels  26 us (12%)
  local copies, waits for them, and re-layouts  3.9 us (2%)
  between operations  2.17 us (1%)
    all_to_all x1, blocking collectives, per_device(): rows_in = lax.all_to_all(returned, group + ('row',), 0, 0, tiled=True)  62.7 us
    all_to_all x1, blocking collectives, per_device(): terms = lax.all_to_all(terms, ('zh',) + group, 0, 0, tiled=True)  40.1 us
    all_to_all x1, waiting for transfers between devices, per_device(): columns = lax.all_to_all(exit_spread, 'row', 0, 0, tiled=True)  37.8 us
    ppermute x2, waiting for transfers between devices, per_device(): lax.ppermute(value, 'row', row_pairs(-1, False) + row_pairs(-1, True))  10.2 us
    pallas_call x1, Pallas kernels, per_device(): pl.pallas_call(detector_kernel, out_shape=shape(GROUP * LEAD, 4, PART, LA...  9.17 us
    pallas_call x1, Pallas kernels, per_device(): pl.pallas_call(gradient_kernel, out_shape=shape(LEAD, 4 * PART + 8, LANES...  8.68 us
    all_to_all x1, starting transfers between devices, per_device(): columns = lax.all_to_all(exit_spread, 'row', 0, 0, tiled=True)  7.79 us
    pallas_call x1, Pallas kernels, per_device(): pl.pallas_call(exit_kernel, out_shape=shape(LEAD, 3, ROWS, LANES), in_spe...  7.23 us
  transfers between devices with their start and end apart: 12, of which 4 were waited for; matrix products, arithmetic and copies ran while one was open for 0% of the time, Pallas kernels for 8%

profile of v4, /device:TPU:1, one launch (start us, length us, event | category | flops | bytes accessed | tf_op | source)
XLA Modules:
  0.0 214.0 jit_solution(15741846405927897942)
XLA Ops:
  0.6 3.3 %collective-permute-start = (f32[128,2304]{1,0:T(8,128)}, f32[128,2304]{1,0:T(8,128)S(1)}, u32[]{:S(2)}, u32[]{:S(2)}) collective-permute-start(f32[128,2304]{1,0:T(8,128)} %refs_8_.1), channel_id=1, source_target_pairs={{0,15},{2,1},{4,3},{6,5},{8,7},{10,9},{12,11},{14,13},{1,0},{3,2},... | collective-permute-start | bytes 3538952 | tf_op jit(solution)/shard_map/ppermute | solution.py:573
  3.9 3.1 %collective-permute-start.1 = (f32[128,2304]{1,0:T(8,128)}, f32[128,2304]{1,0:T(8,128)S(1)}, u32[]{:S(2)}, u32[]{:S(2)}) collective-permute-start(f32[128,2304]{1,0:T(8,128)} %refs_9_.1), channel_id=1, source_target_pairs={{0,15},{2,1},{4,3},{6,5},{8,7},{10,9},{12,11},{14,13},{1,0},{3,2},... | collective-permute-start | bytes 3538952 | tf_op jit(solution)/shard_map/ppermute | solution.py:573
  7.0 1.3 collective-permute-start.5
  8.3 1.3 collective-permute-start.6
  10.9 0.1 pad_add_fusion
  11.0 1.8 collective-permute-start.4
  12.8 1.2 copy-done
  14.0 1.2 copy-done.2
  15.2 0.1 part_kernel.1
  15.3 0.8 copy-done.12
  16.1 2.4 %collective-permute-done.3 = s32[2]{0:T(128)S(1)} collective-permute-done((s32[2]{0:T(128)S(1)}, s32[2]{0:T(128)S(1)}, u32[]{:S(2)}, u32[]{:S(2)}) %collective-permute-start.3) | collective-permute-done | bytes 40 | tf_op jit(solution)/shard_map/ppermute | solution.py:580
  18.5 1.1 collective-permute-start.2
  19.6 1.4 collective-permute-done.2
  20.9 0.6 concatenate.8.shifts
  21.6 10.2 %collective-permute-done.1.below_i.refs_11_ = f32[128,2304]{1,0:T(8,128)S(1)} collective-permute-done((f32[128,2304]{1,0:T(8,128)}, f32[128,2304]{1,0:T(8,128)S(1)}, u32[]{:S(2)}, u32[]{:S(2)}) %collective-permute-start.1) | collective-permute-done | bytes 1179680 | tf_op jit(solution)/shard_map/ppermute | solution.py:573
  31.8 5.6 %collective-permute-start.7 = (f32[2,32,2048]{2,1,0:T(8,128)}, f32[2,32,2048]{2,1,0:T(8,128)}, u32[]{:S(2)}, u32[]{:S(2)}) collective-permute-start(f32[2,32,2048]{2,1,0:T(8,128)} %copy-done.12), channel_id=1, source_target_pairs={{1,2},{3,4},{5,6},{7,8},{9,10},{11,12},{13,14},{15,0},{17,18},{19,... | collective-permute-start | bytes 1572872 | tf_op jit(solution)/shard_map/ppermute | solution.py:588
  37.3 7.2 %exit_kernel.1 = f32[16,3,128,128]{3,2,1,0:T(8,128)} custom-call(s32[11]{0:T(128)} %concatenate.8.shifts, f32[128,2048]{1,0:T(8,128)} %refs_0_.1, f32[128,2048]{1,0:T(8,128)} %refs_1_.1, f32[128,2304]{1,0:T(8,128)} %refs_8_.1, f32[128,2304]{1,0:T(8,128)} %refs_9_.1, f32[128,2304]{1,0:T(8,128)} %copy-done.6, f32[128,2304]{1,0:T(8,128)} %copy-done.8, ...), custom_call_target="tpu_custom_call" | custom-call | flops 2000000000 | bytes 20000000 | tf_op jit(solution)/shard_map/exit_kernel/pallas_call | solution.py:589
  44.6 7.8 %all-to-all-start = ((f32[16,3,128,128]{3,2,1,0:T(8,128)}), f32[16,3,128,128]{3,2,1,0:T(8,128)}, u32[]{:S(2)}, u32[]{:S(2)}) async-start(f32[16,3,128,128]{3,2,1,0:T(8,128)} %exit_kernel.1), calls=%async_computation | async-start | bytes 6291456 | tf_op jit(solution)/shard_map/all_to_all | solution.py:614
  52.4 0.7 collective-permute-start.10
  53.1 0.7 collective-permute-start.9
  53.8 0.7 collective-permute-start.8
  54.5 37.8 %all-to-all-done.columns_in = f32[16,3,128,128]{3,2,1,0:T(8,128)} async-done(((f32[16,3,128,128]{3,2,1,0:T(8,128)}), f32[16,3,128,128]{3,2,1,0:T(8,128)}, u32[]{:S(2)}, u32[]{:S(2)}) %all-to-all-start) | async-done | bytes 3145760 | tf_op jit(solution)/shard_map/all_to_all | solution.py:614
  92.3 9.2 %detector_kernel.1 = f32[64,4,32,128]{3,2,1,0:T(8,128)} custom-call(s32[11]{0:T(128)} %concatenate.8.shifts, f32[16,3,128,128]{3,2,1,0:T(8,128)} %all-to-all-done.columns_in, bf16[16,128,256]{2,1,0:T(8,128)(2,1)} %constant.52.clone.high_in, bf16[16,128,256]{2,1,0:T(8,128)(2,1)} %constant.53.clone.low_in), custom_call_target="tpu_custom_call" | custom-call | flops 4000000000 | bytes 36000000 | tf_op jit(solution)/shard_map/detector_kernel/pallas_call | solution.py:616
  101.5 0.0 copy-start.1
  101.5 0.0 copy-start.3
  101.5 0.0 copy-start.4
  101.5 0.0 copy-start.5
  101.5 0.0 copy-start.10
  101.6 62.7 %all_to_all.15.rows_in = f32[64,4,32,128]{3,2,1,0:T(8,128)S(1)} all-to-all(f32[64,4,32,128]{3,2,1,0:T(8,128)} %detector_kernel.1), channel_id=1, replica_groups=mesh['zh'=4,'zl'=2,'yl'=2,'row'=16] {'zl','yl','row'}, dimensions={0} | all-to-all | bytes 8388608 | tf_op jit(solution)/shard_map/all_to_all | solution.py:638
  164.4 8.7 %gradient_kernel.1 = f32[16,136,128]{2,1,0:T(8,128)S(1)} custom-call(s32[11]{0:T(128)S(1)} %copy-done.13, f32[64,4,32,128]{3,2,1,0:T(8,128)S(1)} %all_to_all.15.rows_in, f32[128,2048]{1,0:T(8,128)S(1)} %copy-done.1, f32[128,2048]{1,0:T(8,128)S(1)} %copy-done.3, f32[128,2048]{1,0:T(8,128)S(1)} %collective-permute-done.5.refs_2_, ...), custom_call_target="tpu_custom_call" | custom-call | flops 4000000000 | bytes 50000000 | tf_op jit(solution)/shard_map/gradient_kernel/pallas_call | solution.py:639
  173.1 40.1 %all_to_all.16.terms = f32[16,136,128]{2,1,0:T(8,128)S(1)} all-to-all(f32[16,136,128]{2,1,0:T(8,128)S(1)} %gradient_kernel.1), channel_id=1, replica_groups=mesh['zh'=4,'zl'=2,'yl'=2,'row'=16] {'zh','zl','yl'}, dimensions={0} | all-to-all | bytes 2228224 | tf_op jit(solution)/shard_map/all_to_all | solution.py:660
  213.1 0.9 total_kernel.1
  (29 shorter events, 0.1 us)
Async XLA Ops:
  0.6 20.9 %collective-permute-start = (f32[128,2304]{1,0:T(8,128)}, f32[128,2304]{1,0:T(8,128)S(1)}, u32[]{:S(2)}, u32[]{:S(2)}) collective-permute-start(f32[128,2304]{1,0:T(8,128)} %refs_8_.1), channel_id=1, source_target_pairs={{0,15},{2,1},{4,3},{6,5},{8,7},{10,9},{12,11},{14,13},{1,0},{3,2},... | collective-permute-start | bytes 3538952 | tf_op jit(solution)/shard_map/ppermute | solution.py:573
  3.9 27.8 %collective-permute-start.1 = (f32[128,2304]{1,0:T(8,128)}, f32[128,2304]{1,0:T(8,128)S(1)}, u32[]{:S(2)}, u32[]{:S(2)}) collective-permute-start(f32[128,2304]{1,0:T(8,128)} %refs_9_.1), channel_id=1, source_target_pairs={{0,15},{2,1},{4,3},{6,5},{8,7},{10,9},{12,11},{14,13},{1,0},{3,2},... | collective-permute-start | bytes 3538952 | tf_op jit(solution)/shard_map/ppermute | solution.py:573
  7.0 14.5 %collective-permute-start.5 = (f32[128,2048]{1,0:T(8,128)}, f32[128,2048]{1,0:T(8,128)S(1)}, u32[]{:S(2)}, u32[]{:S(2)}) collective-permute-start(f32[128,2048]{1,0:T(8,128)} %refs_0_.1), channel_id=1, source_target_pairs={{0,1},{2,3},{4,5},{6,7},{8,9},{10,11},{12,13},{14,15},{16,17},{18,... | collective-permute-start | bytes 3145736 | tf_op jit(solution)/shard_map/ppermute | solution.py:584
  8.3 13.2 %collective-permute-start.6 = (f32[128,2048]{1,0:T(8,128)}, f32[128,2048]{1,0:T(8,128)}, u32[]{:S(2)}, u32[]{:S(2)}) collective-permute-start(f32[128,2048]{1,0:T(8,128)} %refs_1_.1), channel_id=1, source_target_pairs={{0,1},{2,3},{4,5},{6,7},{8,9},{10,11},{12,13},{14,15},{16,17},{18,... | collective-permute-start | bytes 3145736 | tf_op jit(solution)/shard_map/ppermute | solution.py:584
  11.0 5.1 %collective-permute-start.4 = (s32[2]{0:T(128)S(1)}, s32[2]{0:T(128)S(1)}, u32[]{:S(2)}, u32[]{:S(2)}) collective-permute-start(s32[2]{0:T(128)S(1)} %pad_add_fusion), channel_id=1, source_target_pairs={{0,48},{16,32},{32,16},{48,0},{1,49},{17,33},{33,17},{49,1},{2,50}... | collective-permute-start | bytes 32 | tf_op jit(solution)/shard_map/ppermute | solution.py:580
  12.8 1.2 copy-start
  14.0 1.2 copy-start.2
  15.3 0.8 copy-start.12
  16.1 2.4 %collective-permute-start.3 = (s32[2]{0:T(128)S(1)}, s32[2]{0:T(128)S(1)}, u32[]{:S(2)}, u32[]{:S(2)}) collective-permute-start(s32[2]{0:T(128)S(1)} %pad_add_fusion), channel_id=1, source_target_pairs={{0,32},{16,48},{32,0},{48,16},{1,33},{17,49},{33,1},{49,17},{2,34}... | collective-permute-start | bytes 32 | tf_op jit(solution)/shard_map/ppermute | solution.py:580
  18.5 2.5 %collective-permute-start.2 = (s32[2]{0:T(128)S(1)}, s32[2]{0:T(128)S(1)}, u32[]{:S(2)}, u32[]{:S(2)}) collective-permute-start(s32[2]{0:T(128)S(1)} %pad_add_fusion), channel_id=1, source_target_pairs={{0,16},{16,0},{32,48},{48,32},{1,17},{17,1},{33,49},{49,33},{2,18}... | collective-permute-start | bytes 32 | tf_op jit(solution)/shard_map/ppermute | solution.py:580
  21.5 15.8 %copy-start.6 = (f32[128,2304]{1,0:T(8,128)}, f32[128,2304]{1,0:T(8,128)S(1)}, u32[]{:S(2)}) copy-start(f32[128,2304]{1,0:T(8,128)S(1)} %collective-permute-done.below_r.refs_10_) | copy-start | bytes 3538948
  31.8 5.6 %copy-start.8 = (f32[128,2304]{1,0:T(8,128)}, f32[128,2304]{1,0:T(8,128)S(1)}, u32[]{:S(2)}) copy-start(f32[128,2304]{1,0:T(8,128)S(1)} %collective-permute-done.1.below_i.refs_11_) | copy-start | bytes 3538948
  31.8 12.8 %collective-permute-start.7 = (f32[2,32,2048]{2,1,0:T(8,128)}, f32[2,32,2048]{2,1,0:T(8,128)}, u32[]{:S(2)}, u32[]{:S(2)}) collective-permute-start(f32[2,32,2048]{2,1,0:T(8,128)} %copy-done.12), channel_id=1, source_target_pairs={{1,2},{3,4},{5,6},{7,8},{9,10},{11,12},{13,14},{15,0},{17,18},{19,... | collective-permute-start | bytes 1572872 | tf_op jit(solution)/shard_map/ppermute | solution.py:588
  44.6 47.7 %all-to-all-start = ((f32[16,3,128,128]{3,2,1,0:T(8,128)}), f32[16,3,128,128]{3,2,1,0:T(8,128)}, u32[]{:S(2)}, u32[]{:S(2)}) async-start(f32[16,3,128,128]{3,2,1,0:T(8,128)} %exit_kernel.1), calls=%async_computation | async-start | bytes 6291456 | tf_op jit(solution)/shard_map/all_to_all | solution.py:614
  52.4 49.2 %collective-permute-start.10 = (f32[2,32,2048]{2,1,0:T(8,128)}, f32[2,32,2048]{2,1,0:T(8,128)S(1)}, u32[]{:S(2)}, u32[]{:S(2)}) collective-permute-start(f32[2,32,2048]{2,1,0:T(8,128)} %collective-permute-done.7.refs_4_), channel_id=1, source_target_pairs={{32,64},{34,66},{36,68},{38,70},{40,72},{42,74},{44,76},{46,78},{4... | collective-permute-start | bytes 1572872 | tf_op jit(solution)/shard_map/ppermute | solution.py:559
  53.1 48.5 %collective-permute-start.9 = (f32[2,32,2048]{2,1,0:T(8,128)}, f32[2,32,2048]{2,1,0:T(8,128)S(1)}, u32[]{:S(2)}, u32[]{:S(2)}) collective-permute-start(f32[2,32,2048]{2,1,0:T(8,128)} %collective-permute-done.7.refs_4_), channel_id=1, source_target_pairs={{0,64},{2,66},{4,68},{6,70},{8,72},{10,74},{12,76},{14,78},{64,0},... | collective-permute-start | bytes 1572872 | tf_op jit(solution)/shard_map/ppermute | solution.py:559
  53.8 47.8 %collective-permute-start.8 = (f32[2,32,2048]{2,1,0:T(8,128)}, f32[2,32,2048]{2,1,0:T(8,128)S(1)}, u32[]{:S(2)}, u32[]{:S(2)}) collective-permute-start(f32[2,32,2048]{2,1,0:T(8,128)} %collective-permute-done.7.refs_4_), channel_id=1, source_target_pairs={{32,0},{34,2},{36,4},{38,6},{40,8},{42,10},{44,12},{46,14},{48,16}... | collective-permute-start | bytes 1572872 | tf_op jit(solution)/shard_map/ppermute | solution.py:559
  92.3 72.0 %copy-start.11 = (bf16[16,128,256]{2,1,0:T(8,128)(2,1)S(1)}, bf16[16,128,256]{2,1,0:T(8,128)(2,1)}, u32[]{:S(2)}) copy-start(bf16[16,128,256]{2,1,0:T(8,128)(2,1)} %constant.50.clone.high_in.refs_12_) | copy-start | bytes 3145732
  101.5 62.8 %copy-start.1 = (f32[128,2048]{1,0:T(8,128)S(1)}, f32[128,2048]{1,0:T(8,128)}, u32[]{:S(2)}) copy-start(f32[128,2048]{1,0:T(8,128)} %refs_0_.1) | copy-start | bytes 3145732
  101.5 62.8 %copy-start.3 = (f32[128,2048]{1,0:T(8,128)S(1)}, f32[128,2048]{1,0:T(8,128)}, u32[]{:S(2)}) copy-start(f32[128,2048]{1,0:T(8,128)} %refs_1_.1) | copy-start | bytes 3145732
  101.5 62.8 %copy-start.4 = (f32[128,2304]{1,0:T(8,128)S(1)}, f32[128,2304]{1,0:T(8,128)}, u32[]{:S(2)}) copy-start(f32[128,2304]{1,0:T(8,128)} %refs_8_.1) | copy-start | bytes 3538948
  101.5 62.8 %copy-start.5 = (f32[128,2304]{1,0:T(8,128)S(1)}, f32[128,2304]{1,0:T(8,128)}, u32[]{:S(2)}) copy-start(f32[128,2304]{1,0:T(8,128)} %refs_9_.1) | copy-start | bytes 3538948
  101.5 62.8 %copy-start.7 = (f32[128,2304]{1,0:T(8,128)S(1)}, f32[128,2304]{1,0:T(8,128)}, u32[]{:S(2)}) copy-start(f32[128,2304]{1,0:T(8,128)} %copy-done.6) | copy-start | bytes 3538948
  101.5 62.8 %copy-start.9 = (f32[128,2304]{1,0:T(8,128)S(1)}, f32[128,2304]{1,0:T(8,128)}, u32[]{:S(2)}) copy-start(f32[128,2304]{1,0:T(8,128)} %copy-done.8) | copy-start | bytes 3538948
  101.5 62.8 %copy-start.10 = (bf16[16,128,256]{2,1,0:T(8,128)(2,1)S(1)}, bf16[16,128,256]{2,1,0:T(8,128)(2,1)}, u32[]{:S(2)}) copy-start(bf16[16,128,256]{2,1,0:T(8,128)(2,1)} %constant.51.clone.low_in.refs_13_) | copy-start | bytes 3145732
  101.6 62.8 %copy-start.13 = (s32[11]{0:T(128)S(1)}, s32[11]{0:T(128)}, u32[]{:S(2)}) copy-start(s32[11]{0:T(128)} %concatenate.8.shifts) | copy-start | bytes 136

commit v5 on v4

--- a/solution.py
+++ b/solution.py
@@ -203,8 +203,8 @@
 
 
 def exit_kernel(
-    shifts, probe_r, probe_i, object_r, object_i, below_r, below_i, measured, high_in, low_in, out,
-    window, probe, table_high, table_low, store, spread, sems, table_sems, measured_sems, out_sems,
+    shifts, probe_r, probe_i, object_r, object_i, below_r, below_i, high_in, low_in, out,
+    window, probe, table_high, table_low, store, spread, sems, table_sems, out_sems,
 ):
     row_shift = shifts[0]
     held, moved, pieces = [], [], []
@@ -232,17 +232,12 @@
         pltpu.make_async_copy(source, target, table_sems.at[n])
         for n, (source, target) in enumerate(((high_in, table_high), (low_in, table_low)))
     ]
-    passing = [
-        pltpu.make_async_copy(measured.at[0, :, pl.ds(a * LANES, LANES)], spread.at[a, 2], measured_sems.at[a])
-        for a in range(LEAD)
-    ]
     for part in range(GROUP):
         run_held(part, "start")
     for part in range(GROUP):
         run_moved(part, "start")
         run_all(pieces[part], "start")
     run_all(tables, "start")
-    run_all(passing, "start")
     for part in range(GROUP):
         run_held(part, "wait")
     tile, shift = lane_parts(shifts[1])
@@ -279,7 +274,6 @@
             spread[a, 1, rows] = imag
         return carry
 
-    run_all(passing, "wait")
     sends = []
     for part in range(GROUP):
         lax.fori_loop(part * PART // 8, (part + 1) * PART // 8, scatter, 0, unroll=UNROLL)
@@ -291,24 +285,22 @@
 
 
 def detector_kernel(
-    shifts, columns_in, high_in, low_in, out, columns, table_high, table_low, store, wrapped, straight,
-    shifted, sems, table_sems, out_sems,
+    shifts, columns_in, measured_in, high_in, low_in, out, columns, measured, table_high, table_low, store,
+    wrapped, straight, shifted, sems, table_sems, out_sems,
 ):
     pieces = [pl.ds(part * PART, PART) for part in range(GROUP)]
     arriving = [
-        pltpu.make_async_copy(
-            columns_in.at[:, pl.ds(0, 2), rows], columns.at[:, pl.ds(0, 2), rows], sems.at[part]
-        )
+        pltpu.make_async_copy(columns_in.at[:, :, rows], columns.at[:, :, rows], sems.at[part])
         for part, rows in enumerate(pieces)
     ]
     tables = [
         pltpu.make_async_copy(source, target, table_sems.at[n])
         for n, (source, target) in enumerate(((high_in, table_high), (low_in, table_low)))
     ]
-    measured = pltpu.make_async_copy(columns_in.at[:, 2], columns.at[:, 2], table_sems.at[2])
+    amplitudes = pltpu.make_async_copy(measured_in, measured, table_sems.at[2])
     run_all(arriving, "start")
     run_all(tables, "start")
-    measured.start()
+    amplitudes.start()
 
     def load(c, k):
         at = pl.multiple_of(k * 8, 8)
@@ -334,13 +326,13 @@
         rows = pl.ds(pl.multiple_of(k * 8, 8), 8)
         residual = []
         for a, (real, imag) in enumerate(dft16([load(c, k) for c in range(LEAD)], 1)):
-            share = columns[a, 2, rows] * lax.rsqrt(jnp.maximum(real * real + imag * imag, 0.0625))
+            share = measured[a, rows] * lax.rsqrt(jnp.maximum(real * real + imag * imag, 0.0625))
             keep = 1.0 - share
             residual.append((real * keep, -imag * keep))
         save(dft16(residual, -1), k)
         return carry
 
-    measured.wait()
+    amplitudes.wait()
     lax.fori_loop(0, ROWS // 8, modulus, 0, unroll=UNROLL)
     mix_left(store, table_high, table_low)
 
@@ -576,20 +568,16 @@
     core = lax.axis_index("row").astype(jnp.int32) % 2
     part = fetched_part().astype(jnp.int32)
     own_shift = jnp.concatenate([row_shift, col_shift])
-    others = [
-        lax.ppermute(own_shift, group, [(i, i ^ by) for i in range(GROUP)]) for by in range(1, GROUP)
-    ]
-    all_shifts = jnp.concatenate([own_shift] + others + [own[None], core[None], part[None]])
+    measured = amplitudes[0].reshape(ROWS, LEAD, LANES).transpose(1, 0, 2)
+    measured = lax.all_to_all(measured, "row", 0, 0, tiled=True)
     above_part = own_part(part[None], probe_r, probe_i)
     near_above = tuple(lax.ppermute(value, "row", row_pairs(1, True)) for value in (probe_r, probe_i))
-    below_r, below_i, above_part, all_shifts, near_above = together(
-        below_r, below_i, above_part, all_shifts, near_above
-    )
+    below_r, below_i, above_part, near_above = together(below_r, below_i, above_part, near_above)
     above_part = lax.ppermute(above_part, "row", row_pairs(1, False))
     exit_spread = pl.pallas_call(
         exit_kernel,
-        out_shape=shape(LEAD, 3, ROWS, LANES),
-        in_specs=[SMEM, ANY, ANY, ANY, ANY, ANY, ANY, ANY, ANY, ANY],
+        out_shape=shape(LEAD, 2, ROWS, LANES),
+        in_specs=[SMEM] + [ANY] * 8,
         out_specs=ANY,
         scratch_shapes=[
             pltpu.VMEM((2, 2 * ROWS, width), F32),
@@ -597,29 +585,33 @@
             pltpu.VMEM(right_high.shape, BF16),
             pltpu.VMEM(right_low.shape, BF16),
             pltpu.VMEM((LEAD, ROWS, 2 * LANES), F32),
-            pltpu.VMEM((LEAD, 3, ROWS, LANES), F32),
+            pltpu.VMEM((LEAD, 2, ROWS, LANES), F32),
             pltpu.SemaphoreType.DMA((3 * GROUP, 2)),
             pltpu.SemaphoreType.DMA((2,)),
-            pltpu.SemaphoreType.DMA((LEAD,)),
             pltpu.SemaphoreType.DMA((GROUP,)),
         ],
         compiler_params=params(60),
-        cost_estimate=pl.CostEstimate(flops=int(2e9), bytes_accessed=int(20e6), transcendentals=0),
         name="exit_kernel",
     )(
-        all_shifts, probe_r, probe_i, object_r, object_i, below_r, below_i, amplitudes, right_high,
-        right_low,
+        own_shift, probe_r, probe_i, object_r, object_i, below_r, below_i, right_high, right_low,
     )
-    exit_spread, above_part = together(exit_spread, above_part)
+    exit_spread, above_part, measured, late_shift = together(
+        exit_spread, above_part, measured, own_shift
+    )
     columns = lax.all_to_all(exit_spread, "row", 0, 0, tiled=True)
+    others = [
+        lax.ppermute(late_shift, group, [(i, i ^ by) for i in range(GROUP)]) for by in range(1, GROUP)
+    ]
+    all_shifts = jnp.concatenate([late_shift] + others + [own[None], core[None], part[None]])
     above = passed_on(above_part, range(0, LEAD, 2))
     returned = pl.pallas_call(
         detector_kernel,
         out_shape=shape(GROUP * LEAD, 4, PART, LANES),
-        in_specs=[SMEM, ANY, ANY, ANY],
+        in_specs=[SMEM, ANY, ANY, ANY, ANY],
         out_specs=ANY,
         scratch_shapes=[
-            pltpu.VMEM((LEAD, 3, ROWS, LANES), F32),
+            pltpu.VMEM((LEAD, 2, ROWS, LANES), F32),
+            pltpu.VMEM((LEAD, ROWS, LANES), F32),
             pltpu.VMEM(left_high.shape, BF16),
             pltpu.VMEM(left_low.shape, BF16),
             pltpu.VMEM((LEAD, 2 * ROWS, LANES), F32),
@@ -633,8 +625,8 @@
         compiler_params=params(60),
         cost_estimate=pl.CostEstimate(flops=4000000000, bytes_accessed=36000000, transcendentals=0),
         name="detector_kernel",
-    )(all_shifts, columns, left_high, left_low)
-    returned, above = together(returned, above)
+    )(own_shift, columns, measured, left_high, left_low)
+    returned, above, all_shifts = together(returned, above, all_shifts)
     rows_in = lax.all_to_all(returned, group + ("row",), 0, 0, tiled=True)
     terms = pl.pallas_call(
         gradient_kernel,

time: 215 us -> 206 us (0.958)
  waiting for transfers between devices: 51.8 us -> 45 us
  blocking collectives: 103 us -> 99.6 us
    all_to_all x1, waiting for transfers between devices: 37.8 us -> 18.7 us  [per_device(): columns = lax.all_to_all(exit_spread, 'row', 0, 0, tiled=True)]
    ppermute x2, waiting for transfers between devices: 10.2 us -> 21 us  [per_device(): lax.ppermute(value, 'row', row_pairs(-1, False) + row_pairs(-1, True))]
    all_to_all x0 -> x1, starting transfers between devices: none -> 7.27 us  [per_device(): measured = lax.all_to_all(measured, 'row', 0, 0, tiled=True)]
    ppermute x1, starting transfers between devices: 5.55 us -> 1.76 us  [per_device(): above_part = lax.ppermute(above_part, 'row', row_pairs(1, False))]
    all_to_all x1, blocking collectives: 62.7 us -> 59.5 us  [per_device(): rows_in = lax.all_to_all(returned, group + ('row',), 0, 0, tiled=True)]
  transfers between devices with their start and end apart: 12 -> 13, of which waited for: 4 -> 5; matrix products, arithmetic and copies ran while one was open for 0% -> 2% of each run, Pallas kernels for 8% -> 8%
where the time goes in v5:
time: 206 us
  blocking collectives  99.6 us (48%)
  waiting for transfers between devices  45 us (22%)
  starting transfers between devices  29.3 us (14%)
  Pallas kernels  25.8 us (13%)
  local copies, waits for them, and re-layouts  3.01 us (1%)
  between operations  2.23 us (1%)
    all_to_all x1, blocking collectives, per_device(): rows_in = lax.all_to_all(returned, group + ('row',), 0, 0, tiled=True)  59.5 us
    all_to_all x1, blocking collectives, per_device(): terms = lax.all_to_all(terms, ('zh',) + group, 0, 0, tiled=True)  40.2 us
    ppermute x2, waiting for transfers between devices, per_device(): lax.ppermute(value, 'row', row_pairs(-1, False) + row_pairs(-1, True))  21 us
    all_to_all x1, waiting for transfers between devices, per_device(): columns = lax.all_to_all(exit_spread, 'row', 0, 0, tiled=True)  18.7 us
    pallas_call x1, Pallas kernels, per_device(): pl.pallas_call(detector_kernel, out_shape=shape(GROUP * LEAD, 4, PART, LA...  9.2 us
    pallas_call x1, Pallas kernels, per_device(): pl.pallas_call(gradient_kernel, out_shape=shape(LEAD, 4 * PART + 8, LANES...  8.37 us
    all_to_all x1, starting transfers between devices, per_device(): measured = lax.all_to_all(measured, 'row', 0, 0, tiled=True)  7.27 us
    all_to_all x1, starting transfers between devices, per_device(): columns = lax.all_to_all(exit_spread, 'row', 0, 0, tiled=True)  6.78 us
  transfers between devices with their start and end apart: 13, of which 5 were waited for; matrix products, arithmetic and copies ran while one was open for 2% of the time, Pallas kernels for 8%

profile of v5, /device:TPU:1, one launch (start us, length us, event | category | flops | bytes accessed | tf_op | source)
XLA Modules:
  0.0 205.6 jit_solution(11915957264329468740)
XLA Ops:
  0.6 3.3 %collective-permute-start = (f32[128,2304]{1,0:T(8,128)}, f32[128,2304]{1,0:T(8,128)S(1)}, u32[]{:S(2)}, u32[]{:S(2)}) collective-permute-start(f32[128,2304]{1,0:T(8,128)} %refs_8_.1), channel_id=1, source_target_pairs={{0,15},{2,1},{4,3},{6,5},{8,7},{10,9},{12,11},{14,13},{1,0},{3,2},... | collective-permute-start | bytes 3538952 | tf_op jit(solution)/shard_map/ppermute | solution.py:565
  3.9 3.1 %collective-permute-start.1 = (f32[128,2304]{1,0:T(8,128)}, f32[128,2304]{1,0:T(8,128)}, u32[]{:S(2)}, u32[]{:S(2)}) collective-permute-start(f32[128,2304]{1,0:T(8,128)} %refs_9_.1), channel_id=1, source_target_pairs={{0,15},{2,1},{4,3},{6,5},{8,7},{10,9},{12,11},{14,13},{1,0},{3,2},... | collective-permute-start | bytes 3538952 | tf_op jit(solution)/shard_map/ppermute | solution.py:565
  7.0 1.3 collective-permute-start.2
  8.3 1.3 collective-permute-start.3
  9.6 1.5 copy.15
  11.2 1.3 copy.16
  12.5 7.3 %all-to-all-start = ((f32[16,128,128]{2,1,0:T(8,128)}), f32[16,128,128]{2,1,0:T(8,128)}, u32[]{:S(2)}, u32[]{:S(2)}) async-start(f32[16,128,128]{2,1,0:T(8,128)} %bitcast.7), calls=%async_computation | async-start | bytes 2097152 | tf_op jit(solution)/shard_map/all_to_all | solution.py:572
  19.8 0.9 part_kernel.1
  20.7 21.0 %collective-permute-done.1.below_i.refs_11_ = f32[128,2304]{1,0:T(8,128)} collective-permute-done((f32[128,2304]{1,0:T(8,128)}, f32[128,2304]{1,0:T(8,128)}, u32[]{:S(2)}, u32[]{:S(2)}) %collective-permute-start.1) | collective-permute-done | bytes 1179680 | tf_op jit(solution)/shard_map/ppermute | solution.py:565
  41.7 1.8 collective-permute-start.4
  44.8 0.6 pad_add_fusion.shifts
  45.3 6.5 %exit_kernel.1 = f32[16,2,128,128]{3,2,1,0:T(8,128)} custom-call(s32[2]{0:T(128)} %pad_add_fusion.shifts, f32[128,2048]{1,0:T(8,128)} %refs_0_.1, f32[128,2048]{1,0:T(8,128)} %refs_1_.1, f32[128,2304]{1,0:T(8,128)} %refs_8_.1, f32[128,2304]{1,0:T(8,128)} %refs_9_.1, f32[128,2304]{1,0:T(8,128)} %copy-done.6, ...), custom_call_target="tpu_custom_call" | custom-call | tf_op jit(solution)/shard_map/exit_kernel/pallas_call | solution.py:577
  51.9 6.8 %all-to-all-start.1 = ((f32[16,2,128,128]{3,2,1,0:T(8,128)}), f32[16,2,128,128]{3,2,1,0:T(8,128)}, u32[]{:S(2)}, u32[]{:S(2)}) async-start(f32[16,2,128,128]{3,2,1,0:T(8,128)} %exit_kernel.1), calls=%async_computation.1 | async-start | bytes 4194304 | tf_op jit(solution)/shard_map/all_to_all | solution.py:601
  58.7 0.7 collective-permute-start.7
  59.3 0.7 collective-permute-start.6
  60.1 0.7 collective-permute-start.5
  60.8 1.9 collective-permute-start.10
  62.7 1.9 collective-permute-done.10
  64.6 0.5 collective-permute-start.8
  65.0 0.5 collective-permute-done.9
  65.5 3.0 %collective-permute-done.8 = s32[2]{0:T(128)S(1)} collective-permute-done((s32[2]{0:T(128)S(1)}, s32[2]{0:T(128)S(1)}, u32[]{:S(2)}, u32[]{:S(2)}) %collective-permute-start.8) | collective-permute-done | bytes 40 | tf_op jit(solution)/shard_map/ppermute | solution.py:603
  68.5 0.1 concatenate.7.shifts
  68.6 18.7 %all-to-all-done.1.columns_in = f32[16,2,128,128]{3,2,1,0:T(8,128)} async-done(((f32[16,2,128,128]{3,2,1,0:T(8,128)}), f32[16,2,128,128]{3,2,1,0:T(8,128)}, u32[]{:S(2)}, u32[]{:S(2)}) %all-to-all-start.1) | async-done | bytes 2097184 | tf_op jit(solution)/shard_map/all_to_all | solution.py:601
  87.3 9.2 %detector_kernel.1 = f32[64,4,32,128]{3,2,1,0:T(8,128)} custom-call(s32[2]{0:T(128)} %pad_add_fusion.shifts, f32[16,2,128,128]{3,2,1,0:T(8,128)} %all-to-all-done.1.columns_in, f32[16,128,128]{2,1,0:T(8,128)} %all-to-all-done.measured_in, bf16[16,128,256]{2,1,0:T(8,128)(2,1)} %constant.52.clone.high_in, bf16[16,128,256]{2,1,0:T(8,128)(2,1)} %constant.53.clone.low_in), custom_call_target="tpu_custom_call" | custom-call | flops 4000000000 | bytes 36000000 | tf_op jit(solution)/shard_map/detector_kernel/pallas_call | solution.py:607
  96.5 0.0 copy-start.1
  96.5 0.0 copy-start.5
  96.6 0.0 copy-start.8
  96.6 0.0 copy-start.9
  96.6 59.5 %all_to_all.20.rows_in = f32[64,4,32,128]{3,2,1,0:T(8,128)S(1)} all-to-all(f32[64,4,32,128]{3,2,1,0:T(8,128)} %detector_kernel.1), channel_id=1, replica_groups=mesh['zh'=4,'zl'=2,'yl'=2,'row'=16] {'zl','yl','row'}, dimensions={0} | all-to-all | bytes 8388608 | tf_op jit(solution)/shard_map/all_to_all | solution.py:630
  156.1 8.4 %gradient_kernel.1 = f32[16,136,128]{2,1,0:T(8,128)S(1)} custom-call(s32[11]{0:T(128)S(1)} %concatenate.7.shifts, f32[64,4,32,128]{3,2,1,0:T(8,128)S(1)} %all_to_all.20.rows_in, f32[128,2048]{1,0:T(8,128)S(1)} %copy-done.1, f32[128,2048]{1,0:T(8,128)S(1)} %copy-done.3, f32[128,2048]{1,0:T(8,128)} %collective-permute-done.2.refs_2_, ...), custom_call_target="tpu_custom_call" | custom-call | flops 4000000000 | bytes 50000000 | tf_op jit(solution)/shard_map/gradient_kernel/pallas_call | solution.py:631
  164.5 40.2 %all_to_all.21.terms = f32[16,136,128]{2,1,0:T(8,128)S(1)} all-to-all(f32[16,136,128]{2,1,0:T(8,128)S(1)} %gradient_kernel.1), channel_id=1, replica_groups=mesh['zh'=4,'zl'=2,'yl'=2,'row'=16] {'zh','zl','yl'}, dimensions={0} | all-to-all | bytes 2228224 | tf_op jit(solution)/shard_map/all_to_all | solution.py:652
  204.7 0.9 total_kernel.1
  (27 shorter events, 0.1 us)
Async XLA Ops:
  0.6 20.1 %collective-permute-start = (f32[128,2304]{1,0:T(8,128)}, f32[128,2304]{1,0:T(8,128)S(1)}, u32[]{:S(2)}, u32[]{:S(2)}) collective-permute-start(f32[128,2304]{1,0:T(8,128)} %refs_8_.1), channel_id=1, source_target_pairs={{0,15},{2,1},{4,3},{6,5},{8,7},{10,9},{12,11},{14,13},{1,0},{3,2},... | collective-permute-start | bytes 3538952 | tf_op jit(solution)/shard_map/ppermute | solution.py:565
  3.9 37.7 %collective-permute-start.1 = (f32[128,2304]{1,0:T(8,128)}, f32[128,2304]{1,0:T(8,128)}, u32[]{:S(2)}, u32[]{:S(2)}) collective-permute-start(f32[128,2304]{1,0:T(8,128)} %refs_9_.1), channel_id=1, source_target_pairs={{0,15},{2,1},{4,3},{6,5},{8,7},{10,9},{12,11},{14,13},{1,0},{3,2},... | collective-permute-start | bytes 3538952 | tf_op jit(solution)/shard_map/ppermute | solution.py:565
  7.0 13.6 %collective-permute-start.2 = (f32[128,2048]{1,0:T(8,128)}, f32[128,2048]{1,0:T(8,128)}, u32[]{:S(2)}, u32[]{:S(2)}) collective-permute-start(f32[128,2048]{1,0:T(8,128)} %refs_0_.1), channel_id=1, source_target_pairs={{0,1},{2,3},{4,5},{6,7},{8,9},{10,11},{12,13},{14,15},{16,17},{18,... | collective-permute-start | bytes 3145736 | tf_op jit(solution)/shard_map/ppermute | solution.py:574
  8.3 12.4 %collective-permute-start.3 = (f32[128,2048]{1,0:T(8,128)}, f32[128,2048]{1,0:T(8,128)}, u32[]{:S(2)}, u32[]{:S(2)}) collective-permute-start(f32[128,2048]{1,0:T(8,128)} %refs_1_.1), channel_id=1, source_target_pairs={{0,1},{2,3},{4,5},{6,7},{8,9},{10,11},{12,13},{14,15},{16,17},{18,... | collective-permute-start | bytes 3145736 | tf_op jit(solution)/shard_map/ppermute | solution.py:574
  12.5 7.3 %copy-start = (f32[128,2048]{1,0:T(8,128)S(1)}, f32[128,2048]{1,0:T(8,128)}, u32[]{:S(2)}) copy-start(f32[128,2048]{1,0:T(8,128)} %refs_0_.1) | copy-start | bytes 3145732
  12.5 7.3 %copy-start.2 = (f32[128,2048]{1,0:T(8,128)S(1)}, f32[128,2048]{1,0:T(8,128)}, u32[]{:S(2)}) copy-start(f32[128,2048]{1,0:T(8,128)} %refs_1_.1) | copy-start | bytes 3145732
  12.5 39.3 %all-to-all-start = ((f32[16,128,128]{2,1,0:T(8,128)}), f32[16,128,128]{2,1,0:T(8,128)}, u32[]{:S(2)}, u32[]{:S(2)}) async-start(f32[16,128,128]{2,1,0:T(8,128)} %bitcast.7), calls=%async_computation | async-start | bytes 2097152 | tf_op jit(solution)/shard_map/all_to_all | solution.py:572
  20.7 24.6 %copy-start.6 = (f32[128,2304]{1,0:T(8,128)}, f32[128,2304]{1,0:T(8,128)S(1)}, u32[]{:S(2)}) copy-start(f32[128,2304]{1,0:T(8,128)S(1)} %collective-permute-done.below_r.refs_10_) | copy-start | bytes 3538948
  41.7 10.2 %collective-permute-start.4 = (f32[2,32,2048]{2,1,0:T(8,128)}, f32[2,32,2048]{2,1,0:T(8,128)S(1)}, u32[]{:S(2)}, u32[]{:S(2)}) collective-permute-start(f32[2,32,2048]{2,1,0:T(8,128)} %part_kernel.1), channel_id=1, source_target_pairs={{1,2},{3,4},{5,6},{7,8},{9,10},{11,12},{13,14},{15,0},{17,18},{19,... | collective-permute-start | bytes 1572872 | tf_op jit(solution)/shard_map/ppermute | solution.py:576
  51.8 8.9 %copy-start.10 = (s32[2]{0:T(128)S(1)}, s32[2]{0:T(128)}, u32[]{:S(2)}) copy-start(s32[2]{0:T(128)} %pad_add_fusion.shifts) | copy-start | bytes 28
  51.9 35.4 %all-to-all-start.1 = ((f32[16,2,128,128]{3,2,1,0:T(8,128)}), f32[16,2,128,128]{3,2,1,0:T(8,128)}, u32[]{:S(2)}, u32[]{:S(2)}) async-start(f32[16,2,128,128]{3,2,1,0:T(8,128)} %exit_kernel.1), calls=%async_computation.1 | async-start | bytes 4194304 | tf_op jit(solution)/shard_map/all_to_all | solution.py:601
  58.7 37.9 %collective-permute-start.7 = (f32[2,32,2048]{2,1,0:T(8,128)S(1)}, f32[2,32,2048]{2,1,0:T(8,128)S(1)}, u32[]{:S(2)}, u32[]{:S(2)}) collective-permute-start(f32[2,32,2048]{2,1,0:T(8,128)S(1)} %collective-permute-done.4.refs_4_), channel_id=1, source_target_pairs={{32,64},{34,66},{36,68},{38,70},{40,72},{42,74},{44,76},{46,78},{4... | collective-permute-start | bytes 1572872 | tf_op jit(solution)/shard_map/ppermute | solution.py:551
  59.3 37.2 %collective-permute-start.6 = (f32[2,32,2048]{2,1,0:T(8,128)S(1)}, f32[2,32,2048]{2,1,0:T(8,128)S(1)}, u32[]{:S(2)}, u32[]{:S(2)}) collective-permute-start(f32[2,32,2048]{2,1,0:T(8,128)S(1)} %collective-permute-done.4.refs_4_), channel_id=1, source_target_pairs={{0,64},{2,66},{4,68},{6,70},{8,72},{10,74},{12,76},{14,78},{64,0},... | collective-permute-start | bytes 1572872 | tf_op jit(solution)/shard_map/ppermute | solution.py:551
  60.1 36.6 %collective-permute-start.5 = (f32[2,32,2048]{2,1,0:T(8,128)S(1)}, f32[2,32,2048]{2,1,0:T(8,128)S(1)}, u32[]{:S(2)}, u32[]{:S(2)}) collective-permute-start(f32[2,32,2048]{2,1,0:T(8,128)S(1)} %collective-permute-done.4.refs_4_), channel_id=1, source_target_pairs={{32,0},{34,2},{36,4},{38,6},{40,8},{42,10},{44,12},{46,14},{48,16}... | collective-permute-start | bytes 1572872 | tf_op jit(solution)/shard_map/ppermute | solution.py:551
  60.8 3.8 %collective-permute-start.10 = (s32[2]{0:T(128)S(1)}, s32[2]{0:T(128)S(1)}, u32[]{:S(2)}, u32[]{:S(2)}) collective-permute-start(s32[2]{0:T(128)S(1)} %copy-done.10), channel_id=1, source_target_pairs={{0,48},{16,32},{32,16},{48,0},{1,49},{17,33},{33,17},{49,1},{2,50}... | collective-permute-start | bytes 32 | tf_op jit(solution)/shard_map/ppermute | solution.py:603
  62.7 2.8 %collective-permute-start.9 = (s32[2]{0:T(128)S(1)}, s32[2]{0:T(128)S(1)}, u32[]{:S(2)}, u32[]{:S(2)}) collective-permute-start(s32[2]{0:T(128)S(1)} %copy-done.10), channel_id=1, source_target_pairs={{0,32},{16,48},{32,0},{48,16},{1,33},{17,49},{33,1},{49,17},{2,34}... | collective-permute-start | bytes 32 | tf_op jit(solution)/shard_map/ppermute | solution.py:603
  64.6 4.0 %collective-permute-start.8 = (s32[2]{0:T(128)S(1)}, s32[2]{0:T(128)S(1)}, u32[]{:S(2)}, u32[]{:S(2)}) collective-permute-start(s32[2]{0:T(128)S(1)} %copy-done.10), channel_id=1, source_target_pairs={{0,16},{16,0},{32,48},{48,32},{1,17},{17,1},{33,49},{49,33},{2,18}... | collective-permute-start | bytes 32 | tf_op jit(solution)/shard_map/ppermute | solution.py:603
  96.5 59.6 %copy-start.1 = (f32[128,2048]{1,0:T(8,128)S(1)}, f32[128,2048]{1,0:T(8,128)}, u32[]{:S(2)}) copy-start(f32[128,2048]{1,0:T(8,128)} %refs_0_.1) | copy-start | bytes 3145732
  96.5 59.6 %copy-start.3 = (f32[128,2048]{1,0:T(8,128)S(1)}, f32[128,2048]{1,0:T(8,128)}, u32[]{:S(2)}) copy-start(f32[128,2048]{1,0:T(8,128)} %refs_1_.1) | copy-start | bytes 3145732
  96.5 59.6 %copy-start.4 = (f32[128,2304]{1,0:T(8,128)S(1)}, f32[128,2304]{1,0:T(8,128)}, u32[]{:S(2)}) copy-start(f32[128,2304]{1,0:T(8,128)} %refs_8_.1) | copy-start | bytes 3538948
  96.5 59.6 %copy-start.5 = (f32[128,2304]{1,0:T(8,128)S(1)}, f32[128,2304]{1,0:T(8,128)}, u32[]{:S(2)}) copy-start(f32[128,2304]{1,0:T(8,128)} %refs_9_.1) | copy-start | bytes 3538948
  96.5 59.6 %copy-start.7 = (f32[128,2304]{1,0:T(8,128)S(1)}, f32[128,2304]{1,0:T(8,128)}, u32[]{:S(2)}) copy-start(f32[128,2304]{1,0:T(8,128)} %copy-done.6) | copy-start | bytes 3538948
  96.6 59.6 %copy-start.8 = (bf16[16,128,256]{2,1,0:T(8,128)(2,1)S(1)}, bf16[16,128,256]{2,1,0:T(8,128)(2,1)}, u32[]{:S(2)}) copy-start(bf16[16,128,256]{2,1,0:T(8,128)(2,1)} %constant.51.clone.low_in.refs_13_) | copy-start | bytes 3145732
  96.6 59.6 %copy-start.9 = (bf16[16,128,256]{2,1,0:T(8,128)(2,1)S(1)}, bf16[16,128,256]{2,1,0:T(8,128)(2,1)}, u32[]{:S(2)}) copy-start(bf16[16,128,256]{2,1,0:T(8,128)(2,1)} %constant.50.clone.high_in.refs_12_) | copy-start | bytes 3145732

commit v6 on v5

--- a/solution.py
+++ b/solution.py
@@ -572,7 +572,9 @@
     measured = lax.all_to_all(measured, "row", 0, 0, tiled=True)
     above_part = own_part(part[None], probe_r, probe_i)
     near_above = tuple(lax.ppermute(value, "row", row_pairs(1, True)) for value in (probe_r, probe_i))
-    below_r, below_i, above_part, near_above = together(below_r, below_i, above_part, near_above)
+    below_r, below_i, above_part, near_above, own_shift = together(
+        below_r, below_i, above_part, near_above, own_shift
+    )
     above_part = lax.ppermute(above_part, "row", row_pairs(1, False))
     exit_spread = pl.pallas_call(
         exit_kernel,

time: 206 us -> 206 us (level)
  transfers between devices with their start and end apart: 13 -> 13, of which waited for: 5 -> 6; matrix products, arithmetic and copies ran while one was open for 2% -> 2% of each run, Pallas kernels for 8% -> 8%
where the time goes in v6:
time: 206 us
  blocking collectives  99.6 us (48%)
  waiting for transfers between devices  43.7 us (21%)
  starting transfers between devices  30.6 us (15%)
  Pallas kernels  25.8 us (13%)
  local copies, waits for them, and re-layouts  3.01 us (1%)
  between operations  2.22 us (1%)
    all_to_all x1, blocking collectives, per_device(): rows_in = lax.all_to_all(returned, group + ('row',), 0, 0, tiled=True)  59.5 us
    all_to_all x1, blocking collectives, per_device(): terms = lax.all_to_all(terms, ('zh',) + group, 0, 0, tiled=True)  40.2 us
    ppermute x2, waiting for transfers between devices, per_device(): lax.ppermute(value, 'row', row_pairs(-1, False) + row_pairs(-1, True))  19.1 us
    all_to_all x1, waiting for transfers between devices, per_device(): columns = lax.all_to_all(exit_spread, 'row', 0, 0, tiled=True)  18.7 us
    pallas_call x1, Pallas kernels, per_device(): pl.pallas_call(detector_kernel, out_shape=shape(GROUP * LEAD, 4, PART, LA...  9.2 us
    pallas_call x1, Pallas kernels, per_device(): pl.pallas_call(gradient_kernel, out_shape=shape(LEAD, 4 * PART + 8, LANES...  8.37 us
    all_to_all x1, starting transfers between devices, per_device(): columns = lax.all_to_all(exit_spread, 'row', 0, 0, tiled=True)  8.1 us
    all_to_all x1, starting transfers between devices, per_device(): measured = lax.all_to_all(measured, 'row', 0, 0, tiled=True)  7.27 us
  transfers between devices with their start and end apart: 13, of which 6 were waited for; matrix products, arithmetic and copies ran while one was open for 2% of the time, Pallas kernels for 8%

profile of v6, /device:TPU:1, one launch (start us, length us, event | category | flops | bytes accessed | tf_op | source)
XLA Modules:
  0.0 205.6 jit_solution(16887300213198136816)
XLA Ops:
  0.6 3.3 %collective-permute-start = (f32[128,2304]{1,0:T(8,128)}, f32[128,2304]{1,0:T(8,128)S(1)}, u32[]{:S(2)}, u32[]{:S(2)}) collective-permute-start(f32[128,2304]{1,0:T(8,128)} %refs_8_.1), channel_id=1, source_target_pairs={{0,15},{2,1},{4,3},{6,5},{8,7},{10,9},{12,11},{14,13},{1,0},{3,2},... | collective-permute-start | bytes 3538952 | tf_op jit(solution)/shard_map/ppermute | solution.py:565
  3.9 3.1 %collective-permute-start.1 = (f32[128,2304]{1,0:T(8,128)}, f32[128,2304]{1,0:T(8,128)}, u32[]{:S(2)}, u32[]{:S(2)}) collective-permute-start(f32[128,2304]{1,0:T(8,128)} %refs_9_.1), channel_id=1, source_target_pairs={{0,15},{2,1},{4,3},{6,5},{8,7},{10,9},{12,11},{14,13},{1,0},{3,2},... | collective-permute-start | bytes 3538952 | tf_op jit(solution)/shard_map/ppermute | solution.py:565
  7.0 1.3 collective-permute-start.2
  8.3 1.3 collective-permute-start.3
  9.6 1.5 copy.15
  11.2 1.3 copy.16
  12.5 7.3 %all-to-all-start = ((f32[16,128,128]{2,1,0:T(8,128)}), f32[16,128,128]{2,1,0:T(8,128)}, u32[]{:S(2)}, u32[]{:S(2)}) async-start(f32[16,128,128]{2,1,0:T(8,128)} %bitcast.7), calls=%async_computation | async-start | bytes 2097152 | tf_op jit(solution)/shard_map/all_to_all | solution.py:572
  21.1 0.9 part_kernel.1
  22.0 0.6 pad_add_fusion.shifts
  22.6 19.1 %collective-permute-done.1.below_i.refs_11_ = f32[128,2304]{1,0:T(8,128)} collective-permute-done((f32[128,2304]{1,0:T(8,128)}, f32[128,2304]{1,0:T(8,128)}, u32[]{:S(2)}, u32[]{:S(2)}) %collective-permute-start.1) | collective-permute-done | bytes 1179680 | tf_op jit(solution)/shard_map/ppermute | solution.py:565
  41.7 1.8 collective-permute-start.4
  43.5 6.5 %exit_kernel.1 = f32[16,2,128,128]{3,2,1,0:T(8,128)} custom-call(s32[2]{0:T(128)} %pad_add_fusion.shifts, f32[128,2048]{1,0:T(8,128)} %refs_0_.1, f32[128,2048]{1,0:T(8,128)} %refs_1_.1, f32[128,2304]{1,0:T(8,128)} %refs_8_.1, f32[128,2304]{1,0:T(8,128)} %refs_9_.1, f32[128,2304]{1,0:T(8,128)} %copy-done.6, ...), custom_call_target="tpu_custom_call" | custom-call | tf_op jit(solution)/shard_map/exit_kernel/pallas_call | solution.py:579
  50.0 0.0 copy-start.10
  50.0 0.6 collective-permute-done.4.refs_4_
  50.6 8.1 %all-to-all-start.1 = ((f32[16,2,128,128]{3,2,1,0:T(8,128)}), f32[16,2,128,128]{3,2,1,0:T(8,128)}, u32[]{:S(2)}, u32[]{:S(2)}) async-start(f32[16,2,128,128]{3,2,1,0:T(8,128)} %exit_kernel.1), calls=%async_computation.1 | async-start | bytes 4194304 | tf_op jit(solution)/shard_map/all_to_all | solution.py:603
  58.7 0.7 collective-permute-start.7
  59.3 0.7 collective-permute-start.6
  60.1 0.7 collective-permute-start.5
  60.8 1.9 collective-permute-start.10
  62.7 1.9 collective-permute-done.10
  64.6 0.5 collective-permute-start.8
  65.0 0.5 collective-permute-done.9
  65.5 3.0 %collective-permute-done.8 = s32[2]{0:T(128)S(1)} collective-permute-done((s32[2]{0:T(128)S(1)}, s32[2]{0:T(128)S(1)}, u32[]{:S(2)}, u32[]{:S(2)}) %collective-permute-start.8) | collective-permute-done | bytes 40 | tf_op jit(solution)/shard_map/ppermute | solution.py:605
  68.5 0.1 concatenate.7.shifts
  68.6 18.7 %all-to-all-done.1.columns_in = f32[16,2,128,128]{3,2,1,0:T(8,128)} async-done(((f32[16,2,128,128]{3,2,1,0:T(8,128)}), f32[16,2,128,128]{3,2,1,0:T(8,128)}, u32[]{:S(2)}, u32[]{:S(2)}) %all-to-all-start.1) | async-done | bytes 2097184 | tf_op jit(solution)/shard_map/all_to_all | solution.py:603
  87.3 9.2 %detector_kernel.1 = f32[64,4,32,128]{3,2,1,0:T(8,128)} custom-call(s32[2]{0:T(128)} %pad_add_fusion.shifts, f32[16,2,128,128]{3,2,1,0:T(8,128)} %all-to-all-done.1.columns_in, f32[16,128,128]{2,1,0:T(8,128)} %all-to-all-done.measured_in, bf16[16,128,256]{2,1,0:T(8,128)(2,1)} %constant.52.clone.high_in, bf16[16,128,256]{2,1,0:T(8,128)(2,1)} %constant.53.clone.low_in), custom_call_target="tpu_custom_call" | custom-call | flops 4000000000 | bytes 36000000 | tf_op jit(solution)/shard_map/detector_kernel/pallas_call | solution.py:609
  96.6 0.0 copy-start.8
  96.6 0.0 copy-start.9
  96.6 59.5 %all_to_all.20.rows_in = f32[64,4,32,128]{3,2,1,0:T(8,128)S(1)} all-to-all(f32[64,4,32,128]{3,2,1,0:T(8,128)} %detector_kernel.1), channel_id=1, replica_groups=mesh['zh'=4,'zl'=2,'yl'=2,'row'=16] {'zl','yl','row'}, dimensions={0} | all-to-all | bytes 8388608 | tf_op jit(solution)/shard_map/all_to_all | solution.py:632
  156.1 8.4 %gradient_kernel.1 = f32[16,136,128]{2,1,0:T(8,128)S(1)} custom-call(s32[11]{0:T(128)S(1)} %concatenate.7.shifts, f32[64,4,32,128]{3,2,1,0:T(8,128)S(1)} %all_to_all.20.rows_in, f32[128,2048]{1,0:T(8,128)S(1)} %copy-done.1, f32[128,2048]{1,0:T(8,128)S(1)} %copy-done.3, f32[128,2048]{1,0:T(8,128)} %collective-permute-done.2.refs_2_, ...), custom_call_target="tpu_custom_call" | custom-call | flops 4000000000 | bytes 50000000 | tf_op jit(solution)/shard_map/gradient_kernel/pallas_call | solution.py:633
  164.5 40.2 %all_to_all.21.terms = f32[16,136,128]{2,1,0:T(8,128)S(1)} all-to-all(f32[16,136,128]{2,1,0:T(8,128)S(1)} %gradient_kernel.1), channel_id=1, replica_groups=mesh['zh'=4,'zl'=2,'yl'=2,'row'=16] {'zh','zl','yl'}, dimensions={0} | all-to-all | bytes 2228224 | tf_op jit(solution)/shard_map/all_to_all | solution.py:654
  204.7 0.9 total_kernel.1
  (27 shorter events, 0.1 us)
Async XLA Ops:
  0.6 21.9 %collective-permute-start = (f32[128,2304]{1,0:T(8,128)}, f32[128,2304]{1,0:T(8,128)S(1)}, u32[]{:S(2)}, u32[]{:S(2)}) collective-permute-start(f32[128,2304]{1,0:T(8,128)} %refs_8_.1), channel_id=1, source_target_pairs={{0,15},{2,1},{4,3},{6,5},{8,7},{10,9},{12,11},{14,13},{1,0},{3,2},... | collective-permute-start | bytes 3538952 | tf_op jit(solution)/shard_map/ppermute | solution.py:565
  3.9 37.7 %collective-permute-start.1 = (f32[128,2304]{1,0:T(8,128)}, f32[128,2304]{1,0:T(8,128)}, u32[]{:S(2)}, u32[]{:S(2)}) collective-permute-start(f32[128,2304]{1,0:T(8,128)} %refs_9_.1), channel_id=1, source_target_pairs={{0,15},{2,1},{4,3},{6,5},{8,7},{10,9},{12,11},{14,13},{1,0},{3,2},... | collective-permute-start | bytes 3538952 | tf_op jit(solution)/shard_map/ppermute | solution.py:565
  7.0 15.5 %collective-permute-start.2 = (f32[128,2048]{1,0:T(8,128)}, f32[128,2048]{1,0:T(8,128)}, u32[]{:S(2)}, u32[]{:S(2)}) collective-permute-start(f32[128,2048]{1,0:T(8,128)} %refs_0_.1), channel_id=1, source_target_pairs={{0,1},{2,3},{4,5},{6,7},{8,9},{10,11},{12,13},{14,15},{16,17},{18,... | collective-permute-start | bytes 3145736 | tf_op jit(solution)/shard_map/ppermute | solution.py:574
  8.3 14.2 %collective-permute-start.3 = (f32[128,2048]{1,0:T(8,128)}, f32[128,2048]{1,0:T(8,128)}, u32[]{:S(2)}, u32[]{:S(2)}) collective-permute-start(f32[128,2048]{1,0:T(8,128)} %refs_1_.1), channel_id=1, source_target_pairs={{0,1},{2,3},{4,5},{6,7},{8,9},{10,11},{12,13},{14,15},{16,17},{18,... | collective-permute-start | bytes 3145736 | tf_op jit(solution)/shard_map/ppermute | solution.py:574
  12.5 8.6 %copy-start = (f32[128,2048]{1,0:T(8,128)S(1)}, f32[128,2048]{1,0:T(8,128)}, u32[]{:S(2)}) copy-start(f32[128,2048]{1,0:T(8,128)} %refs_0_.1) | copy-start | bytes 3145732
  12.5 8.6 %copy-start.2 = (f32[128,2048]{1,0:T(8,128)S(1)}, f32[128,2048]{1,0:T(8,128)}, u32[]{:S(2)}) copy-start(f32[128,2048]{1,0:T(8,128)} %refs_1_.1) | copy-start | bytes 3145732
  12.5 37.5 %all-to-all-start = ((f32[16,128,128]{2,1,0:T(8,128)}), f32[16,128,128]{2,1,0:T(8,128)}, u32[]{:S(2)}, u32[]{:S(2)}) async-start(f32[16,128,128]{2,1,0:T(8,128)} %bitcast.7), calls=%async_computation | async-start | bytes 2097152 | tf_op jit(solution)/shard_map/all_to_all | solution.py:572
  22.6 20.9 %copy-start.6 = (f32[128,2304]{1,0:T(8,128)}, f32[128,2304]{1,0:T(8,128)S(1)}, u32[]{:S(2)}) copy-start(f32[128,2304]{1,0:T(8,128)S(1)} %collective-permute-done.below_r.refs_10_) | copy-start | bytes 3538948
  41.7 8.9 %collective-permute-start.4 = (f32[2,32,2048]{2,1,0:T(8,128)}, f32[2,32,2048]{2,1,0:T(8,128)S(1)}, u32[]{:S(2)}, u32[]{:S(2)}) collective-permute-start(f32[2,32,2048]{2,1,0:T(8,128)} %part_kernel.1), channel_id=1, source_target_pairs={{1,2},{3,4},{5,6},{7,8},{9,10},{11,12},{13,14},{15,0},{17,18},{19,... | collective-permute-start | bytes 1572872 | tf_op jit(solution)/shard_map/ppermute | solution.py:578
  50.0 10.8 %copy-start.10 = (s32[2]{0:T(128)S(1)}, s32[2]{0:T(128)}, u32[]{:S(2)}) copy-start(s32[2]{0:T(128)} %pad_add_fusion.shifts) | copy-start | bytes 28
  50.6 36.7 %all-to-all-start.1 = ((f32[16,2,128,128]{3,2,1,0:T(8,128)}), f32[16,2,128,128]{3,2,1,0:T(8,128)}, u32[]{:S(2)}, u32[]{:S(2)}) async-start(f32[16,2,128,128]{3,2,1,0:T(8,128)} %exit_kernel.1), calls=%async_computation.1 | async-start | bytes 4194304 | tf_op jit(solution)/shard_map/all_to_all | solution.py:603
  58.7 37.9 %collective-permute-start.7 = (f32[2,32,2048]{2,1,0:T(8,128)S(1)}, f32[2,32,2048]{2,1,0:T(8,128)S(1)}, u32[]{:S(2)}, u32[]{:S(2)}) collective-permute-start(f32[2,32,2048]{2,1,0:T(8,128)S(1)} %collective-permute-done.4.refs_4_), channel_id=1, source_target_pairs={{32,64},{34,66},{36,68},{38,70},{40,72},{42,74},{44,76},{46,78},{4... | collective-permute-start | bytes 1572872 | tf_op jit(solution)/shard_map/ppermute | solution.py:551
  59.3 37.2 %collective-permute-start.6 = (f32[2,32,2048]{2,1,0:T(8,128)S(1)}, f32[2,32,2048]{2,1,0:T(8,128)S(1)}, u32[]{:S(2)}, u32[]{:S(2)}) collective-permute-start(f32[2,32,2048]{2,1,0:T(8,128)S(1)} %collective-permute-done.4.refs_4_), channel_id=1, source_target_pairs={{0,64},{2,66},{4,68},{6,70},{8,72},{10,74},{12,76},{14,78},{64,0},... | collective-permute-start | bytes 1572872 | tf_op jit(solution)/shard_map/ppermute | solution.py:551
  60.1 36.6 %collective-permute-start.5 = (f32[2,32,2048]{2,1,0:T(8,128)S(1)}, f32[2,32,2048]{2,1,0:T(8,128)S(1)}, u32[]{:S(2)}, u32[]{:S(2)}) collective-permute-start(f32[2,32,2048]{2,1,0:T(8,128)S(1)} %collective-permute-done.4.refs_4_), channel_id=1, source_target_pairs={{32,0},{34,2},{36,4},{38,6},{40,8},{42,10},{44,12},{46,14},{48,16}... | collective-permute-start | bytes 1572872 | tf_op jit(solution)/shard_map/ppermute | solution.py:551
  60.8 3.8 %collective-permute-start.10 = (s32[2]{0:T(128)S(1)}, s32[2]{0:T(128)S(1)}, u32[]{:S(2)}, u32[]{:S(2)}) collective-permute-start(s32[2]{0:T(128)S(1)} %copy-done.10), channel_id=1, source_target_pairs={{0,48},{16,32},{32,16},{48,0},{1,49},{17,33},{33,17},{49,1},{2,50}... | collective-permute-start | bytes 32 | tf_op jit(solution)/shard_map/ppermute | solution.py:605
  62.7 2.8 %collective-permute-start.9 = (s32[2]{0:T(128)S(1)}, s32[2]{0:T(128)S(1)}, u32[]{:S(2)}, u32[]{:S(2)}) collective-permute-start(s32[2]{0:T(128)S(1)} %copy-done.10), channel_id=1, source_target_pairs={{0,32},{16,48},{32,0},{48,16},{1,33},{17,49},{33,1},{49,17},{2,34}... | collective-permute-start | bytes 32 | tf_op jit(solution)/shard_map/ppermute | solution.py:605
  64.6 4.0 %collective-permute-start.8 = (s32[2]{0:T(128)S(1)}, s32[2]{0:T(128)S(1)}, u32[]{:S(2)}, u32[]{:S(2)}) collective-permute-start(s32[2]{0:T(128)S(1)} %copy-done.10), channel_id=1, source_target_pairs={{0,16},{16,0},{32,48},{48,32},{1,17},{17,1},{33,49},{49,33},{2,18}... | collective-permute-start | bytes 32 | tf_op jit(solution)/shard_map/ppermute | solution.py:605
  96.5 59.6 %copy-start.1 = (f32[128,2048]{1,0:T(8,128)S(1)}, f32[128,2048]{1,0:T(8,128)}, u32[]{:S(2)}) copy-start(f32[128,2048]{1,0:T(8,128)} %refs_0_.1) | copy-start | bytes 3145732
  96.5 59.6 %copy-start.3 = (f32[128,2048]{1,0:T(8,128)S(1)}, f32[128,2048]{1,0:T(8,128)}, u32[]{:S(2)}) copy-start(f32[128,2048]{1,0:T(8,128)} %refs_1_.1) | copy-start | bytes 3145732
  96.5 59.6 %copy-start.4 = (f32[128,2304]{1,0:T(8,128)S(1)}, f32[128,2304]{1,0:T(8,128)}, u32[]{:S(2)}) copy-start(f32[128,2304]{1,0:T(8,128)} %refs_8_.1) | copy-start | bytes 3538948
  96.5 59.6 %copy-start.5 = (f32[128,2304]{1,0:T(8,128)S(1)}, f32[128,2304]{1,0:T(8,128)}, u32[]{:S(2)}) copy-start(f32[128,2304]{1,0:T(8,128)} %refs_9_.1) | copy-start | bytes 3538948
  96.5 59.6 %copy-start.7 = (f32[128,2304]{1,0:T(8,128)S(1)}, f32[128,2304]{1,0:T(8,128)}, u32[]{:S(2)}) copy-start(f32[128,2304]{1,0:T(8,128)} %copy-done.6) | copy-start | bytes 3538948
  96.6 59.6 %copy-start.8 = (bf16[16,128,256]{2,1,0:T(8,128)(2,1)S(1)}, bf16[16,128,256]{2,1,0:T(8,128)(2,1)}, u32[]{:S(2)}) copy-start(bf16[16,128,256]{2,1,0:T(8,128)(2,1)} %constant.51.clone.low_in.refs_13_) | copy-start | bytes 3145732
  96.6 59.6 %copy-start.9 = (bf16[16,128,256]{2,1,0:T(8,128)(2,1)S(1)}, bf16[16,128,256]{2,1,0:T(8,128)(2,1)}, u32[]{:S(2)}) copy-start(bf16[16,128,256]{2,1,0:T(8,128)(2,1)} %constant.50.clone.high_in.refs_12_) | copy-start | bytes 3145732
